TPU v7x, 128 devices: a whole 4x4x4 slice. The times are simulated.
128 devices in a mesh: lsec: 8 (over y, core), rsec: 4 (over z), mpo: 4 (over x).
Axes of the slice: x: 4, y: 4, z: 4, core: 2. Of those that a mesh axis runs over, the one named last changes fastest.
Arguments:
- wavefunction: bfloat16 [512, 256, 256], P(('lsec', 'rsec')), may hold values from -6 to 6
- left_env: bfloat16 [40, 32, 256, 256], P('mpo', 'lsec'), may hold values from -0.125 to 0.125
- right_env: bfloat16 [40, 16, 256, 256], P('mpo', 'rsec'), may hold values from -0.375 to 0.375
- block_left: int32 [512], P(('lsec', 'rsec')), may hold values from 0 to 31, as said below
- block_right: int32 [512], P(('lsec', 'rsec')), may hold values from 0 to 15, as said below
- channel_class: int32 [40], replicated, may hold values from 0 to 4
- hop_target: int32 [512, 4], replicated, may hold values from 0 to 511, as said below
Outputs:
- result: float32 [512, 256, 256], P(('lsec', 'rsec'), 'mpo')
Inputs may be any that keep to these rules, and one draw needn't show every extreme that they name: `block_left`: block k's left sector is one of the 4 sectors [s * 4, (s + 1) * 4) with s = k // 64. `block_right`: block k's right sector is one of the 4 sectors [s * 4, (s + 1) * 4) with s = (k // 16) % 4. `hop_target`: owner pair of a block t is t // 16. Over the 64 entries of the rows of one aligned run of 16 blocks, at most 4 name blocks of any one owner pair; some owner pair is named exactly 4 times by every run.
All inputs are finite; a program needn't handle non-finite values.
Results may differ from a plain program's by a relative error of at most 0.014.
Values may be sent and summed in bfloat16 or wider, within the bound.
No kernel may reach another device: no remote copies, remote signals or barrier semaphores. Data moves between devices by JAX's collectives and lax.ppermute only.
A program may use at most 128 MiB of HBM per device.

v0:
```python
from functools import partial

import jax
import jax.numpy as jnp
from jax import lax
from jax.sharding import PartitionSpec as P


def item_places(targets, block_count, owner_count):
    destined = targets // block_count
    owner_marks = (destined[..., None] == jnp.arange(owner_count, dtype=jnp.int32)).astype(
        jnp.int32
    )
    earlier = jnp.cumsum(owner_marks, axis=-2) - owner_marks
    slot_index = jnp.sum(earlier * owner_marks, axis=-1)
    return (destined, slot_index)


def add_class(class_number, totals, product):
    return tuple(
        (
            member + product if place == class_number else member
            for place, member in enumerate(totals)
        )
    )


def shards(wavefunction, left_env, right_env, block_left, block_right, channel_class, hop_target):
    block_count = wavefunction.shape[0]
    block_size = wavefunction.shape[1]
    group_width = left_env.shape[0]
    hop_count = hop_target.shape[1]
    class_count = hop_count + 1
    lsec_count = lax.axis_size("lsec")
    rsec_count = lax.axis_size("rsec")
    owner_count = lsec_count * rsec_count
    item_count = block_count * hop_count
    capacity = 2 * ((item_count + owner_count - 1) // owner_count)
    slot_count = owner_count * capacity
    own_flat = lax.axis_index("lsec") * rsec_count + lax.axis_index("rsec")
    local_left = block_left - lax.axis_index("lsec") * left_env.shape[1]
    local_right = block_right - lax.axis_index("rsec") * right_env.shape[1]
    group_class = lax.dynamic_slice_in_dim(
        channel_class, lax.axis_index("mpo") * group_width, group_width, 0
    )
    branches = [partial(add_class, number) for number in range(class_count)]

    def channel_step(totals, inputs):
        left_one, right_one, class_id = inputs
        left_pick = jnp.take(left_one, local_left, axis=0)
        right_pick = jnp.take(right_one, local_right, axis=0)
        half_product = jnp.einsum(
            "kab,kbc->kac", left_pick, wavefunction, preferred_element_type=jnp.float32
        ).astype(jnp.bfloat16)
        full_product = jnp.einsum(
            "kac,kcd->kad", half_product, right_pick, preferred_element_type=jnp.float32
        )
        return (lax.switch(class_id, branches, totals, full_product), None)

    zero_block = jnp.zeros((block_count, block_size, block_size), jnp.float32)
    totals, _ = lax.scan(
        channel_step,
        tuple((zero_block for number in range(class_count))),
        (left_env, right_env, group_class),
    )
    partial_sums = jnp.stack([member.astype(jnp.bfloat16) for member in totals])
    own_rows = lax.dynamic_slice_in_dim(hop_target, own_flat * block_count, block_count, 0)
    own_items = jnp.transpose(own_rows).reshape(-1)
    destined, slot_index = item_places(own_items, block_count, owner_count)
    position = destined * capacity + slot_index
    send_table = position[:, None] == jnp.arange(slot_count, dtype=jnp.int32)[None, :]
    all_targets = jnp.transpose(
        hop_target.reshape(owner_count, block_count, hop_count), (0, 2, 1)
    ).reshape(owner_count, item_count)
    dest_all, slot_all = item_places(all_targets, block_count, owner_count)
    column = jnp.arange(owner_count, dtype=jnp.int32)[:, None] * capacity + slot_all
    to_myself = dest_all == own_flat
    local_block = all_targets - own_flat * block_count
    row_hit = (local_block[..., None] == jnp.arange(block_count, dtype=jnp.int32)) & to_myself[
        ..., None
    ]
    col_hit = column[..., None] == jnp.arange(slot_count, dtype=jnp.int32)
    gather_table = jnp.einsum(
        "sib,sic->bc", row_hit.astype(jnp.float32), col_hit.astype(jnp.float32)
    )
    table_half = gather_table.astype(jnp.bfloat16)
    moved_items = partial_sums[1:].reshape(item_count, block_size * block_size)
    buffer = jnp.dot(
        send_table.astype(jnp.bfloat16).T, moved_items, preferred_element_type=jnp.float32
    ).astype(jnp.bfloat16)
    received = lax.all_to_all(
        buffer.reshape(owner_count, capacity, block_size, block_size),
        ("lsec", "rsec"),
        split_axis=0,
        concat_axis=0,
        tiled=True,
    )
    incoming = jnp.dot(
        table_half,
        received.reshape(slot_count, block_size * block_size),
        preferred_element_type=jnp.float32,
    )
    local_sum = partial_sums[0].astype(jnp.float32) + incoming.reshape(
        block_count, block_size, block_size
    )
    result = lax.psum_scatter(
        local_sum.astype(jnp.bfloat16), "mpo", scatter_dimension=1, tiled=True
    ).astype(jnp.float32)
    return result


def solution(mesh):
    in_specs = (
        P(("lsec", "rsec"), None, None),
        P("mpo", "lsec", None, None),
        P("mpo", "rsec", None, None),
        P(("lsec", "rsec")),
        P(("lsec", "rsec")),
        P(),
        P(),
    )
    out_specs = P(("lsec", "rsec"), "mpo", None)
    return jax.shard_map(shards, mesh=mesh, in_specs=in_specs, out_specs=out_specs, check_vma=False)
```

profile of v0, /device:TPU:1, one launch (start us, length us, event | category | flops | bytes accessed | tf_op | source)
XLA Modules:
  0.0 577.7 jit_solution(2038328952629152013)
XLA Ops:
  20.0 168.4 %while.18 = (s32[]{:T(128)}, f32[16,256,256]{2,1,0:T(8,128)}, f32[16,256,256]{2,1,0:T(8,128)}, f32[16,256,256]{2,1,0:T(8,128)}, f32[16,256,256]{2,1,0:T(8,128)},...) while((s32[]{:T(128)}, f32[16,256,256]{2,1,0:T(8,128)}, ...), condition=%wide.region_6.8_spmd, body=%wide.region_0.7_spmd.sunk | while | flops 1077938432 | bytes 33563780 | solution.py:61
  30.7 6.1 %conditional.2 = (f32[16,256,256]{2,1,0:T(8,128)}, f32[16,256,256]{2,1,0:T(8,128)}, f32[16,256,256]{2,1,0:T(8,128)}, f32[16,256,256]{2,1,0:T(8,128)}, f32[16,256,256]{2,1,0:T(8,128)}) conditional(s32[]{:T(128)} %bitcast.52, (f32[16,256,256]{2,1,0:T(8,128)}, f32[16,256,256]{2,1,0:T(8,128)}, f32[16,256,256]{2,1,0:T(8,128)}, ...), branch_computations={%region_1.2_spmd, %region_2.3_spmd, %region_3.4_spmd, %region_4.5_... | conditional | flops 1048576 | bytes 12582952 | solution.py:58
  30.8 6.0 %add.61 = f32[16,256,256]{2,1,0:T(8,128)} add(f32[16,256,256]{2,1,0:T(8,128)} %get-tuple-element.142, f32[16,256,256]{2,1,0:T(8,128)} %get-tuple-element.143) | non-fusion elementwise | flops 1048576 | bytes 12582912 | tf_op jit(solution)/shard_map/while/body/eval_jaxpr/cond/branch_4_fun/add | solution.py:22
  47.5 6.1 %conditional.2 = (f32[16,256,256]{2,1,0:T(8,128)}, f32[16,256,256]{2,1,0:T(8,128)}, f32[16,256,256]{2,1,0:T(8,128)}, f32[16,256,256]{2,1,0:T(8,128)}, f32[16,256,256]{2,1,0:T(8,128)}) conditional(s32[]{:T(128)} %bitcast.52, (f32[16,256,256]{2,1,0:T(8,128)}, f32[16,256,256]{2,1,0:T(8,128)}, f32[16,256,256]{2,1,0:T(8,128)}, ...), branch_computations={%region_1.2_spmd, %region_2.3_spmd, %region_3.4_spmd, %region_4.5_... | conditional | flops 1048576 | bytes 12582952 | solution.py:58
  47.6 6.0 %add.60 = f32[16,256,256]{2,1,0:T(8,128)} add(f32[16,256,256]{2,1,0:T(8,128)} %get-tuple-element.135, f32[16,256,256]{2,1,0:T(8,128)} %get-tuple-element.136) | non-fusion elementwise | flops 1048576 | bytes 12582912 | tf_op jit(solution)/shard_map/while/body/eval_jaxpr/cond/branch_3_fun/add | solution.py:22
  57.6 5.5 fusion.47
  64.3 6.1 %conditional.2 = (f32[16,256,256]{2,1,0:T(8,128)}, f32[16,256,256]{2,1,0:T(8,128)}, f32[16,256,256]{2,1,0:T(8,128)}, f32[16,256,256]{2,1,0:T(8,128)}, f32[16,256,256]{2,1,0:T(8,128)}) conditional(s32[]{:T(128)} %bitcast.52, (f32[16,256,256]{2,1,0:T(8,128)}, f32[16,256,256]{2,1,0:T(8,128)}, f32[16,256,256]{2,1,0:T(8,128)}, ...), branch_computations={%region_1.2_spmd, %region_2.3_spmd, %region_3.4_spmd, %region_4.5_... | conditional | flops 1048576 | bytes 12582952 | solution.py:58
  64.4 6.0 %add.60 = f32[16,256,256]{2,1,0:T(8,128)} add(f32[16,256,256]{2,1,0:T(8,128)} %get-tuple-element.135, f32[16,256,256]{2,1,0:T(8,128)} %get-tuple-element.136) | non-fusion elementwise | flops 1048576 | bytes 12582912 | tf_op jit(solution)/shard_map/while/body/eval_jaxpr/cond/branch_3_fun/add | solution.py:22
  81.1 6.2 %conditional.2 = (f32[16,256,256]{2,1,0:T(8,128)}, f32[16,256,256]{2,1,0:T(8,128)}, f32[16,256,256]{2,1,0:T(8,128)}, f32[16,256,256]{2,1,0:T(8,128)}, f32[16,256,256]{2,1,0:T(8,128)}) conditional(s32[]{:T(128)} %bitcast.52, (f32[16,256,256]{2,1,0:T(8,128)}, f32[16,256,256]{2,1,0:T(8,128)}, f32[16,256,256]{2,1,0:T(8,128)}, ...), branch_computations={%region_1.2_spmd, %region_2.3_spmd, %region_3.4_spmd, %region_4.5_... | conditional | flops 1048576 | bytes 12582952 | solution.py:58
  81.2 6.1 %add.57 = f32[16,256,256]{2,1,0:T(8,128)} add(f32[16,256,256]{2,1,0:T(8,128)} %get-tuple-element.114, f32[16,256,256]{2,1,0:T(8,128)} %get-tuple-element.115) | non-fusion elementwise | flops 1048576 | bytes 12582912 | tf_op jit(solution)/shard_map/while/body/eval_jaxpr/cond/branch_0_fun/add | solution.py:22
  91.3 5.5 fusion.47
  98.0 6.1 %conditional.2 = (f32[16,256,256]{2,1,0:T(8,128)}, f32[16,256,256]{2,1,0:T(8,128)}, f32[16,256,256]{2,1,0:T(8,128)}, f32[16,256,256]{2,1,0:T(8,128)}, f32[16,256,256]{2,1,0:T(8,128)}) conditional(s32[]{:T(128)} %bitcast.52, (f32[16,256,256]{2,1,0:T(8,128)}, f32[16,256,256]{2,1,0:T(8,128)}, f32[16,256,256]{2,1,0:T(8,128)}, ...), branch_computations={%region_1.2_spmd, %region_2.3_spmd, %region_3.4_spmd, %region_4.5_... | conditional | flops 1048576 | bytes 12582952 | solution.py:58
  98.1 6.0 %add.60 = f32[16,256,256]{2,1,0:T(8,128)} add(f32[16,256,256]{2,1,0:T(8,128)} %get-tuple-element.135, f32[16,256,256]{2,1,0:T(8,128)} %get-tuple-element.136) | non-fusion elementwise | flops 1048576 | bytes 12582912 | tf_op jit(solution)/shard_map/while/body/eval_jaxpr/cond/branch_3_fun/add | solution.py:22
  114.8 6.1 %conditional.2 = (f32[16,256,256]{2,1,0:T(8,128)}, f32[16,256,256]{2,1,0:T(8,128)}, f32[16,256,256]{2,1,0:T(8,128)}, f32[16,256,256]{2,1,0:T(8,128)}, f32[16,256,256]{2,1,0:T(8,128)}) conditional(s32[]{:T(128)} %bitcast.52, (f32[16,256,256]{2,1,0:T(8,128)}, f32[16,256,256]{2,1,0:T(8,128)}, f32[16,256,256]{2,1,0:T(8,128)}, ...), branch_computations={%region_1.2_spmd, %region_2.3_spmd, %region_3.4_spmd, %region_4.5_... | conditional | flops 1048576 | bytes 12582952 | solution.py:58
  114.9 6.0 %add.60 = f32[16,256,256]{2,1,0:T(8,128)} add(f32[16,256,256]{2,1,0:T(8,128)} %get-tuple-element.135, f32[16,256,256]{2,1,0:T(8,128)} %get-tuple-element.136) | non-fusion elementwise | flops 1048576 | bytes 12582912 | tf_op jit(solution)/shard_map/while/body/eval_jaxpr/cond/branch_3_fun/add | solution.py:22
  131.6 6.2 %conditional.2 = (f32[16,256,256]{2,1,0:T(8,128)}, f32[16,256,256]{2,1,0:T(8,128)}, f32[16,256,256]{2,1,0:T(8,128)}, f32[16,256,256]{2,1,0:T(8,128)}, f32[16,256,256]{2,1,0:T(8,128)}) conditional(s32[]{:T(128)} %bitcast.52, (f32[16,256,256]{2,1,0:T(8,128)}, f32[16,256,256]{2,1,0:T(8,128)}, f32[16,256,256]{2,1,0:T(8,128)}, ...), branch_computations={%region_1.2_spmd, %region_2.3_spmd, %region_3.4_spmd, %region_4.5_... | conditional | flops 1048576 | bytes 12582952 | solution.py:58
  131.7 6.1 %add.57 = f32[16,256,256]{2,1,0:T(8,128)} add(f32[16,256,256]{2,1,0:T(8,128)} %get-tuple-element.114, f32[16,256,256]{2,1,0:T(8,128)} %get-tuple-element.115) | non-fusion elementwise | flops 1048576 | bytes 12582912 | tf_op jit(solution)/shard_map/while/body/eval_jaxpr/cond/branch_0_fun/add | solution.py:22
  148.5 6.2 %conditional.2 = (f32[16,256,256]{2,1,0:T(8,128)}, f32[16,256,256]{2,1,0:T(8,128)}, f32[16,256,256]{2,1,0:T(8,128)}, f32[16,256,256]{2,1,0:T(8,128)}, f32[16,256,256]{2,1,0:T(8,128)}) conditional(s32[]{:T(128)} %bitcast.52, (f32[16,256,256]{2,1,0:T(8,128)}, f32[16,256,256]{2,1,0:T(8,128)}, f32[16,256,256]{2,1,0:T(8,128)}, ...), branch_computations={%region_1.2_spmd, %region_2.3_spmd, %region_3.4_spmd, %region_4.5_... | conditional | flops 1048576 | bytes 12582952 | solution.py:58
  148.5 6.1 %add.57 = f32[16,256,256]{2,1,0:T(8,128)} add(f32[16,256,256]{2,1,0:T(8,128)} %get-tuple-element.114, f32[16,256,256]{2,1,0:T(8,128)} %get-tuple-element.115) | non-fusion elementwise | flops 1048576 | bytes 12582912 | tf_op jit(solution)/shard_map/while/body/eval_jaxpr/cond/branch_0_fun/add | solution.py:22
  165.4 6.1 %conditional.2 = (f32[16,256,256]{2,1,0:T(8,128)}, f32[16,256,256]{2,1,0:T(8,128)}, f32[16,256,256]{2,1,0:T(8,128)}, f32[16,256,256]{2,1,0:T(8,128)}, f32[16,256,256]{2,1,0:T(8,128)}) conditional(s32[]{:T(128)} %bitcast.52, (f32[16,256,256]{2,1,0:T(8,128)}, f32[16,256,256]{2,1,0:T(8,128)}, f32[16,256,256]{2,1,0:T(8,128)}, ...), branch_computations={%region_1.2_spmd, %region_2.3_spmd, %region_3.4_spmd, %region_4.5_... | conditional | flops 1048576 | bytes 12582952 | solution.py:58
  165.5 6.0 %add.61 = f32[16,256,256]{2,1,0:T(8,128)} add(f32[16,256,256]{2,1,0:T(8,128)} %get-tuple-element.142, f32[16,256,256]{2,1,0:T(8,128)} %get-tuple-element.143) | non-fusion elementwise | flops 1048576 | bytes 12582912 | tf_op jit(solution)/shard_map/while/body/eval_jaxpr/cond/branch_4_fun/add | solution.py:22
  182.2 6.2 %conditional.2 = (f32[16,256,256]{2,1,0:T(8,128)}, f32[16,256,256]{2,1,0:T(8,128)}, f32[16,256,256]{2,1,0:T(8,128)}, f32[16,256,256]{2,1,0:T(8,128)}, f32[16,256,256]{2,1,0:T(8,128)}) conditional(s32[]{:T(128)} %bitcast.52, (f32[16,256,256]{2,1,0:T(8,128)}, f32[16,256,256]{2,1,0:T(8,128)}, f32[16,256,256]{2,1,0:T(8,128)}, ...), branch_computations={%region_1.2_spmd, %region_2.3_spmd, %region_3.4_spmd, %region_4.5_... | conditional | flops 1048576 | bytes 12582952 | solution.py:58
  182.2 6.1 %add.57 = f32[16,256,256]{2,1,0:T(8,128)} add(f32[16,256,256]{2,1,0:T(8,128)} %get-tuple-element.114, f32[16,256,256]{2,1,0:T(8,128)} %get-tuple-element.115) | non-fusion elementwise | flops 1048576 | bytes 12582912 | tf_op jit(solution)/shard_map/while/body/eval_jaxpr/cond/branch_0_fun/add | solution.py:22
  198.8 11.8 %copy.43 = bf16[8,8,256,256]{3,1,2,0:T(8,128)(2,1)} copy(bf16[8,8,256,256]{3,2,1,0:T(8,128)(2,1)} %bitcast.58) | data formatting | bytes 16777216
  211.1 13.7 %convolution_convert_fusion = bf16[128,65536]{1,0:T(8,128)(2,1)} fusion(bf16[64,65536]{1,0:T(8,128)(2,1)} %bitcast.57, s32[64]{0:T(128)S(1)} %multiply_add_fusion), kind=kOutput, calls=%fused_computation.19 | convolution fusion | flops 1082138624 | bytes 25166080 | tf_op jit(solution)/shard_map/dot_general | solution.py:88
  224.8 15.6 %copy.44 = bf16[16,8,256,256]{3,2,1,0:T(8,128)(2,1)} copy(bf16[16,8,256,256]{3,1,2,0:T(8,128)(2,1)} %bitcast.55) | data formatting | bytes 33554432
  240.4 9.7 %all-to-all-start = ((bf16[32,4,256,256]{3,2,1,0:T(8,128)(2,1)}), bf16[32,4,256,256]{3,2,1,0:T(8,128)(2,1)}, u32[]{:S(2)}, u32[]{:S(2)}) async-start(bf16[32,4,256,256]{3,2,1,0:T(8,128)(2,1)} %bitcast.53), calls=%async_computation | async-start | bytes 33554432 | tf_op jit(solution)/shard_map/all_to_all | solution.py:91
  252.7 218.4 %all-to-all-done = bf16[32,4,256,256]{3,2,1,0:T(8,128)(2,1)} async-done(((bf16[32,4,256,256]{3,2,1,0:T(8,128)(2,1)}), bf16[32,4,256,256]{3,2,1,0:T(8,128)(2,1)}, u32[]{:S(2)}, u32[]{:S(2)}) %all-to-all-start) | async-done | bytes 16777248 | tf_op jit(solution)/shard_map/all_to_all | solution.py:91
  471.1 17.8 %copy.45 = bf16[16,8,256,256]{3,1,2,0:T(8,128)(2,1)} copy(bf16[16,8,256,256]{3,2,1,0:T(8,128)(2,1)} %bitcast.23) | data formatting | bytes 33554432
  488.9 22.4 %copy.41 = bf16[128,65536]{0,1:T(8,128)(2,1)} copy(bf16[128,65536]{1,0:T(8,128)(2,1)} %bitcast.56) | data formatting | bytes 33554432 | tf_op jit(solution)/shard_map/reshape | solution.py:100
  511.3 13.2 %add_convert_fusion = bf16[16,256,256]{2,0,1:T(8,128)(2,1)} fusion(bf16[256,256,128]{2,1,0:T(8,128)(2,1)} %bitcast.54, f32[16,256,256]{2,1,0:T(8,128)} %get-tuple-element.167, s32[32,64]{1,0:T(8,128)S(1)} %broadcast_add_fusion, s32[32,64]{1,0:T(8,128)S(1)} %copy.34, pred[32,64]{1,0:T(8,128)(4,1)S(1)} %get-tuple-element.196), kind=kOutput, calls=%fused_computation.22 | convolution fusion | flops 280299520 | bytes 23087104 | tf_op jit(solution)/shard_map/dot_general | solution.py:98
  524.6 44.1 %reduce-scatter.2.cloned.1.call-done = bf16[16,64,256]{2,0,1:T(8,128)(2,1)} async-done(((bf16[16,256,256]{2,0,1:T(8,128)(2,1)}), bf16[16,64,256]{2,0,1:T(8,128)(2,1)}) %reduce-scatter.2.cloned.1.call-update) | async-done | bytes 524304 | tf_op jit(solution)/shard_map/reduce_scatter | solution.py:106
  (129 shorter events, 118.8 us)
Async XLA Ops:
  188.4 3.4 copy-start.2
  191.0 2.4 copy-start.1
  192.1 2.5 copy-start
  198.8 11.8 %copy-start.3 = (s32[512,4]{0,1:T(4,128)S(1)}, s32[512,4]{0,1:T(4,128)}, u32[]{:S(2)}) copy-start(s32[512,4]{0,1:T(4,128)} %param.22) | copy-start | bytes 24580
  240.4 230.7 %all-to-all-start = ((bf16[32,4,256,256]{3,2,1,0:T(8,128)(2,1)}), bf16[32,4,256,256]{3,2,1,0:T(8,128)(2,1)}, u32[]{:S(2)}, u32[]{:S(2)}) async-start(bf16[32,4,256,256]{3,2,1,0:T(8,128)(2,1)} %bitcast.53), calls=%async_computation | async-start | bytes 33554432 | tf_op jit(solution)/shard_map/all_to_all | solution.py:91
  250.1 318.6 %reduce-scatter.2.cloned.1.call-start = ((), (), s32[]{:S(2)}) async-start(), calls=%async_computation.2 | async-start | bytes 2621440 | tf_op jit(solution)/shard_map/reduce_scatter | solution.py:106
Sparse Core Ops, SparseCore 0:
  524.7 43.9 reduce-scatter.1
where the time goes:
time: 579 us; the launch traced here: 578 us
  waiting for transfers between devices  263 us (45%)
  local copies, waits for them, and re-layouts  132 us (23%)
  matrix products  81.9 us (14%)
  other arithmetic  71.2 us (12%)
  between operations  13.5 us (2%)
  starting transfers between devices  9.92 us (2%)
  loops' own time  6.87 us (1%)
    all_to_all x1, waiting for transfers between devices, shards(): lax.all_to_all(buffer.reshape(owner_count, capacity, block_size, block_si...  218 us
    add x10, other arithmetic, add_class(): member + product  60.8 us
    dot_general x10, matrix products, channel_step(): jnp.einsum('kac,kcd->kad', half_product, right_pick, preferred_element_ty...  55 us
    unnamed x11, local copies, waits for them, and re-layouts  48.3 us
    reduce_scatter x1, waiting for transfers between devices, shards(): lax.psum_scatter(local_sum.astype(jnp.bfloat16), 'mpo', scatter_dimension...  44.1 us
    reshape x1, local copies, waits for them, and re-layouts, shards(): received.reshape(slot_count, block_size * block_size)  22.4 us
    gather x10, local copies, waits for them, and re-layouts, channel_step(): left_pick = jnp.take(left_one, local_left, axis=0)  19.9 us
    dot_general x1, matrix products, shards(): jnp.dot(send_table.astype(jnp.bfloat16).T, moved_items, preferred_element...  13.7 us
  transfers between devices with their start and end apart: 2, of which 2 were waited for; matrix products, arithmetic and copies ran while one was open for 0% of the time, Pallas kernels for 0%

commit v1 on v0

v1 whole, which is shorter than its diff:
```python
import functools

import jax
import jax.numpy as jnp
from jax import lax
from jax.experimental import pallas as pl
from jax.experimental.pallas import tpu as pltpu
from jax.sharding import PartitionSpec as P

LANES = 128
ROW_CHUNKS = (16, 16, 16, 16)


def products_kernel(
    chunks, x_ref, left_ids, right_ids, class_ids, first_ref, psi_ref, left_hbm, right_hbm, *rest
):
    chunk_count = len(chunks)
    outs = rest[: 4 * chunk_count]
    left_ref, right_ref, half_ref, acc_ref, left_sems, right_sems = rest[4 * chunk_count :]
    channels = left_ref.shape[0]
    classes = acc_ref.shape[0]
    block = acc_ref.shape[1]
    quarter = block // 4
    step = pl.program_id(0)

    def left_copy(w):
        return pltpu.make_async_copy(left_hbm.at[w], left_ref.at[w], left_sems.at[w])

    def right_copy(w):
        return pltpu.make_async_copy(right_hbm.at[w], right_ref.at[w], right_sems.at[w])

    @pl.when(step == 0)
    def _():
        for w in range(channels):
            left_copy(w).start()
        for w in range(channels):
            right_copy(w).start()
        acc_ref[...] = jnp.zeros_like(acc_ref)
        for w in range(channels):
            left_copy(w).wait()
        for w in range(channels):
            right_copy(w).wait()

    left_id = left_ids[step]
    right_id = right_ids[step]
    psi = psi_ref[0]
    for w in range(channels):
        half_ref[w] = jnp.dot(
            left_ref[w, left_id], psi, preferred_element_type=jnp.float32
        ).astype(jnp.bfloat16)
    for w in range(channels):
        full = jnp.dot(half_ref[w], right_ref[w, right_id], preferred_element_type=jnp.float32)
        member = class_ids[w]
        before = acc_ref[member]
        acc_ref[member] = jnp.where(first_ref[w] != 0, 0.0, before) + full

    x = x_ref[0]
    mirror = 3 - x
    beside = x ^ 1
    across = mirror ^ 1
    orders = ((x, mirror, beside, across), (x, beside, mirror, across))
    start = 0
    for j, rows in enumerate(chunks):
        for s in range(2):
            keep, send = outs[4 * j + 2 * s], outs[4 * j + 2 * s + 1]
            for place, q in enumerate(orders[s]):
                target = keep if place < 2 else send
                at = pl.multiple_of(q * quarter + start, 16)
                for c in range(classes):
                    target[c, place % 2] = acc_ref[
                        c, pl.ds(at, rows), s * LANES : (s + 1) * LANES
                    ].astype(jnp.bfloat16)
        start += rows


def products(x, left_ids, right_ids, class_ids, first, psi, left_env, right_env, classes, chunks):
    blocks, block, _ = psi.shape
    channels = left_env.shape[0]
    out_shape, out_specs = [], []
    for rows in chunks:
        for _ in range(4):
            out_shape.append(
                jax.ShapeDtypeStruct((blocks * classes, 2, rows, LANES), jnp.bfloat16)
            )
            out_specs.append(
                pl.BlockSpec((classes, 2, rows, LANES), lambda k, *_: (k, 0, 0, 0))
            )
    return pl.pallas_call(
        functools.partial(products_kernel, chunks),
        out_shape=out_shape,
        grid_spec=pltpu.PrefetchScalarGridSpec(
            num_scalar_prefetch=5,
            grid=(blocks,),
            in_specs=[
                pl.BlockSpec((1, block, block), lambda k, *_: (k, 0, 0)),
                pl.BlockSpec(memory_space=pl.ANY),
                pl.BlockSpec(memory_space=pl.ANY),
            ],
            out_specs=out_specs,
            scratch_shapes=[
                pltpu.VMEM(left_env.shape, jnp.bfloat16),
                pltpu.VMEM(right_env.shape, jnp.bfloat16),
                pltpu.VMEM((channels, block, block), jnp.bfloat16),
                pltpu.VMEM((classes, block, block), jnp.float32),
                pltpu.SemaphoreType.DMA((channels,)),
                pltpu.SemaphoreType.DMA((channels,)),
            ],
        ),
        compiler_params=pltpu.CompilerParams(vmem_limit_bytes=40 * 2**20),
        cost_estimate=pl.CostEstimate(
            flops=4 * channels * blocks * block**3,
            bytes_accessed=2 * (left_env.size + right_env.size + psi.size * (1 + classes)),
            transcendentals=0,
        ),
        name="products",
    )(x, left_ids, right_ids, class_ids, first, psi, left_env, right_env)


def slots_kernel(classes, items, keep_a, got_a, last_a, keep_b, got_b, last_b, slots, own):
    slot_count = slots.shape[0]
    block_count = own.shape[0]

    def total(keep, got, last, i):
        return (
            keep[i, 0].astype(jnp.float32)
            + got[i, 0].astype(jnp.float32)
            + last[i].astype(jnp.float32)
        )

    def fill(p, _):
        i = items[p]
        slots[p, :, :LANES] = total(keep_a, got_a, last_a, i).astype(jnp.bfloat16)
        slots[p, :, LANES:] = total(keep_b, got_b, last_b, i).astype(jnp.bfloat16)
        return 0

    lax.fori_loop(0, slot_count, fill, 0, unroll=4)

    def stay(k, _):
        i = k * classes
        own[k, :, :LANES] = total(keep_a, got_a, last_a, i)
        own[k, :, LANES:] = total(keep_b, got_b, last_b, i)
        return 0

    lax.fori_loop(0, block_count, stay, 0, unroll=4)


def fill_slots(items, parts, classes):
    keep_a, got_a, last_a, keep_b, got_b, last_b = parts
    count, _, rows, _ = keep_a.shape
    blocks = count // classes
    pair = pl.BlockSpec((count, 1, rows, LANES), lambda i, *_: (0, 0, 0, 0))
    one = pl.BlockSpec((count, rows, LANES), lambda i, *_: (0, 0, 0))
    slot_count = items.shape[0]
    return pl.pallas_call(
        functools.partial(slots_kernel, classes),
        out_shape=(
            jax.ShapeDtypeStruct((slot_count, rows, 2 * LANES), jnp.bfloat16),
            jax.ShapeDtypeStruct((blocks, rows, 2 * LANES), jnp.float32),
        ),
        grid_spec=pltpu.PrefetchScalarGridSpec(
            num_scalar_prefetch=1,
            grid=(1,),
            in_specs=[pair, pair, one, pair, pair, one],
            out_specs=(
                pl.BlockSpec((slot_count, rows, 2 * LANES), lambda i, *_: (0, 0, 0)),
                pl.BlockSpec((blocks, rows, 2 * LANES), lambda i, *_: (0, 0, 0)),
            ),
        ),
        compiler_params=pltpu.CompilerParams(vmem_limit_bytes=32 * 2**20),
        name="fill_slots",
    )(items, keep_a, got_a, last_a, keep_b, got_b, last_b)


def gather_kernel(places, received, own, *rest):
    result = rest[-1]
    result[...] = own[...]

    def add(p, _):
        b = places[p]

        @pl.when(b >= 0)
        def _():
            result[b] += received[p].astype(jnp.float32)

        return 0

    lax.fori_loop(0, received.shape[0], add, 0)


def add_received(places, received, own, so_far, start, quarter):
    blocks, rows, width = own.shape
    at = start // rows
    operands = [places, received, own]
    in_specs = [
        pl.BlockSpec(received.shape, lambda i, *_: (0, 0, 0)),
        pl.BlockSpec(own.shape, lambda i, *_: (0, 0, 0)),
    ]
    aliases = {}
    if so_far is not None:
        operands.append(so_far)
        in_specs.append(pl.BlockSpec(memory_space=pl.ANY))
        aliases = {3: 0}
    return pl.pallas_call(
        gather_kernel,
        out_shape=jax.ShapeDtypeStruct((blocks, quarter, width), jnp.float32),
        grid_spec=pltpu.PrefetchScalarGridSpec(
            num_scalar_prefetch=1,
            grid=(1,),
            in_specs=in_specs,
            out_specs=pl.BlockSpec((blocks, rows, width), lambda i, *_: (0, at, 0)),
        ),
        input_output_aliases=aliases,
        compiler_params=pltpu.CompilerParams(vmem_limit_bytes=32 * 2**20),
        name="add_received",
    )(*operands)


def item_places(targets, block_count):
    destined = targets // block_count
    count = targets.shape[-1]
    earlier = jnp.arange(count)[:, None] > jnp.arange(count)[None, :]
    same = (destined[..., :, None] == destined[..., None, :]) & earlier
    return destined, jnp.sum(same.astype(jnp.int32), axis=-1)


def shards(wavefunction, left_env, right_env, block_left, block_right, channel_class, hop_target):
    block_count, block_size, _ = wavefunction.shape
    group_width = left_env.shape[0]
    hop_count = hop_target.shape[1]
    classes = hop_count + 1
    owners = lax.axis_size("lsec") * lax.axis_size("rsec")
    item_count = block_count * hop_count
    capacity = 2 * ((item_count + owners - 1) // owners)
    slot_count = owners * capacity
    quarter = block_size // lax.axis_size("mpo")
    me = lax.axis_index("lsec") * lax.axis_size("rsec") + lax.axis_index("rsec")
    x = lax.axis_index("mpo")
    local_left = block_left - lax.axis_index("lsec") * left_env.shape[1]
    local_right = block_right - lax.axis_index("rsec") * right_env.shape[1]
    group_class = lax.dynamic_slice_in_dim(channel_class, x * group_width, group_width, 0)
    w = jnp.arange(group_width)
    seen = jnp.any((group_class[:, None] == group_class[None, :]) & (w[:, None] > w[None, :]), 1)
    first = jnp.logical_not(seen).astype(jnp.int32)

    parts = products(
        x.astype(jnp.int32)[None],
        local_left,
        local_right,
        group_class,
        first,
        wavefunction,
        left_env,
        right_env,
        classes,
        ROW_CHUNKS,
    )

    targets = hop_target.reshape(owners, item_count)
    own_targets = lax.dynamic_index_in_dim(targets, me, 0, False)
    destined, slot = item_places(own_targets, block_count)
    position = destined * capacity + slot
    held = position[:, None] == jnp.arange(slot_count, dtype=jnp.int32)[None, :]
    index = jnp.arange(item_count, dtype=jnp.int32)
    index = (index // hop_count) * classes + 1 + index % hop_count
    slot_items = jnp.sum(jnp.where(held, index[:, None], 0), axis=0)
    destined_all, slot_all = item_places(targets, block_count)
    mine = (destined_all == me)[:, :, None] & (
        slot_all[:, :, None] == jnp.arange(capacity, dtype=jnp.int32)
    )
    local = targets - me * block_count + 1
    places = jnp.sum(jnp.where(mine, local[:, :, None], 0), axis=1).reshape(slot_count) - 1

    beside = [(i, i ^ 1) for i in range(4)]
    mirror = [(i, 3 - i) for i in range(4)]
    result = None
    start = 0
    for j, rows in enumerate(ROW_CHUNKS):
        keep_a, send_a, keep_b, send_b = parts[4 * j : 4 * j + 4]
        got_a = lax.ppermute(send_a, "mpo", beside)
        got_b = lax.ppermute(send_b, "mpo", mirror)

        def second(keep, got):
            return (
                keep[:, 1].astype(jnp.float32) + got[:, 1].astype(jnp.float32)
            ).astype(jnp.bfloat16)

        last_a = lax.ppermute(second(keep_a, got_a), "mpo", mirror)
        last_b = lax.ppermute(second(keep_b, got_b), "mpo", beside)
        slots, own = fill_slots(
            slot_items, (keep_a, got_a, last_a, keep_b, got_b, last_b), classes
        )
        received = lax.all_to_all(slots, ("lsec", "rsec"), 0, 0, tiled=True)
        result = add_received(places, received, own, result, start, quarter)
        start += rows
    return result


def solution(mesh):
    in_specs = (
        P(("lsec", "rsec"), None, None),
        P("mpo", "lsec", None, None),
        P("mpo", "rsec", None, None),
        P(("lsec", "rsec")),
        P(("lsec", "rsec")),
        P(),
        P(),
    )
    out_specs = P(("lsec", "rsec"), "mpo", None)
    return jax.shard_map(shards, mesh=mesh, in_specs=in_specs, out_specs=out_specs, check_vma=False)
```

time: 579 us -> 213 us (0.37)
  waiting for transfers between devices: 263 us -> 64.9 us
  local copies, waits for them, and re-layouts: 132 us -> 43.4 us
  matrix products: 81.9 us -> 0 us
  other arithmetic: 71.2 us -> 12.7 us
  Pallas kernels: 0 us -> 41.3 us
  starting transfers between devices: 9.92 us -> 48.9 us
  between operations: 13.5 us -> 0.34 us
  loops' own time: 6.87 us -> 0 us
    all_to_all x1 -> x4, waiting for transfers between devices: 218 us -> 3.03 us  [shards(): received = lax.all_to_all(slots, ('lsec', 'rsec'), 0, 0, tiled=True)]
    dot_general x12 -> x0, matrix products: 81.9 us -> none  [the longest x10 55 us: channel_step(): jnp.einsum('kac,kcd->kad', half_product, right_pick, preferred_element_ty...]
    ppermute x0 -> x16, waiting for transfers between devices: none -> 61.8 us  [the longest x4 31.5 us: shards(): last_a = lax.ppermute(second(keep_a, got_a), 'mpo', mirror)]
    add x12 -> x2, other arithmetic: 60.8 us -> 0.03 us  [the longest x1 0.02 us: shards(): index = index // hop_count * classes + 1 + index % hop_count]
    reduce_scatter x1 -> x0, waiting for transfers between devices: 44.1 us -> none  [shards(): lax.psum_scatter(local_sum.astype(jnp.bfloat16), 'mpo', scatter_dimension...]
    pallas_call x0 -> x9, Pallas kernels: none -> 41.3 us  [the longest x1 21.4 us: products(): pl.pallas_call(functools.partial(products_kernel, chunks), out_shape=out_...]
    unnamed x11 -> x53, local copies, waits for them, and re-layouts: 48.3 us -> 20.6 us
    gather x20 -> x0, local copies, waits for them, and re-layouts: 26.7 us -> none  [the longest x10 19.9 us: channel_step(): left_pick = jnp.take(left_one, local_left, axis=0)]
  transfers between devices with their start and end apart: 2 -> 20, of which waited for: 2 -> 8; matrix products, arithmetic and copies ran while one was open for 0% -> 16% of each run, Pallas kernels for 0% -> 7%
where the time goes in v1:
time: 213 us; the launch traced here: 212 us
  waiting for transfers between devices  64.9 us (30%)
  starting transfers between devices  48.9 us (23%)
  local copies, waits for them, and re-layouts  43.4 us (20%)
  Pallas kernels  41.3 us (19%)
  other arithmetic  12.7 us (6%)
    all_to_all x4, starting transfers between devices, shards(): received = lax.all_to_all(slots, ('lsec', 'rsec'), 0, 0, tiled=True)  34.2 us
    ppermute x4, waiting for transfers between devices, shards(): last_a = lax.ppermute(second(keep_a, got_a), 'mpo', mirror)  31.5 us
    pallas_call x1, Pallas kernels, products(): pl.pallas_call(functools.partial(products_kernel, chunks), out_shape=out_...  21.4 us
    unnamed x53, local copies, waits for them, and re-layouts  20.6 us
    ppermute x4, waiting for transfers between devices, shards(): last_b = lax.ppermute(second(keep_b, got_b), 'mpo', beside)  20.3 us
    pallas_call x4, Pallas kernels, add_received(): pl.pallas_call(gather_kernel, out_shape=jax.ShapeDtypeStruct((blocks, qua...  13.4 us
    pallas_call x8, local copies, waits for them, and re-layouts, products(): pl.pallas_call(functools.partial(products_kernel, chunks), out_shape=out_...  12.2 us
    convert_element_type x8, other arithmetic, second(): return (keep[:, 1].astype(jnp.float32) + got[:, 1].astype(jnp.float32)).a...  10.3 us
  transfers between devices with their start and end apart: 20, of which 8 were waited for; matrix products, arithmetic and copies ran while one was open for 16% of the time, Pallas kernels for 7%

profile of v1, /device:TPU:1, one launch (start us, length us, event | category | flops | bytes accessed | tf_op | source)
XLA Modules:
  0.0 211.6 jit_solution(8058175661500782997)
XLA Ops:
  1.6 1.6 copy-done.24
  3.2 21.4 %products.1 = (bf16[80,2,16,128]{3,2,1,0:T(8,128)(2,1)S(1)}, bf16[80,2,16,128]{3,2,1,0:T(8,128)(2,1)S(1)}, bf16[80,2,16,128]{3,2,1,0:T(8,128)(2,1)S(1)}, bf16[80...) custom-call(s32[1]{0:T(128)} %bitcast.2.x_ref, ...), custom_call_target="tpu_custom_call" | custom-call | flops 10737418240 | bytes 23068672 | tf_op jit(solution)/shard_map/products/pallas_call | solution.py:88
  32.3 3.3 %collective-permute-start.14 = (bf16[80,2,16,128]{3,2,0,1:T(8,128)(2,1)}, bf16[80,2,16,128]{3,2,0,1:T(8,128)(2,1)}, u32[]{:S(2)}, u32[]{:S(2)}) collective-permute-start(bf16[80,2,16,128]{3,2,0,1:T(8,128)(2,1)} %copy.82), channel_id=1, source_target_pairs={{0,3},{1,2},{2,1},{3,0},{4,7},{5,6},{6,5},{7,4},{8,11},{9,10},{10,... | collective-permute-start | bytes 1966088 | tf_op jit(solution)/shard_map/ppermute | solution.py:280
  40.6 9.4 %collective-permute-done.14 = bf16[80,2,16,128]{3,2,0,1:T(8,128)(2,1)} collective-permute-done((bf16[80,2,16,128]{3,2,0,1:T(8,128)(2,1)}, bf16[80,2,16,128]{3,2,0,1:T(8,128)(2,1)}, u32[]{:S(2)}, u32[]{:S(2)}) %collective-permute-start.14) | collective-permute-done | bytes 655392 | tf_op jit(solution)/shard_map/ppermute | solution.py:280
  53.2 1.9 collective-permute-start.13
  55.3 1.2 copy.85.got_b
  57.7 15.4 %collective-permute-done.15.last_b = bf16[80,16,128]{2,1,0:T(8,128)(2,1)S(1)} collective-permute-done((bf16[80,16,128]{2,1,0:T(8,128)(2,1)S(1)}, bf16[80,16,128]{2,1,0:T(8,128)(2,1)S(1)}, u32[]{:S(2)}, u32[]{:S(2)}) %collective-permute-start.15) | collective-permute-done | bytes 327712 | tf_op jit(solution)/shard_map/ppermute | solution.py:288
  74.2 1.4 fill_slots.7
  77.3 10.0 %all-to-all-start.3 = ((bf16[128,16,256]{2,1,0:T(8,128)(2,1)}), bf16[128,16,256]{2,1,0:T(8,128)(2,1)S(1)}, u32[]{:S(2)}, u32[]{:S(2)}) async-start(bf16[128,16,256]{2,1,0:T(8,128)(2,1)} %copy-done.9), calls=%async_computation.3 | async-start | bytes 2097152 | tf_op jit(solution)/shard_map/all_to_all | solution.py:292
  87.3 2.1 copy.70
  92.0 2.5 %collective-permute-start.9 = (bf16[80,16,128]{2,1,0:T(8,128)(2,1)S(1)}, bf16[80,16,128]{2,1,0:T(8,128)(2,1)S(1)}, u32[]{:S(2)}, u32[]{:S(2)}) collective-permute-start(bf16[80,16,128]{2,1,0:T(8,128)(2,1)S(1)} %fusion.4), channel_id=1, source_target_pairs={{0,3},{1,2},{2,1},{3,0},{4,7},{5,6},{6,5},{7,4},{8,11},{9,10},{10,... | collective-permute-start | bytes 983048 | tf_op jit(solution)/shard_map/ppermute | solution.py:287
  94.5 2.0 copy.68
  99.8 14.1 %collective-permute-done.9.last_a = bf16[80,16,128]{2,1,0:T(8,128)(2,1)S(1)} collective-permute-done((bf16[80,16,128]{2,1,0:T(8,128)(2,1)S(1)}, bf16[80,16,128]{2,1,0:T(8,128)(2,1)S(1)}, u32[]{:S(2)}, u32[]{:S(2)}) %collective-permute-start.9) | collective-permute-done | bytes 327712 | tf_op jit(solution)/shard_map/ppermute | solution.py:287
  113.9 1.4 fill_slots.6
  117.0 8.1 %all-to-all-start.2 = ((bf16[128,16,256]{2,1,0:T(8,128)(2,1)}), bf16[128,16,256]{2,1,0:T(8,128)(2,1)S(1)}, u32[]{:S(2)}, u32[]{:S(2)}) async-start(bf16[128,16,256]{2,1,0:T(8,128)(2,1)} %copy-done.8), calls=%async_computation.2 | async-start | bytes 2097152 | tf_op jit(solution)/shard_map/all_to_all | solution.py:292
  125.1 2.1 copy.64
  129.6 2.5 %collective-permute-start.5 = (bf16[80,16,128]{2,1,0:T(8,128)(2,1)S(1)}, bf16[80,16,128]{2,1,0:T(8,128)(2,1)S(1)}, u32[]{:S(2)}, u32[]{:S(2)}) collective-permute-start(bf16[80,16,128]{2,1,0:T(8,128)(2,1)S(1)} %fusion.2), channel_id=1, source_target_pairs={{0,3},{1,2},{2,1},{3,0},{4,7},{5,6},{6,5},{7,4},{8,11},{9,10},{10,... | collective-permute-start | bytes 983048 | tf_op jit(solution)/shard_map/ppermute | solution.py:287
  132.1 2.0 copy.62
  137.4 14.3 %collective-permute-done.5.last_a = bf16[80,16,128]{2,1,0:T(8,128)(2,1)S(1)} collective-permute-done((bf16[80,16,128]{2,1,0:T(8,128)(2,1)S(1)}, bf16[80,16,128]{2,1,0:T(8,128)(2,1)S(1)}, u32[]{:S(2)}, u32[]{:S(2)}) %collective-permute-start.5) | collective-permute-done | bytes 327712 | tf_op jit(solution)/shard_map/ppermute | solution.py:287
  151.7 1.4 fill_slots.5
  154.7 8.1 %all-to-all-start.1 = ((bf16[128,16,256]{2,1,0:T(8,128)(2,1)}), bf16[128,16,256]{2,1,0:T(8,128)(2,1)S(1)}, u32[]{:S(2)}, u32[]{:S(2)}) async-start(bf16[128,16,256]{2,1,0:T(8,128)(2,1)} %copy-done.10), calls=%async_computation.1 | async-start | bytes 2097152 | tf_op jit(solution)/shard_map/all_to_all | solution.py:292
  162.8 1.9 fusion.1
  164.7 1.9 fusion
  169.3 4.8 %collective-permute-done.3.last_b = bf16[80,16,128]{2,1,0:T(8,128)(2,1)} collective-permute-done((bf16[80,16,128]{2,1,0:T(8,128)(2,1)}, bf16[80,16,128]{2,1,0:T(8,128)(2,1)}, u32[]{:S(2)}, u32[]{:S(2)}) %collective-permute-start.3) | collective-permute-done | bytes 327712 | tf_op jit(solution)/shard_map/ppermute | solution.py:288
  174.1 3.1 %collective-permute-done.1.last_a = bf16[80,16,128]{2,1,0:T(8,128)(2,1)} collective-permute-done((bf16[80,16,128]{2,1,0:T(8,128)(2,1)}, bf16[80,16,128]{2,1,0:T(8,128)(2,1)}, u32[]{:S(2)}, u32[]{:S(2)}) %collective-permute-start.1) | collective-permute-done | bytes 327712 | tf_op jit(solution)/shard_map/ppermute | solution.py:287
  179.4 2.4 %fill_slots.4 = (bf16[128,16,256]{2,1,0:T(8,128)(2,1)S(1)}, f32[16,16,256]{2,1,0:T(8,128)S(1)}) custom-call(s32[128]{0:T(128)S(1)} %select_reduce_fusion.1.items, bf16[80,2,16,128]{3,2,1,0:T(8,128)(2,1)S(1)} %copy-done.1, bf16[80,2,16,128]{3,2,1,0:T(8,128)(2,1)S(1)} %copy.66.got_a, bf16[80,16,128]{2,1,0:T(8,128)(2,1)} %collective-permute-done.1.last_a, ...), custom_call_target="tpu_custom_call" | custom-call | tf_op jit(solution)/shard_map/fill_slots/pallas_call | solution.py:154
  182.8 8.1 %all-to-all-start = ((bf16[128,16,256]{2,1,0:T(8,128)(2,1)}), bf16[128,16,256]{2,1,0:T(8,128)(2,1)}, u32[]{:S(2)}, u32[]{:S(2)}) async-start(bf16[128,16,256]{2,1,0:T(8,128)(2,1)} %copy-done.11), calls=%async_computation | async-start | bytes 2097152 | tf_op jit(solution)/shard_map/all_to_all | solution.py:292
  193.2 3.0 %add_received.4.rest_0_ = f32[16,64,256]{2,1,0:T(8,128)} custom-call(s32[128]{0:T(128)S(1)} %sub.50.places, bf16[128,16,256]{2,1,0:T(8,128)(2,1)S(1)} %all-to-all-done.3.received, f32[16,16,256]{2,1,0:T(8,128)S(1)} %copy-done.17), custom_call_target="tpu_custom_call" | custom-call | tf_op jit(solution)/shard_map/add_received/pallas_call | solution.py:203
  197.2 3.0 %add_received.5.rest_0_ = f32[16,64,256]{2,1,0:T(8,128)} custom-call(s32[128]{0:T(128)S(1)} %sub.50.places, bf16[128,16,256]{2,1,0:T(8,128)(2,1)S(1)} %all-to-all-done.2.received, f32[16,16,256]{2,1,0:T(8,128)S(1)} %copy-done.19, f32[16,64,256]{2,1,0:T(8,128)} %add_received.4.rest_0_), custom_call_target="tpu_custom_call", output_to_operand_aliasing={{}: (3, {})} | custom-call | tf_op jit(solution)/shard_map/add_received/pallas_call | solution.py:203
  201.2 3.0 %add_received.6.rest_0_ = f32[16,64,256]{2,1,0:T(8,128)} custom-call(s32[128]{0:T(128)S(1)} %sub.50.places, bf16[128,16,256]{2,1,0:T(8,128)(2,1)S(1)} %all-to-all-done.1.received, f32[16,16,256]{2,1,0:T(8,128)S(1)} %copy-done.21, f32[16,64,256]{2,1,0:T(8,128)} %add_received.5.rest_0_), custom_call_target="tpu_custom_call", output_to_operand_aliasing={{}: (3, {})} | custom-call | tf_op jit(solution)/shard_map/add_received/pallas_call | solution.py:203
  204.2 3.0 %all-to-all-done.received = bf16[128,16,256]{2,1,0:T(8,128)(2,1)} async-done(((bf16[128,16,256]{2,1,0:T(8,128)(2,1)}), bf16[128,16,256]{2,1,0:T(8,128)(2,1)}, u32[]{:S(2)}, u32[]{:S(2)}) %all-to-all-start) | async-done | bytes 1048608 | tf_op jit(solution)/shard_map/all_to_all | solution.py:292
  207.3 4.3 %add_received.7 = f32[16,64,256]{2,1,0:T(8,128)} custom-call(s32[128]{0:T(128)S(1)} %sub.50.places, bf16[128,16,256]{2,1,0:T(8,128)(2,1)} %all-to-all-done.received, f32[16,16,256]{2,1,0:T(8,128)S(1)} %copy-done.23, f32[16,64,256]{2,1,0:T(8,128)} %add_received.6.rest_0_), custom_call_target="tpu_custom_call", output_to_operand_aliasing={{}: (3, {})} | custom-call | tf_op jit(solution)/shard_map/add_received/pallas_call | solution.py:203
  (112 shorter events, 46.5 us)
Async XLA Ops:
  1.6 1.6 copy-start.24
  31.4 8.7 %copy-start.25 = (s32[512,4]{0,1:T(4,128)S(1)}, s32[512,4]{0,1:T(4,128)}, u32[]{:S(2)}) copy-start(s32[512,4]{0,1:T(4,128)} %param.13) | copy-start | bytes 24580
  32.3 17.6 %collective-permute-start.14 = (bf16[80,2,16,128]{3,2,0,1:T(8,128)(2,1)}, bf16[80,2,16,128]{3,2,0,1:T(8,128)(2,1)}, u32[]{:S(2)}, u32[]{:S(2)}) collective-permute-start(bf16[80,2,16,128]{3,2,0,1:T(8,128)(2,1)} %copy.82), channel_id=1, source_target_pairs={{0,3},{1,2},{2,1},{3,0},{4,7},{5,6},{6,5},{7,4},{8,11},{9,10},{10,... | collective-permute-start | bytes 1966088 | tf_op jit(solution)/shard_map/ppermute | solution.py:280
  36.6 15.6 %collective-permute-start.12 = (bf16[80,2,16,128]{3,2,0,1:T(8,128)(2,1)}, bf16[80,2,16,128]{3,2,0,1:T(8,128)(2,1)}, u32[]{:S(2)}, u32[]{:S(2)}) collective-permute-start(bf16[80,2,16,128]{3,2,0,1:T(8,128)(2,1)} %copy.80), channel_id=1, source_target_pairs={{0,1},{1,0},{2,3},{3,2},{4,5},{5,4},{6,7},{7,6},{8,9},{9,8},{10,11... | collective-permute-start | bytes 1966088 | tf_op jit(solution)/shard_map/ppermute | solution.py:279
  37.6 52.0 %collective-permute-start.10 = (bf16[80,2,16,128]{3,2,0,1:T(8,128)(2,1)}, bf16[80,2,16,128]{3,2,0,1:T(8,128)(2,1)}, u32[]{:S(2)}, u32[]{:S(2)}) collective-permute-start(bf16[80,2,16,128]{3,2,0,1:T(8,128)(2,1)} %copy.76), channel_id=1, source_target_pairs={{0,3},{1,2},{2,1},{3,0},{4,7},{5,6},{6,5},{7,4},{8,11},{9,10},{10,... | collective-permute-start | bytes 1966088 | tf_op jit(solution)/shard_map/ppermute | solution.py:280
  39.4 51.5 %collective-permute-start.8 = (bf16[80,2,16,128]{3,2,0,1:T(8,128)(2,1)}, bf16[80,2,16,128]{3,2,0,1:T(8,128)(2,1)}, u32[]{:S(2)}, u32[]{:S(2)}) collective-permute-start(bf16[80,2,16,128]{3,2,0,1:T(8,128)(2,1)} %copy.74), channel_id=1, source_target_pairs={{0,1},{1,0},{2,3},{3,2},{4,5},{5,4},{6,7},{7,6},{8,9},{9,8},{10,11... | collective-permute-start | bytes 1966088 | tf_op jit(solution)/shard_map/ppermute | solution.py:279
  51.1 22.0 %collective-permute-start.15 = (bf16[80,16,128]{2,1,0:T(8,128)(2,1)S(1)}, bf16[80,16,128]{2,1,0:T(8,128)(2,1)S(1)}, u32[]{:S(2)}, u32[]{:S(2)}) collective-permute-start(bf16[80,16,128]{2,1,0:T(8,128)(2,1)S(1)} %fusion.7), channel_id=1, source_target_pairs={{0,1},{1,0},{2,3},{3,2},{4,5},{5,4},{6,7},{7,6},{8,9},{9,8},{10,11... | collective-permute-start | bytes 983048 | tf_op jit(solution)/shard_map/ppermute | solution.py:288
  53.2 19.9 %collective-permute-start.13 = (bf16[80,16,128]{2,1,0:T(8,128)(2,1)S(1)}, bf16[80,16,128]{2,1,0:T(8,128)(2,1)S(1)}, u32[]{:S(2)}, u32[]{:S(2)}) collective-permute-start(bf16[80,16,128]{2,1,0:T(8,128)(2,1)S(1)} %fusion.6), channel_id=1, source_target_pairs={{0,3},{1,2},{2,1},{3,0},{4,7},{5,6},{6,5},{7,4},{8,11},{9,10},{10,... | collective-permute-start | bytes 983048 | tf_op jit(solution)/shard_map/ppermute | solution.py:287
  73.1 1.1 copy-start.7
  75.6 1.0 copy-start.9
  77.3 39.7 %all-to-all-start.3 = ((bf16[128,16,256]{2,1,0:T(8,128)(2,1)}), bf16[128,16,256]{2,1,0:T(8,128)(2,1)S(1)}, u32[]{:S(2)}, u32[]{:S(2)}) async-start(bf16[128,16,256]{2,1,0:T(8,128)(2,1)} %copy-done.9), calls=%async_computation.3 | async-start | bytes 2097152 | tf_op jit(solution)/shard_map/all_to_all | solution.py:292
  87.3 26.7 %copy-start.5 = (bf16[80,2,16,128]{3,2,1,0:T(8,128)(2,1)S(1)}, bf16[80,2,16,128]{3,2,1,0:T(8,128)(2,1)}, u32[]{:S(2)}) copy-start(bf16[80,2,16,128]{3,2,1,0:T(8,128)(2,1)} %copy-done.4) | copy-start | bytes 1966084
  89.4 38.0 %collective-permute-start.6 = (bf16[80,2,16,128]{3,2,0,1:T(8,128)(2,1)}, bf16[80,2,16,128]{3,2,0,1:T(8,128)(2,1)}, u32[]{:S(2)}, u32[]{:S(2)}) collective-permute-start(bf16[80,2,16,128]{3,2,0,1:T(8,128)(2,1)} %copy.70), channel_id=1, source_target_pairs={{0,3},{1,2},{2,1},{3,0},{4,7},{5,6},{6,5},{7,4},{8,11},{9,10},{10,... | collective-permute-start | bytes 1966088 | tf_op jit(solution)/shard_map/ppermute | solution.py:280
  90.8 9.0 %collective-permute-start.11 = (bf16[80,16,128]{2,1,0:T(8,128)(2,1)S(1)}, bf16[80,16,128]{2,1,0:T(8,128)(2,1)S(1)}, u32[]{:S(2)}, u32[]{:S(2)}) collective-permute-start(bf16[80,16,128]{2,1,0:T(8,128)(2,1)S(1)} %fusion.5), channel_id=1, source_target_pairs={{0,1},{1,0},{2,3},{3,2},{4,5},{5,4},{6,7},{7,6},{8,9},{9,8},{10,11... | collective-permute-start | bytes 983048 | tf_op jit(solution)/shard_map/ppermute | solution.py:288
  92.0 21.9 %collective-permute-start.9 = (bf16[80,16,128]{2,1,0:T(8,128)(2,1)S(1)}, bf16[80,16,128]{2,1,0:T(8,128)(2,1)S(1)}, u32[]{:S(2)}, u32[]{:S(2)}) collective-permute-start(bf16[80,16,128]{2,1,0:T(8,128)(2,1)S(1)} %fusion.4), channel_id=1, source_target_pairs={{0,3},{1,2},{2,1},{3,0},{4,7},{5,6},{6,5},{7,4},{8,11},{9,10},{10,... | collective-permute-start | bytes 983048 | tf_op jit(solution)/shard_map/ppermute | solution.py:287
  96.5 32.0 %collective-permute-start.4 = (bf16[80,2,16,128]{3,2,0,1:T(8,128)(2,1)}, bf16[80,2,16,128]{3,2,0,1:T(8,128)(2,1)}, u32[]{:S(2)}, u32[]{:S(2)}) collective-permute-start(bf16[80,2,16,128]{3,2,0,1:T(8,128)(2,1)} %copy.68), channel_id=1, source_target_pairs={{0,1},{1,0},{2,3},{3,2},{4,5},{5,4},{6,7},{7,6},{8,9},{9,8},{10,11... | collective-permute-start | bytes 1966088 | tf_op jit(solution)/shard_map/ppermute | solution.py:279
  115.3 1.0 copy-start.8
  117.0 37.7 %all-to-all-start.2 = ((bf16[128,16,256]{2,1,0:T(8,128)(2,1)}), bf16[128,16,256]{2,1,0:T(8,128)(2,1)S(1)}, u32[]{:S(2)}, u32[]{:S(2)}) async-start(bf16[128,16,256]{2,1,0:T(8,128)(2,1)} %copy-done.8), calls=%async_computation.2 | async-start | bytes 2097152 | tf_op jit(solution)/shard_map/all_to_all | solution.py:292
  127.1 35.7 %collective-permute-start.2 = (bf16[80,2,16,128]{3,2,0,1:T(8,128)(2,1)}, bf16[80,2,16,128]{3,2,0,1:T(8,128)(2,1)}, u32[]{:S(2)}, u32[]{:S(2)}) collective-permute-start(bf16[80,2,16,128]{3,2,0,1:T(8,128)(2,1)} %copy.64), channel_id=1, source_target_pairs={{0,3},{1,2},{2,1},{3,0},{4,7},{5,6},{6,5},{7,4},{8,11},{9,10},{10,... | collective-permute-start | bytes 1966088 | tf_op jit(solution)/shard_map/ppermute | solution.py:280
  128.4 9.0 %collective-permute-start.7 = (bf16[80,16,128]{2,1,0:T(8,128)(2,1)S(1)}, bf16[80,16,128]{2,1,0:T(8,128)(2,1)S(1)}, u32[]{:S(2)}, u32[]{:S(2)}) collective-permute-start(bf16[80,16,128]{2,1,0:T(8,128)(2,1)S(1)} %fusion.3), channel_id=1, source_target_pairs={{0,1},{1,0},{2,3},{3,2},{4,5},{5,4},{6,7},{7,6},{8,9},{9,8},{10,11... | collective-permute-start | bytes 983048 | tf_op jit(solution)/shard_map/ppermute | solution.py:288
  129.6 22.0 %collective-permute-start.5 = (bf16[80,16,128]{2,1,0:T(8,128)(2,1)S(1)}, bf16[80,16,128]{2,1,0:T(8,128)(2,1)S(1)}, u32[]{:S(2)}, u32[]{:S(2)}) collective-permute-start(bf16[80,16,128]{2,1,0:T(8,128)(2,1)S(1)} %fusion.2), channel_id=1, source_target_pairs={{0,3},{1,2},{2,1},{3,0},{4,7},{5,6},{6,5},{7,4},{8,11},{9,10},{10,... | collective-permute-start | bytes 983048 | tf_op jit(solution)/shard_map/ppermute | solution.py:287
  134.2 30.6 %collective-permute-start = (bf16[80,2,16,128]{3,2,0,1:T(8,128)(2,1)}, bf16[80,2,16,128]{3,2,0,1:T(8,128)(2,1)}, u32[]{:S(2)}, u32[]{:S(2)}) collective-permute-start(bf16[80,2,16,128]{3,2,0,1:T(8,128)(2,1)} %copy.62), channel_id=1, source_target_pairs={{0,1},{1,0},{2,3},{3,2},{4,5},{5,4},{6,7},{7,6},{8,9},{9,8},{10,11... | collective-permute-start | bytes 1966088 | tf_op jit(solution)/shard_map/ppermute | solution.py:279
  153.1 1.0 copy-start.10
  154.7 28.0 %all-to-all-start.1 = ((bf16[128,16,256]{2,1,0:T(8,128)(2,1)}), bf16[128,16,256]{2,1,0:T(8,128)(2,1)S(1)}, u32[]{:S(2)}, u32[]{:S(2)}) async-start(bf16[128,16,256]{2,1,0:T(8,128)(2,1)} %copy-done.10), calls=%async_computation.1 | async-start | bytes 2097152 | tf_op jit(solution)/shard_map/all_to_all | solution.py:292
  164.7 9.4 %collective-permute-start.3 = (bf16[80,16,128]{2,1,0:T(8,128)(2,1)}, bf16[80,16,128]{2,1,0:T(8,128)(2,1)}, u32[]{:S(2)}, u32[]{:S(2)}) collective-permute-start(bf16[80,16,128]{2,1,0:T(8,128)(2,1)} %fusion.1), channel_id=1, source_target_pairs={{0,1},{1,0},{2,3},{3,2},{4,5},{5,4},{6,7},{7,6},{8,9},{9,8},{10,11... | collective-permute-start | bytes 983048 | tf_op jit(solution)/shard_map/ppermute | solution.py:288
  166.6 10.6 %collective-permute-start.1 = (bf16[80,16,128]{2,1,0:T(8,128)(2,1)}, bf16[80,16,128]{2,1,0:T(8,128)(2,1)}, u32[]{:S(2)}, u32[]{:S(2)}) collective-permute-start(bf16[80,16,128]{2,1,0:T(8,128)(2,1)} %fusion), channel_id=1, source_target_pairs={{0,3},{1,2},{2,1},{3,0},{4,7},{5,6},{6,5},{7,4},{8,11},{9,10},{10,... | collective-permute-start | bytes 983048 | tf_op jit(solution)/shard_map/ppermute | solution.py:287
  177.2 1.1 copy-start.1
  178.3 1.1 copy-start.3
  181.8 1.0 copy-start.11
  182.8 9.5 %copy-start.22 = (f32[16,16,256]{2,1,0:T(8,128)}, f32[16,16,256]{2,1,0:T(8,128)S(1)}, u32[]{:S(2)}) copy-start(f32[16,16,256]{2,1,0:T(8,128)S(1)} %get-tuple-element.34.own) | copy-start | bytes 786436
  182.8 24.5 %all-to-all-start = ((bf16[128,16,256]{2,1,0:T(8,128)(2,1)}), bf16[128,16,256]{2,1,0:T(8,128)(2,1)}, u32[]{:S(2)}, u32[]{:S(2)}) async-start(bf16[128,16,256]{2,1,0:T(8,128)(2,1)} %copy-done.11), calls=%async_computation | async-start | bytes 2097152 | tf_op jit(solution)/shard_map/all_to_all | solution.py:292
  197.2 10.1 %copy-start.23 = (f32[16,16,256]{2,1,0:T(8,128)S(1)}, f32[16,16,256]{2,1,0:T(8,128)}, u32[]{:S(2)}) copy-start(f32[16,16,256]{2,1,0:T(8,128)} %copy-done.22) | copy-start | bytes 786436
  (14 other events, 11.7 us)

commit v2 on v1

--- a/solution.py
+++ b/solution.py
@@ -8,19 +8,19 @@
 from jax.sharding import PartitionSpec as P
 
 LANES = 128
-ROW_CHUNKS = (16, 16, 16, 16)
+EARLY_ROWS = 16
+ROW_CHUNKS = (16, 32)
 
 
 def products_kernel(
     chunks, x_ref, left_ids, right_ids, class_ids, first_ref, psi_ref, left_hbm, right_hbm, *rest
 ):
-    chunk_count = len(chunks)
-    outs = rest[: 4 * chunk_count]
-    left_ref, right_ref, half_ref, acc_ref, left_sems, right_sems = rest[4 * chunk_count :]
+    count = 2 + 4 * len(chunks)
+    early_own, early_moved, *outs = rest[:count]
+    left_ref, right_ref, half_ref, acc_ref, left_sems, right_sems = rest[count:]
     channels = left_ref.shape[0]
     classes = acc_ref.shape[0]
-    block = acc_ref.shape[1]
-    quarter = block // 4
+    quarter = acc_ref.shape[1] // 4
     step = pl.program_id(0)
 
     def left_copy(w):
@@ -28,6 +28,23 @@
 
     def right_copy(w):
         return pltpu.make_async_copy(right_hbm.at[w], right_ref.at[w], right_sems.at[w])
+
+    def multiply(arriving):
+        left_id = left_ids[step]
+        right_id = right_ids[step]
+        for w in range(channels):
+            if arriving:
+                left_copy(w).wait()
+            half_ref[w] = jnp.dot(
+                left_ref[w, left_id], psi_ref[0], preferred_element_type=jnp.float32
+            ).astype(jnp.bfloat16)
+        for w in range(channels):
+            if arriving:
+                right_copy(w).wait()
+            full = jnp.dot(half_ref[w], right_ref[w, right_id], preferred_element_type=jnp.float32)
+            member = class_ids[w]
+            before = acc_ref[member]
+            acc_ref[member] = jnp.where(first_ref[w] != 0, 0.0, before) + full
 
     @pl.when(step == 0)
     def _():
@@ -36,30 +53,24 @@
         for w in range(channels):
             right_copy(w).start()
         acc_ref[...] = jnp.zeros_like(acc_ref)
-        for w in range(channels):
-            left_copy(w).wait()
-        for w in range(channels):
-            right_copy(w).wait()
-
-    left_id = left_ids[step]
-    right_id = right_ids[step]
-    psi = psi_ref[0]
-    for w in range(channels):
-        half_ref[w] = jnp.dot(
-            left_ref[w, left_id], psi, preferred_element_type=jnp.float32
-        ).astype(jnp.bfloat16)
-    for w in range(channels):
-        full = jnp.dot(half_ref[w], right_ref[w, right_id], preferred_element_type=jnp.float32)
-        member = class_ids[w]
-        before = acc_ref[member]
-        acc_ref[member] = jnp.where(first_ref[w] != 0, 0.0, before) + full
+        multiply(True)
+
+    @pl.when(step != 0)
+    def _():
+        multiply(False)
 
     x = x_ref[0]
     mirror = 3 - x
     beside = x ^ 1
     across = mirror ^ 1
     orders = ((x, mirror, beside, across), (x, beside, mirror, across))
-    start = 0
+    for q in range(4):
+        rows = slice(q * EARLY_ROWS, (q + 1) * EARLY_ROWS)
+        at = q * quarter
+        early_own[0, rows] = acc_ref[0, at : at + EARLY_ROWS].astype(jnp.bfloat16)
+        for c in range(1, classes):
+            early_moved[c - 1, rows] = acc_ref[c, at : at + EARLY_ROWS].astype(jnp.bfloat16)
+    start = EARLY_ROWS
     for j, rows in enumerate(chunks):
         for s in range(2):
             keep, send = outs[4 * j + 2 * s], outs[4 * j + 2 * s + 1]
@@ -67,7 +78,7 @@
                 target = keep if place < 2 else send
                 at = pl.multiple_of(q * quarter + start, 16)
                 for c in range(classes):
-                    target[c, place % 2] = acc_ref[
+                    target[place % 2, c] = acc_ref[
                         c, pl.ds(at, rows), s * LANES : (s + 1) * LANES
                     ].astype(jnp.bfloat16)
         start += rows
@@ -76,15 +87,20 @@
 def products(x, left_ids, right_ids, class_ids, first, psi, left_env, right_env, classes, chunks):
     blocks, block, _ = psi.shape
     channels = left_env.shape[0]
-    out_shape, out_specs = [], []
+    early = 4 * EARLY_ROWS
+    hops = classes - 1
+    out_shape = [
+        pltpu.HBM((blocks, early, block), jnp.bfloat16),
+        pltpu.HBM((blocks * hops, early, block), jnp.bfloat16),
+    ]
+    out_specs = [
+        pl.BlockSpec((1, early, block), lambda k, *_: (k, 0, 0)),
+        pl.BlockSpec((hops, early, block), lambda k, *_: (k, 0, 0)),
+    ]
     for rows in chunks:
         for _ in range(4):
-            out_shape.append(
-                jax.ShapeDtypeStruct((blocks * classes, 2, rows, LANES), jnp.bfloat16)
-            )
-            out_specs.append(
-                pl.BlockSpec((classes, 2, rows, LANES), lambda k, *_: (k, 0, 0, 0))
-            )
+            out_shape.append(pltpu.HBM((2, blocks * classes, rows, LANES), jnp.bfloat16))
+            out_specs.append(pl.BlockSpec((2, classes, rows, LANES), lambda k, *_: (0, k, 0, 0)))
     return pl.pallas_call(
         functools.partial(products_kernel, chunks),
         out_shape=out_shape,
@@ -116,14 +132,72 @@
     )(x, left_ids, right_ids, class_ids, first, psi, left_env, right_env)
 
 
+def place_kernel(items, moved, slots):
+    def fill(p, _):
+        slots[p] = moved[items[p]]
+        return 0
+
+    lax.fori_loop(0, slots.shape[0], fill, 0, unroll=4)
+
+
+def place_items(items, moved):
+    slot_count = items.shape[0]
+    _, rows, width = moved.shape
+    return pl.pallas_call(
+        place_kernel,
+        out_shape=pltpu.HBM((slot_count, rows, width), jnp.bfloat16),
+        grid_spec=pltpu.PrefetchScalarGridSpec(
+            num_scalar_prefetch=1,
+            grid=(1,),
+            in_specs=[pl.BlockSpec(moved.shape, lambda i, *_: (0, 0, 0))],
+            out_specs=pl.BlockSpec((slot_count, rows, width), lambda i, *_: (0, 0, 0)),
+        ),
+        compiler_params=pltpu.CompilerParams(vmem_limit_bytes=32 * 2**20),
+        name="place_items",
+    )(items, moved)
+
+
+def merge_kernel(places, received, own, out, acc):
+    blocks, rows, _ = own.shape
+    acc[:blocks] = own[...].astype(jnp.float32)
+
+    def add(p, _):
+        acc[places[p]] += received[p].astype(jnp.float32)
+        return 0
+
+    lax.fori_loop(0, received.shape[0], add, 0, unroll=4)
+    for q in range(4):
+        out[q] = acc[:blocks, q * (rows // 4) : (q + 1) * (rows // 4)].astype(jnp.bfloat16)
+
+
+def merge_early(places, received, own):
+    blocks, rows, width = own.shape
+    return pl.pallas_call(
+        merge_kernel,
+        out_shape=pltpu.HBM((4, blocks, rows // 4, width), jnp.bfloat16),
+        grid_spec=pltpu.PrefetchScalarGridSpec(
+            num_scalar_prefetch=1,
+            grid=(1,),
+            in_specs=[
+                pl.BlockSpec(received.shape, lambda i, *_: (0, 0, 0)),
+                pl.BlockSpec(own.shape, lambda i, *_: (0, 0, 0)),
+            ],
+            out_specs=pl.BlockSpec((4, blocks, rows // 4, width), lambda i, *_: (0, 0, 0, 0)),
+            scratch_shapes=[pltpu.VMEM((blocks + 1, rows, width), jnp.float32)],
+        ),
+        compiler_params=pltpu.CompilerParams(vmem_limit_bytes=32 * 2**20),
+        name="merge_early",
+    )(places, received, own)
+
+
 def slots_kernel(classes, items, keep_a, got_a, last_a, keep_b, got_b, last_b, slots, own):
     slot_count = slots.shape[0]
     block_count = own.shape[0]
 
     def total(keep, got, last, i):
         return (
-            keep[i, 0].astype(jnp.float32)
-            + got[i, 0].astype(jnp.float32)
+            keep[0, i].astype(jnp.float32)
+            + got[0, i].astype(jnp.float32)
             + last[i].astype(jnp.float32)
         )
 
@@ -146,16 +220,16 @@
 
 def fill_slots(items, parts, classes):
     keep_a, got_a, last_a, keep_b, got_b, last_b = parts
-    count, _, rows, _ = keep_a.shape
+    _, count, rows, _ = keep_a.shape
     blocks = count // classes
-    pair = pl.BlockSpec((count, 1, rows, LANES), lambda i, *_: (0, 0, 0, 0))
+    pair = pl.BlockSpec((1, count, rows, LANES), lambda i, *_: (0, 0, 0, 0))
     one = pl.BlockSpec((count, rows, LANES), lambda i, *_: (0, 0, 0))
     slot_count = items.shape[0]
     return pl.pallas_call(
         functools.partial(slots_kernel, classes),
         out_shape=(
-            jax.ShapeDtypeStruct((slot_count, rows, 2 * LANES), jnp.bfloat16),
-            jax.ShapeDtypeStruct((blocks, rows, 2 * LANES), jnp.float32),
+            pltpu.HBM((slot_count, rows, 2 * LANES), jnp.bfloat16),
+            pltpu.HBM((blocks, rows, 2 * LANES), jnp.float32),
         ),
         grid_spec=pltpu.PrefetchScalarGridSpec(
             num_scalar_prefetch=1,
@@ -171,48 +245,60 @@
     )(items, keep_a, got_a, last_a, keep_b, got_b, last_b)
 
 
-def gather_kernel(places, received, own, *rest):
-    result = rest[-1]
-    result[...] = own[...]
-
-    def add(p, _):
-        b = places[p]
-
-        @pl.when(b >= 0)
-        def _():
-            result[b] += received[p].astype(jnp.float32)
-
-        return 0
-
-    lax.fori_loop(0, received.shape[0], add, 0)
-
-
-def add_received(places, received, own, so_far, start, quarter):
+def add_received(places, received, own, so_far, start):
     blocks, rows, width = own.shape
-    at = start // rows
-    operands = [places, received, own]
-    in_specs = [
-        pl.BlockSpec(received.shape, lambda i, *_: (0, 0, 0)),
-        pl.BlockSpec(own.shape, lambda i, *_: (0, 0, 0)),
-    ]
-    aliases = {}
-    if so_far is not None:
-        operands.append(so_far)
-        in_specs.append(pl.BlockSpec(memory_space=pl.ANY))
-        aliases = {3: 0}
-    return pl.pallas_call(
-        gather_kernel,
-        out_shape=jax.ShapeDtypeStruct((blocks, quarter, width), jnp.float32),
+
+    def kernel(places, received, own, so_far, result, acc, sem):
+        acc[:blocks] = own[...]
+
+        def add(p, _):
+            acc[places[p]] += received[p].astype(jnp.float32)
+            return 0
+
+        lax.fori_loop(0, received.shape[0], add, 0, unroll=4)
+        copy = pltpu.make_async_copy(
+            acc.at[pl.ds(0, blocks)], result.at[:, pl.ds(start, rows)], sem
+        )
+        copy.start()
+        copy.wait()
+
+    return pl.pallas_call(
+        kernel,
+        out_shape=pltpu.HBM(so_far.shape, jnp.float32),
         grid_spec=pltpu.PrefetchScalarGridSpec(
             num_scalar_prefetch=1,
             grid=(1,),
-            in_specs=in_specs,
-            out_specs=pl.BlockSpec((blocks, rows, width), lambda i, *_: (0, at, 0)),
-        ),
-        input_output_aliases=aliases,
+            in_specs=[
+                pl.BlockSpec(received.shape, lambda i, *_: (0, 0, 0)),
+                pl.BlockSpec(own.shape, lambda i, *_: (0, 0, 0)),
+                pl.BlockSpec(memory_space=pl.ANY),
+            ],
+            out_specs=pl.BlockSpec(memory_space=pl.ANY),
+            scratch_shapes=[
+                pltpu.VMEM((blocks + 1, rows, width), jnp.float32),
+                pltpu.SemaphoreType.DMA,
+            ],
+        ),
+        input_output_aliases={3: 0},
         compiler_params=pltpu.CompilerParams(vmem_limit_bytes=32 * 2**20),
         name="add_received",
-    )(*operands)
+    )(places, received, own, so_far)
+
+
+def place_early(scattered, quarter):
+    blocks, rows, width = scattered.shape
+
+    def kernel(scattered, result):
+        result[...] = scattered[...].astype(jnp.float32)
+
+    return pl.pallas_call(
+        kernel,
+        out_shape=pltpu.HBM((blocks, quarter, width), jnp.float32),
+        grid=(1,),
+        in_specs=[pl.BlockSpec((blocks, rows, width), lambda i: (0, 0, 0))],
+        out_specs=pl.BlockSpec((blocks, rows, width), lambda i: (0, 0, 0)),
+        name="place_early",
+    )(scattered)
 
 
 def item_places(targets, block_count):
@@ -242,7 +328,7 @@
     seen = jnp.any((group_class[:, None] == group_class[None, :]) & (w[:, None] > w[None, :]), 1)
     first = jnp.logical_not(seen).astype(jnp.int32)
 
-    parts = products(
+    early_own, early_moved, *parts = products(
         x.astype(jnp.int32)[None],
         local_left,
         local_right,
@@ -267,22 +353,30 @@
     mine = (destined_all == me)[:, :, None] & (
         slot_all[:, :, None] == jnp.arange(capacity, dtype=jnp.int32)
     )
-    local = targets - me * block_count + 1
-    places = jnp.sum(jnp.where(mine, local[:, :, None], 0), axis=1).reshape(slot_count) - 1
+    local = targets - (me + 1) * block_count
+    places = jnp.sum(jnp.where(mine, local[:, :, None], 0), axis=1).reshape(slot_count)
+    places = places + block_count
+    plain_items = jnp.sum(
+        jnp.where(held, jnp.arange(item_count, dtype=jnp.int32)[:, None], 0), axis=0
+    )
+
+    early = lax.all_to_all(
+        place_items(plain_items, early_moved), ("lsec", "rsec"), 0, 0, tiled=True
+    )
+    merged = merge_early(places, early, early_own)
+    scattered = lax.psum_scatter(merged, "mpo", scatter_dimension=0, tiled=False)
+    result = place_early(scattered, quarter)
 
     beside = [(i, i ^ 1) for i in range(4)]
     mirror = [(i, 3 - i) for i in range(4)]
-    result = None
-    start = 0
+    start = EARLY_ROWS
     for j, rows in enumerate(ROW_CHUNKS):
         keep_a, send_a, keep_b, send_b = parts[4 * j : 4 * j + 4]
         got_a = lax.ppermute(send_a, "mpo", beside)
         got_b = lax.ppermute(send_b, "mpo", mirror)
 
         def second(keep, got):
-            return (
-                keep[:, 1].astype(jnp.float32) + got[:, 1].astype(jnp.float32)
-            ).astype(jnp.bfloat16)
+            return (keep[1].astype(jnp.float32) + got[1].astype(jnp.float32)).astype(jnp.bfloat16)
 
         last_a = lax.ppermute(second(keep_a, got_a), "mpo", mirror)
         last_b = lax.ppermute(second(keep_b, got_b), "mpo", beside)
@@ -290,7 +384,7 @@
             slot_items, (keep_a, got_a, last_a, keep_b, got_b, last_b), classes
         )
         received = lax.all_to_all(slots, ("lsec", "rsec"), 0, 0, tiled=True)
-        result = add_received(places, received, own, result, start, quarter)
+        result = add_received(places, received, own, result, start)
         start += rows
     return result
 

time: 213 us -> 210 us (0.986)
  waiting for transfers between devices: 64.9 us -> 96.7 us
  local copies, waits for them, and re-layouts: 43.4 us -> 13.9 us
  starting transfers between devices: 48.9 us -> 35.3 us
  between operations: 0.34 us -> 13.6 us
  other arithmetic: 12.7 us -> 5.9 us
    ppermute x4 -> x2, waiting for transfers between devices: 0.67 us -> 41 us  [shards(): got_a = lax.ppermute(send_a, 'mpo', beside)]
    reduce_scatter x0 -> x1, waiting for transfers between devices: none -> 20 us  [shards(): lax.psum_scatter(merged, 'mpo', scatter_dimension=0, tiled=False)]
    ppermute x4 -> x2, waiting for transfers between devices: 20.3 us -> 2.1 us  [shards(): last_b = lax.ppermute(second(keep_b, got_b), 'mpo', beside)]
    all_to_all x4 -> x2, starting transfers between devices: 34.2 us -> 20.5 us  [shards(): received = lax.all_to_all(slots, ('lsec', 'rsec'), 0, 0, tiled=True)]
    pallas_call x8 -> x0, local copies, waits for them, and re-layouts: 12.2 us -> none  [products(): pl.pallas_call(functools.partial(products_kernel, chunks), out_shape=out_...]
    ppermute x4 -> x2, waiting for transfers between devices: 31.5 us -> 20.3 us  [shards(): last_a = lax.ppermute(second(keep_a, got_a), 'mpo', mirror)]
    all_to_all x4 -> x2, waiting for transfers between devices: 3.03 us -> 13.4 us  [shards(): received = lax.all_to_all(slots, ('lsec', 'rsec'), 0, 0, tiled=True)]
    ppermute x8 -> x0, local copies, waits for them, and re-layouts: 9.61 us -> none  [the longest x4 4.8 us: shards(): got_a = lax.ppermute(send_a, 'mpo', beside)]
  transfers between devices with their start and end apart: 20 -> 12, of which waited for: 8 -> 8; matrix products, arithmetic and copies ran while one was open for 16% -> 3% of each run, Pallas kernels for 7% -> 7%
where the time goes in v2:
time: 210 us; the launch traced here: 208 us
  waiting for transfers between devices  96.7 us (46%)
  Pallas kernels  43.1 us (21%)
  starting transfers between devices  35.3 us (17%)
  local copies, waits for them, and re-layouts  13.9 us (7%)
  between operations  13.6 us (6%)
  other arithmetic  5.9 us (3%)
    ppermute x2, waiting for transfers between devices, shards(): got_a = lax.ppermute(send_a, 'mpo', beside)  41 us
    pallas_call x1, Pallas kernels, products(): pl.pallas_call(functools.partial(products_kernel, chunks), out_shape=out_...  23.2 us
    all_to_all x2, starting transfers between devices, shards(): received = lax.all_to_all(slots, ('lsec', 'rsec'), 0, 0, tiled=True)  20.5 us
    ppermute x2, waiting for transfers between devices, shards(): last_a = lax.ppermute(second(keep_a, got_a), 'mpo', mirror)  20.3 us
    reduce_scatter x1, waiting for transfers between devices, shards(): lax.psum_scatter(merged, 'mpo', scatter_dimension=0, tiled=False)  20 us
    all_to_all x2, waiting for transfers between devices, shards(): received = lax.all_to_all(slots, ('lsec', 'rsec'), 0, 0, tiled=True)  13.4 us
    unnamed x35, local copies, waits for them, and re-layouts  12.8 us
    pallas_call x2, Pallas kernels, fill_slots(): pl.pallas_call(functools.partial(slots_kernel, classes), out_shape=(pltpu...  6.68 us
  transfers between devices with their start and end apart: 12, of which 8 were waited for; matrix products, arithmetic and copies ran while one was open for 3% of the time, Pallas kernels for 7%

profile of v2, /device:TPU:1, one launch (start us, length us, event | category | flops | bytes accessed | tf_op | source)
XLA Modules:
  0.0 208.4 jit_solution(18070698507192272307)
XLA Ops:
  8.1 2.5 %copy-done.13 = bf16[10,4,256,256]{3,2,1,0:T(8,128)(2,1)S(1)} copy-done((bf16[10,4,256,256]{3,2,1,0:T(8,128)(2,1)S(1)}, bf16[10,4,256,256]{3,2,1,0:T(8,128)(2,1)}, u32[]{:S(2)}) %copy-start.13) | copy-done | bytes 5242904
  10.6 2.5 %copy-done.14 = bf16[10,4,256,256]{3,2,1,0:T(8,128)(2,1)S(1)} copy-done((bf16[10,4,256,256]{3,2,1,0:T(8,128)(2,1)S(1)}, bf16[10,4,256,256]{3,2,1,0:T(8,128)(2,1)}, u32[]{:S(2)}) %copy-start.14) | copy-done | bytes 5242904
  13.1 1.6 copy-done.15
  14.7 23.2 %products.1 = (bf16[16,64,256]{2,1,0:T(8,128)(2,1)}, bf16[64,64,256]{2,1,0:T(8,128)(2,1)}, bf16[2,80,16,128]{3,2,1,0:T(8,128)(2,1)}, bf16[2,80,16,128]{3,2,1,0:T...) custom-call(s32[1]{0:T(128)} %bitcast.2.x_ref, ...), custom_call_target="tpu_custom_call" | custom-call | flops 10737418240 | bytes 23068672 | tf_op jit(solution)/shard_map/products/pallas_call | solution.py:104
  37.9 2.1 %collective-permute-start.4 = (bf16[2,80,16,128]{3,2,1,0:T(8,128)(2,1)}, bf16[2,80,16,128]{3,2,1,0:T(8,128)(2,1)S(1)}, u32[]{:S(2)}, u32[]{:S(2)}) collective-permute-start(bf16[2,80,16,128]{3,2,1,0:T(8,128)(2,1)} %get-tuple-element.26), channel_id=1, source_target_pairs={{0,1},{1,0},{2,3},{3,2},{4,5},{5,4},{6,7},{7,6},{8,9},{9,8},{10,11... | collective-permute-start | bytes 1966088 | tf_op jit(solution)/shard_map/ppermute | solution.py:375
  40.0 1.8 collective-permute-start.6
  42.4 11.8 %collective-permute-done.4.got_a = bf16[2,80,16,128]{3,2,1,0:T(8,128)(2,1)S(1)} collective-permute-done((bf16[2,80,16,128]{3,2,1,0:T(8,128)(2,1)}, bf16[2,80,16,128]{3,2,1,0:T(8,128)(2,1)S(1)}, u32[]{:S(2)}, u32[]{:S(2)}) %collective-permute-start.4) | collective-permute-done | bytes 655392 | tf_op jit(solution)/shard_map/ppermute | solution.py:375
  54.2 1.1 fusion.2
  55.2 3.0 %collective-permute-start.5 = (bf16[80,16,128]{2,1,0:T(8,128)(2,1)S(1)}, bf16[80,16,128]{2,1,0:T(8,128)(2,1)S(1)}, u32[]{:S(2)}, u32[]{:S(2)}) collective-permute-start(bf16[80,16,128]{2,1,0:T(8,128)(2,1)S(1)} %fusion.2), channel_id=1, source_target_pairs={{0,3},{1,2},{2,1},{3,0},{4,7},{5,6},{6,5},{7,4},{8,11},{9,10},{10,... | collective-permute-start | bytes 983048 | tf_op jit(solution)/shard_map/ppermute | solution.py:381
  58.6 5.9 %collective-permute-done.5.last_a = bf16[80,16,128]{2,1,0:T(8,128)(2,1)S(1)} collective-permute-done((bf16[80,16,128]{2,1,0:T(8,128)(2,1)S(1)}, bf16[80,16,128]{2,1,0:T(8,128)(2,1)S(1)}, u32[]{:S(2)}, u32[]{:S(2)}) %collective-permute-start.5) | collective-permute-done | bytes 327712 | tf_op jit(solution)/shard_map/ppermute | solution.py:381
  64.5 1.3 collective-permute-done.7.last_b
  65.8 2.3 %fill_slots.3 = (bf16[128,16,256]{2,1,0:T(8,128)(2,1)}, f32[16,16,256]{2,1,0:T(8,128)}) custom-call(s32[128]{0:T(128)S(1)} %get-tuple-element.34.items, bf16[2,80,16,128]{3,2,1,0:T(8,128)(2,1)S(1)} %copy-done.8, bf16[2,80,16,128]{3,2,1,0:T(8,128)(2,1)S(1)} %collective-permute-done.4.got_a, bf16[80,16,128]{2,1,0:T(8,128)(2,1)S(1)} %collective-permute-done.5.last_a, ...), custom_call_target="tpu_custom_call" | custom-call | tf_op jit(solution)/shard_map/fill_slots/pallas_call | solution.py:228
  68.2 11.0 %all-to-all-start.1 = ((bf16[128,16,256]{2,1,0:T(8,128)(2,1)}), bf16[128,16,256]{2,1,0:T(8,128)(2,1)S(1)}, u32[]{:S(2)}, u32[]{:S(2)}) async-start(bf16[128,16,256]{2,1,0:T(8,128)(2,1)} %get-tuple-element.29), calls=%async_computation.1 | async-start | bytes 2097152 | tf_op jit(solution)/shard_map/all_to_all | solution.py:386
  79.1 3.0 %place_items.1 = bf16[128,64,256]{2,1,0:T(8,128)(2,1)} custom-call(s32[128]{0:T(128)S(1)} %get-tuple-element.33.items, bf16[64,64,256]{2,1,0:T(8,128)(2,1)S(1)} %copy-done.7), custom_call_target="tpu_custom_call" | custom-call | tf_op jit(solution)/shard_map/place_items/pallas_call | solution.py:146
  82.1 13.3 %all-to-all-done.1.received = bf16[128,16,256]{2,1,0:T(8,128)(2,1)S(1)} async-done(((bf16[128,16,256]{2,1,0:T(8,128)(2,1)}), bf16[128,16,256]{2,1,0:T(8,128)(2,1)S(1)}, u32[]{:S(2)}, u32[]{:S(2)}) %all-to-all-start.1) | async-done | bytes 1048608 | tf_op jit(solution)/shard_map/all_to_all | solution.py:386
  95.5 5.5 %all-to-all-start.2 = ((bf16[128,64,256]{2,1,0:T(8,128)(2,1)}), bf16[128,64,256]{2,1,0:T(8,128)(2,1)}, u32[]{:S(2)}, u32[]{:S(2)}) async-start(bf16[128,64,256]{2,1,0:T(8,128)(2,1)} %place_items.1), calls=%async_computation.2 | async-start | bytes 8388608 | tf_op jit(solution)/shard_map/all_to_all | solution.py:363
  101.1 1.1 collective-permute-start.2
  102.2 29.1 %collective-permute-done.got_a = bf16[2,80,32,128]{3,2,1,0:T(8,128)(2,1)S(1)} collective-permute-done((bf16[2,80,32,128]{3,2,1,0:T(8,128)(2,1)}, bf16[2,80,32,128]{3,2,1,0:T(8,128)(2,1)S(1)}, u32[]{:S(2)}, u32[]{:S(2)}) %collective-permute-start) | collective-permute-done | bytes 1310752 | tf_op jit(solution)/shard_map/ppermute | solution.py:375
  131.3 1.2 fusion
  133.6 1.2 fusion.1
  134.9 14.3 %collective-permute-done.1.last_a = bf16[80,32,128]{2,1,0:T(8,128)(2,1)S(1)} collective-permute-done((bf16[80,32,128]{2,1,0:T(8,128)(2,1)}, bf16[80,32,128]{2,1,0:T(8,128)(2,1)S(1)}, u32[]{:S(2)}, u32[]{:S(2)}) %collective-permute-start.1) | collective-permute-done | bytes 655392 | tf_op jit(solution)/shard_map/ppermute | solution.py:381
  150.0 1.3 copy-done.2
  151.3 1.3 copy-done.4
  152.6 1.3 copy-done.6
  153.9 4.3 %fill_slots.2 = (bf16[128,32,256]{2,1,0:T(8,128)(2,1)}, f32[16,32,256]{2,1,0:T(8,128)}) custom-call(s32[128]{0:T(128)S(1)} %get-tuple-element.34.items, bf16[2,80,32,128]{3,2,1,0:T(8,128)(2,1)S(1)} %copy-done, bf16[2,80,32,128]{3,2,1,0:T(8,128)(2,1)S(1)} %copy-done.4, bf16[80,32,128]{2,1,0:T(8,128)(2,1)S(1)} %collective-permute-done.1.last_a, ...), custom_call_target="tpu_custom_call" | custom-call | tf_op jit(solution)/shard_map/fill_slots/pallas_call | solution.py:228
  158.3 9.5 %all-to-all-start = ((bf16[128,32,256]{2,1,0:T(8,128)(2,1)}), bf16[128,32,256]{2,1,0:T(8,128)(2,1)S(1)}, u32[]{:S(2)}, u32[]{:S(2)}) async-start(bf16[128,32,256]{2,1,0:T(8,128)(2,1)} %get-tuple-element.23), calls=%async_computation | async-start | bytes 4194304 | tf_op jit(solution)/shard_map/all_to_all | solution.py:386
  169.2 1.0 copy-done.11
  170.2 4.7 %merge_early.1 = bf16[4,16,16,256]{3,2,1,0:T(8,128)(2,1)} custom-call(s32[128]{0:T(128)S(1)} %add.101.places, bf16[128,64,256]{2,1,0:T(8,128)(2,1)} %all-to-all-done.2.received, bf16[16,64,256]{2,1,0:T(8,128)(2,1)S(1)} %copy-done.11), custom_call_target="tpu_custom_call" | custom-call | tf_op jit(solution)/shard_map/merge_early/pallas_call | solution.py:175
  174.9 20.0 %reduce-scatter.2.cloned.1.call-done = bf16[1,16,16,256]{3,2,1,0:T(8,128)(2,1)} async-done(((bf16[4,16,16,256]{3,2,1,0:T(8,128)(2,1)}), bf16[1,16,16,256]{3,2,1,0:T(8,128)(2,1)}) %reduce-scatter.2.cloned.1.call-update) | async-done | bytes 131088 | tf_op jit(solution)/shard_map/reduce_scatter | solution.py:367
  194.9 1.6 place_early.1.so_far
  196.5 1.9 add_received.2.so_far
  199.5 2.1 %add_received.3 = f32[16,64,256]{2,1,0:T(8,128)} custom-call(s32[128]{0:T(128)S(1)} %add.101.places, bf16[128,32,256]{2,1,0:T(8,128)(2,1)S(1)} %all-to-all-done.received, f32[16,32,256]{2,1,0:T(8,128)S(1)} %copy-done.10, f32[16,64,256]{2,1,0:T(8,128)} %add_received.2.so_far), custom_call_target="tpu_custom_call", output_to_operand_aliasing={{}: (3, {})} | custom-call | tf_op jit(solution)/shard_map/add_received/pallas_call | solution.py:265
  (58 shorter events, 6.8 us)
Async XLA Ops:
  8.1 2.5 %copy-start.13 = (bf16[10,4,256,256]{3,2,1,0:T(8,128)(2,1)S(1)}, bf16[10,4,256,256]{3,2,1,0:T(8,128)(2,1)}, u32[]{:S(2)}) copy-start(bf16[10,4,256,256]{3,2,1,0:T(8,128)(2,1)} %left_hbm.1) | copy-start | bytes 15728644
  10.6 2.5 %copy-start.14 = (bf16[10,4,256,256]{3,2,1,0:T(8,128)(2,1)S(1)}, bf16[10,4,256,256]{3,2,1,0:T(8,128)(2,1)}, u32[]{:S(2)}) copy-start(bf16[10,4,256,256]{3,2,1,0:T(8,128)(2,1)} %right_hbm.1) | copy-start | bytes 15728644
  13.1 1.6 copy-start.15
  14.7 27.1 %copy-start.16 = (s32[512,4]{0,1:T(4,128)S(1)}, s32[512,4]{0,1:T(4,128)}, u32[]{:S(2)}) copy-start(s32[512,4]{0,1:T(4,128)} %param.13) | copy-start | bytes 24580
  37.9 20.4 %copy-start.9 = (bf16[2,80,16,128]{3,2,1,0:T(8,128)(2,1)S(1)}, bf16[2,80,16,128]{3,2,1,0:T(8,128)(2,1)}, u32[]{:S(2)}) copy-start(bf16[2,80,16,128]{3,2,1,0:T(8,128)(2,1)} %get-tuple-element.27.keep_b) | copy-start | bytes 1966084
  37.9 27.9 %copy-start.8 = (bf16[2,80,16,128]{3,2,1,0:T(8,128)(2,1)S(1)}, bf16[2,80,16,128]{3,2,1,0:T(8,128)(2,1)}, u32[]{:S(2)}) copy-start(bf16[2,80,16,128]{3,2,1,0:T(8,128)(2,1)} %get-tuple-element.25.keep_a) | copy-start | bytes 1966084
  37.9 16.3 %collective-permute-start.4 = (bf16[2,80,16,128]{3,2,1,0:T(8,128)(2,1)}, bf16[2,80,16,128]{3,2,1,0:T(8,128)(2,1)S(1)}, u32[]{:S(2)}, u32[]{:S(2)}) collective-permute-start(bf16[2,80,16,128]{3,2,1,0:T(8,128)(2,1)} %get-tuple-element.26), channel_id=1, source_target_pairs={{0,1},{1,0},{2,3},{3,2},{4,5},{5,4},{6,7},{7,6},{8,9},{9,8},{10,11... | collective-permute-start | bytes 1966088 | tf_op jit(solution)/shard_map/ppermute | solution.py:375
  40.0 18.2 %collective-permute-start.6 = (bf16[2,80,16,128]{3,2,1,0:T(8,128)(2,1)}, bf16[2,80,16,128]{3,2,1,0:T(8,128)(2,1)S(1)}, u32[]{:S(2)}, u32[]{:S(2)}) collective-permute-start(bf16[2,80,16,128]{3,2,1,0:T(8,128)(2,1)} %get-tuple-element.28), channel_id=1, source_target_pairs={{0,3},{1,2},{2,1},{3,0},{4,7},{5,6},{6,5},{7,4},{8,11},{9,10},{10,... | collective-permute-start | bytes 1966088 | tf_op jit(solution)/shard_map/ppermute | solution.py:376
  55.2 9.3 %collective-permute-start.5 = (bf16[80,16,128]{2,1,0:T(8,128)(2,1)S(1)}, bf16[80,16,128]{2,1,0:T(8,128)(2,1)S(1)}, u32[]{:S(2)}, u32[]{:S(2)}) collective-permute-start(bf16[80,16,128]{2,1,0:T(8,128)(2,1)S(1)} %fusion.2), channel_id=1, source_target_pairs={{0,3},{1,2},{2,1},{3,0},{4,7},{5,6},{6,5},{7,4},{8,11},{9,10},{10,... | collective-permute-start | bytes 983048 | tf_op jit(solution)/shard_map/ppermute | solution.py:381
  58.3 7.5 %collective-permute-start.7 = (bf16[80,16,128]{2,1,0:T(8,128)(2,1)S(1)}, bf16[80,16,128]{2,1,0:T(8,128)(2,1)S(1)}, u32[]{:S(2)}, u32[]{:S(2)}) collective-permute-start(bf16[80,16,128]{2,1,0:T(8,128)(2,1)S(1)} %fusion.3), channel_id=1, source_target_pairs={{0,1},{1,0},{2,3},{3,2},{4,5},{5,4},{6,7},{7,6},{8,9},{9,8},{10,11... | collective-permute-start | bytes 983048 | tf_op jit(solution)/shard_map/ppermute | solution.py:382
  68.2 11.0 %copy-start.7 = (bf16[64,64,256]{2,1,0:T(8,128)(2,1)S(1)}, bf16[64,64,256]{2,1,0:T(8,128)(2,1)}, u32[]{:S(2)}) copy-start(bf16[64,64,256]{2,1,0:T(8,128)(2,1)} %get-tuple-element.31.moved) | copy-start | bytes 6291460
  68.2 27.3 %all-to-all-start.1 = ((bf16[128,16,256]{2,1,0:T(8,128)(2,1)}), bf16[128,16,256]{2,1,0:T(8,128)(2,1)S(1)}, u32[]{:S(2)}, u32[]{:S(2)}) async-start(bf16[128,16,256]{2,1,0:T(8,128)(2,1)} %get-tuple-element.29), calls=%async_computation.1 | async-start | bytes 2097152 | tf_op jit(solution)/shard_map/all_to_all | solution.py:386
  82.1 49.2 %copy-start = (bf16[2,80,32,128]{3,2,1,0:T(8,128)(2,1)S(1)}, bf16[2,80,32,128]{3,2,1,0:T(8,128)(2,1)}, u32[]{:S(2)}) copy-start(bf16[2,80,32,128]{3,2,1,0:T(8,128)(2,1)} %get-tuple-element.19.keep_a) | copy-start | bytes 3932164
  95.5 62.8 %all-to-all-start.2 = ((bf16[128,64,256]{2,1,0:T(8,128)(2,1)}), bf16[128,64,256]{2,1,0:T(8,128)(2,1)}, u32[]{:S(2)}, u32[]{:S(2)}) async-start(bf16[128,64,256]{2,1,0:T(8,128)(2,1)} %place_items.1), calls=%async_computation.2 | async-start | bytes 8388608 | tf_op jit(solution)/shard_map/all_to_all | solution.py:363
  101.0 32.7 %copy-start.1 = (bf16[2,80,32,128]{3,2,1,0:T(8,128)(2,1)S(1)}, bf16[2,80,32,128]{3,2,1,0:T(8,128)(2,1)}, u32[]{:S(2)}) copy-start(bf16[2,80,32,128]{3,2,1,0:T(8,128)(2,1)} %get-tuple-element.21.keep_b) | copy-start | bytes 3932164
  101.0 30.3 %collective-permute-start = (bf16[2,80,32,128]{3,2,1,0:T(8,128)(2,1)}, bf16[2,80,32,128]{3,2,1,0:T(8,128)(2,1)S(1)}, u32[]{:S(2)}, u32[]{:S(2)}) collective-permute-start(bf16[2,80,32,128]{3,2,1,0:T(8,128)(2,1)} %get-tuple-element.20), channel_id=1, source_target_pairs={{0,1},{1,0},{2,3},{3,2},{4,5},{5,4},{6,7},{7,6},{8,9},{9,8},{10,11... | collective-permute-start | bytes 3932168 | tf_op jit(solution)/shard_map/ppermute | solution.py:375
  101.1 32.5 %collective-permute-start.2 = (bf16[2,80,32,128]{3,2,1,0:T(8,128)(2,1)}, bf16[2,80,32,128]{3,2,1,0:T(8,128)(2,1)S(1)}, u32[]{:S(2)}, u32[]{:S(2)}) collective-permute-start(bf16[2,80,32,128]{3,2,1,0:T(8,128)(2,1)} %get-tuple-element.22), channel_id=1, source_target_pairs={{0,3},{1,2},{2,1},{3,0},{4,7},{5,6},{6,5},{7,4},{8,11},{9,10},{10,... | collective-permute-start | bytes 3932168 | tf_op jit(solution)/shard_map/ppermute | solution.py:376
  131.3 3.5 %copy-start.3 = (bf16[2,80,32,128]{3,2,1,0:T(8,128)(2,1)}, bf16[2,80,32,128]{3,2,1,0:T(8,128)(2,1)S(1)}, u32[]{:S(2)}) copy-start(bf16[2,80,32,128]{3,2,1,0:T(8,128)(2,1)S(1)} %collective-permute-done.got_a) | copy-start | bytes 3932164
  132.6 16.6 %collective-permute-start.1 = (bf16[80,32,128]{2,1,0:T(8,128)(2,1)}, bf16[80,32,128]{2,1,0:T(8,128)(2,1)S(1)}, u32[]{:S(2)}, u32[]{:S(2)}) collective-permute-start(bf16[80,32,128]{2,1,0:T(8,128)(2,1)} %fusion), channel_id=1, source_target_pairs={{0,3},{1,2},{2,1},{3,0},{4,7},{5,6},{6,5},{7,4},{8,11},{9,10},{10,... | collective-permute-start | bytes 1966088 | tf_op jit(solution)/shard_map/ppermute | solution.py:381
  133.6 1.3 copy-start.5
  134.9 15.1 %collective-permute-start.3 = (bf16[80,32,128]{2,1,0:T(8,128)(2,1)}, bf16[80,32,128]{2,1,0:T(8,128)(2,1)}, u32[]{:S(2)}, u32[]{:S(2)}) collective-permute-start(bf16[80,32,128]{2,1,0:T(8,128)(2,1)} %fusion.1), channel_id=1, source_target_pairs={{0,1},{1,0},{2,3},{3,2},{4,5},{5,4},{6,7},{7,6},{8,9},{9,8},{10,11... | collective-permute-start | bytes 1966088 | tf_op jit(solution)/shard_map/ppermute | solution.py:382
  150.0 1.3 copy-start.2
  151.3 1.3 copy-start.4
  152.6 1.3 copy-start.6
  158.3 40.1 %all-to-all-start = ((bf16[128,32,256]{2,1,0:T(8,128)(2,1)}), bf16[128,32,256]{2,1,0:T(8,128)(2,1)S(1)}, u32[]{:S(2)}, u32[]{:S(2)}) async-start(bf16[128,32,256]{2,1,0:T(8,128)(2,1)} %get-tuple-element.23), calls=%async_computation | async-start | bytes 4194304 | tf_op jit(solution)/shard_map/all_to_all | solution.py:386
  167.8 27.1 %reduce-scatter.2.cloned.1.call-start = ((), (), s32[]{:S(2)}) async-start(), calls=%async_computation.4 | async-start | bytes 655360 | tf_op jit(solution)/shard_map/reduce_scatter | solution.py:367
  169.2 1.0 copy-start.11
  174.9 21.6 %copy-start.12 = (f32[16,16,256]{2,1,0:T(8,128)S(1)}, f32[16,16,256]{2,1,0:T(8,128)}, u32[]{:S(2)}) copy-start(f32[16,16,256]{2,1,0:T(8,128)} %get-tuple-element.30.own) | copy-start | bytes 786436
  198.4 1.0 copy-start.10
Sparse Core Ops, SparseCore 0:
  175.0 19.7 reduce-scatter.1

commit v3 on v1

v3 whole, which is shorter than its diff:
```python
import functools

import jax
import jax.numpy as jnp
from jax import lax
from jax.experimental import pallas as pl
from jax.experimental.pallas import tpu as pltpu
from jax.sharding import PartitionSpec as P

LANES = 128
EARLY_ROWS = 16
CHUNKS = (16, 32)
BF16 = jnp.bfloat16
F32 = jnp.float32


def small_cost():
    return pl.CostEstimate(flops=1, bytes_accessed=1, transcendentals=0)


def large_cost():
    return pl.CostEstimate(flops=6 * 10**10, bytes_accessed=1, transcendentals=0)


def whole(shape):
    return pl.BlockSpec(shape, lambda i, *_: (0,) * len(shape))


def relative_quarters(x):
    return x, x ^ 1, 3 - x, (3 - x) ^ 1


def products_kernel(
    capacity, device, block_left, block_right, channel_class, own_targets, psi_ref, left_hbm,
    right_hbm, *rest
):
    *outs, left_ref, right_ref, half_ref, acc_ref, stage_ref = rest[:-8]
    seen_ref, first_ref, slot_ref, left_here, right_here, left_sems, right_sems, slot_sems = rest[-8:]
    own, slots_hbm, *chunk_outs = outs
    channels, left_count, _, _ = left_ref.shape
    right_count = right_ref.shape[1]
    classes = acc_ref.shape[0]
    hops = classes - 1
    quarter = acc_ref.shape[1] // 4
    step = pl.program_id(0)
    x = device[0]
    left_id = block_left[step] - device[1] * left_count
    right_id = block_right[step] - device[2] * right_count

    def left_copy(i):
        return pltpu.make_async_copy(left_hbm.at[:, i], left_ref.at[:, i], left_sems.at[i])

    def right_copy(i):
        return pltpu.make_async_copy(right_hbm.at[:, i], right_ref.at[:, i], right_sems.at[i])

    def slot_copy(k, h):
        side = lax.rem(k, 2)
        return pltpu.make_async_copy(
            stage_ref.at[side, h], slots_hbm.at[slot_ref[k * hops + h]], slot_sems.at[side, h]
        )

    def need(copy, here, i):
        @pl.when(here[i] == 0)
        def _():
            copy(i).wait()
            here[i] = 1

    @pl.when(step == 0)
    def _():
        for i in range(left_count):
            left_here[i] = 0
        for i in range(right_count):
            right_here[i] = 0
        for turn in range(max(left_count, right_count)):
            if turn < left_count:
                left_copy(lax.rem(left_id + turn, left_count)).start()
            if turn < right_count:
                right_copy(lax.rem(right_id + turn, right_count)).start()
        acc_ref[...] = jnp.zeros_like(acc_ref)
        blocks = pl.num_programs(0)
        for i in range(seen_ref.shape[0]):
            seen_ref[i] = 0

        def place(i, _):
            owner = lax.div(own_targets[i], blocks)
            earlier = seen_ref[owner]
            slot_ref[i] = owner * capacity + earlier
            seen_ref[owner] = earlier + 1
            return 0

        lax.fori_loop(0, slot_ref.shape[0], place, 0)
        for w in range(channels):
            before = [channel_class[x * channels + v] for v in range(w)]
            same = [jnp.int32(b == channel_class[x * channels + w]) for b in before]
            first_ref[w] = jnp.int32(sum(same, jnp.int32(0)) == 0)

    @pl.when(step >= 2)
    def _():
        for h in range(hops):
            slot_copy(step - 2, h).wait()

    need(left_copy, left_here, left_id)
    need(right_copy, right_here, right_id)

    for w in range(channels):
        half_ref[w] = jnp.dot(
            left_ref[w, left_id], psi_ref[0], preferred_element_type=F32
        ).astype(BF16)
    for w in range(channels):
        full = jnp.dot(half_ref[w], right_ref[w, right_id], preferred_element_type=F32)
        member = channel_class[x * channels + w]
        before = acc_ref[member]
        acc_ref[member] = jnp.where(first_ref[w] != 0, 0.0, before) + full

    side = lax.rem(step, 2)
    for q in range(4):
        rows = slice(q * EARLY_ROWS, (q + 1) * EARLY_ROWS)
        at = q * quarter
        for h in range(hops):
            stage_ref[side, h, rows] = acc_ref[h + 1, at : at + EARLY_ROWS].astype(BF16)
    for place, q in enumerate(relative_quarters(x)):
        at = pl.multiple_of(q * quarter, quarter)
        own[place, 0] = acc_ref[0, pl.ds(at, quarter)].astype(BF16)
    here, beside, mirror, across = relative_quarters(x)
    orders = ((here, mirror, beside, across), (here, beside, mirror, across))
    start = EARLY_ROWS
    for j, rows in enumerate(CHUNKS):
        for s in range(2):
            keep, send = chunk_outs[4 * j + 2 * s : 4 * j + 2 * s + 2]
            for place, q in enumerate(orders[s]):
                target = keep if place < 2 else send
                at = pl.multiple_of(q * quarter + start, 16)
                for h in range(hops):
                    target[place % 2, h] = acc_ref[
                        h + 1, pl.ds(at, rows), s * LANES : (s + 1) * LANES
                    ].astype(BF16)
        start += rows
    for h in range(hops):
        slot_copy(step, h).start()

    @pl.when(step == pl.num_programs(0) - 1)
    def _():
        for h in range(hops):
            slot_copy(step - 1, h).wait()
        for h in range(hops):
            slot_copy(step, h).wait()
        for i in range(left_count):
            need(left_copy, left_here, i)
        for i in range(right_count):
            need(right_copy, right_here, i)


def products(tables, owners, capacity, psi, left_env, right_env, classes):
    blocks, block, _ = psi.shape
    channels, left_count = left_env.shape[:2]
    right_count = right_env.shape[1]
    quarter = block // 4
    early = 4 * EARLY_ROWS
    hops = classes - 1
    out_shape = [
        pltpu.HBM((4, blocks, quarter, block), BF16),
        pltpu.HBM((owners * capacity, early, block), BF16),
    ]
    out_specs = [
        pl.BlockSpec((4, 1, quarter, block), lambda k, *_: (0, k, 0, 0)),
        pl.BlockSpec(memory_space=pltpu.HBM),
    ]
    for rows in CHUNKS:
        out_shape += [pltpu.HBM((2, blocks * hops, rows, LANES), BF16)] * 4
        out_specs += [pl.BlockSpec((2, hops, rows, LANES), lambda k, *_: (0, k, 0, 0))] * 4
    return pl.pallas_call(
        functools.partial(products_kernel, capacity),
        out_shape=out_shape,
        grid_spec=pltpu.PrefetchScalarGridSpec(
            num_scalar_prefetch=len(tables),
            grid=(blocks,),
            in_specs=[
                pl.BlockSpec((1, block, block), lambda k, *_: (k, 0, 0)),
                pl.BlockSpec(memory_space=pltpu.HBM),
                pl.BlockSpec(memory_space=pltpu.HBM),
            ],
            out_specs=out_specs,
            scratch_shapes=[
                pltpu.VMEM(left_env.shape, BF16),
                pltpu.VMEM(right_env.shape, BF16),
                pltpu.VMEM((channels, block, block), BF16),
                pltpu.VMEM((classes, block, block), F32),
                pltpu.VMEM((2, hops, early, block), BF16),
                pltpu.SMEM((owners,), jnp.int32),
                pltpu.SMEM((channels,), jnp.int32),
                pltpu.SMEM((blocks * hops,), jnp.int32),
                pltpu.SMEM((left_count,), jnp.int32),
                pltpu.SMEM((right_count,), jnp.int32),
                pltpu.SemaphoreType.DMA((left_count,)),
                pltpu.SemaphoreType.DMA((right_count,)),
                pltpu.SemaphoreType.DMA((2, hops)),
            ],
        ),
        compiler_params=pltpu.CompilerParams(vmem_limit_bytes=60 * 2**20),
        cost_estimate=pl.CostEstimate(
            flops=4 * channels * blocks * block**3,
            bytes_accessed=2 * (left_env.size + right_env.size + psi.size * (1 + classes)),
            transcendentals=0,
        ),
        name="products",
    )(*tables, psi, left_env, right_env)


def slots_kernel(items, keep_a, got_a, last_a, keep_b, got_b, last_b, slots):
    def total(keep, got, last, i):
        value = keep[0, i].astype(F32) + got[0, i].astype(F32) + last[i].astype(F32)
        return value.astype(BF16)

    def fill(p, _):
        i = items[p]
        slots[p, :, :LANES] = total(keep_a, got_a, last_a, i)
        slots[p, :, LANES:] = total(keep_b, got_b, last_b, i)
        return 0

    lax.fori_loop(0, slots.shape[0], fill, 0, unroll=4)


def fill_slots(items, parts, final):
    _, count, rows, _ = parts[0].shape
    slot_count = items.shape[0]
    pair = whole((1, count, rows, LANES))
    one = whole((count, rows, LANES))
    return pl.pallas_call(
        slots_kernel,
        out_shape=pltpu.HBM((slot_count, rows, 2 * LANES), BF16),
        grid_spec=pltpu.PrefetchScalarGridSpec(
            num_scalar_prefetch=1,
            grid=(1,),
            in_specs=[pair, pair, one, pair, pair, one],
            out_specs=whole((slot_count, rows, 2 * LANES)),
        ),
        compiler_params=pltpu.CompilerParams(vmem_limit_bytes=60 * 2**20),
        cost_estimate=large_cost() if final else small_cost(),
        name="fill_slots",
    )(items, *parts)


def merge_kernel(device, places, received, own, *rest):
    *outs, acc = rest
    _, blocks, quarter, _ = own.shape
    at = [pl.multiple_of(q * EARLY_ROWS, EARLY_ROWS) for q in relative_quarters(device[0])]
    for p in range(4):
        acc[:blocks, pl.ds(at[p], EARLY_ROWS)] = own[p, :, :EARLY_ROWS].astype(F32)

    def add(p, _):
        acc[places[p]] += received[p].astype(F32)
        return 0

    lax.fori_loop(0, received.shape[0], add, 0, unroll=4)
    for p in range(4):
        outs[p][:, :EARLY_ROWS] = acc[:blocks, pl.ds(at[p], EARLY_ROWS)].astype(BF16)
        outs[p][:, EARLY_ROWS:] = own[p, :, EARLY_ROWS:]


def merge_early(device, places, received, own):
    _, blocks, quarter, width = own.shape
    return pl.pallas_call(
        merge_kernel,
        out_shape=[pltpu.HBM((blocks, quarter, width), BF16)] * 4,
        grid_spec=pltpu.PrefetchScalarGridSpec(
            num_scalar_prefetch=2,
            grid=(1,),
            in_specs=[whole(received.shape), whole(own.shape)],
            out_specs=[whole((blocks, quarter, width))] * 4,
            scratch_shapes=[pltpu.VMEM((blocks + 1, 4 * EARLY_ROWS, width), F32)],
        ),
        compiler_params=pltpu.CompilerParams(vmem_limit_bytes=60 * 2**20),
        cost_estimate=small_cost(),
        name="merge_early",
    )(device, places, received, own)


def add_slots(acc, places, received):
    def add(p, _):
        acc[places[p]] += received[p].astype(F32)
        return 0

    lax.fori_loop(0, received.shape[0], add, 0, unroll=4)


def first_sum(places, received, mine, others, start):
    blocks, quarter, width = mine.shape
    rows = received.shape[1]

    def kernel(places, received, *rest):
        *parts, result, acc = rest

        def total(at):
            value = parts[0][:, at].astype(F32)
            for part in parts[1:]:
                value = value + part[:, at].astype(F32)
            return value

        acc[:blocks] = total(slice(start, start + rows))
        add_slots(acc, places, received)
        result[:, :start] = total(slice(0, start))
        result[:, start : start + rows] = acc[:blocks]
        result[:, start + rows :] = total(slice(start + rows, quarter))

    return pl.pallas_call(
        kernel,
        out_shape=pltpu.HBM(mine.shape, F32),
        grid_spec=pltpu.PrefetchScalarGridSpec(
            num_scalar_prefetch=1,
            grid=(1,),
            in_specs=[whole(received.shape)] + [whole(mine.shape)] * (1 + len(others)),
            out_specs=whole(mine.shape),
            scratch_shapes=[pltpu.VMEM((blocks + 1, rows, width), F32)],
        ),
        compiler_params=pltpu.CompilerParams(vmem_limit_bytes=60 * 2**20),
        cost_estimate=large_cost(),
        name="first_sum",
    )(places, received, mine, *others)


def last_sum(places, received, so_far, start):
    blocks, _, width = so_far.shape
    rows = received.shape[1]
    part = pl.BlockSpec((blocks, rows, width), lambda i, *_: (0, start // rows, 0))

    def kernel(places, received, so_far, result, acc):
        acc[:blocks] = so_far[...]
        add_slots(acc, places, received)
        result[...] = acc[:blocks]

    return pl.pallas_call(
        kernel,
        out_shape=pltpu.HBM(so_far.shape, F32),
        grid_spec=pltpu.PrefetchScalarGridSpec(
            num_scalar_prefetch=1,
            grid=(1,),
            in_specs=[whole(received.shape), part],
            out_specs=part,
            scratch_shapes=[pltpu.VMEM((blocks + 1, rows, width), F32)],
        ),
        input_output_aliases={2: 0},
        compiler_params=pltpu.CompilerParams(vmem_limit_bytes=60 * 2**20),
        cost_estimate=small_cost(),
        name="last_sum",
    )(places, received, so_far)


def item_places(targets, block_count):
    destined = targets // block_count
    count = targets.shape[-1]
    earlier = jnp.arange(count)[:, None] > jnp.arange(count)[None, :]
    same = (destined[..., :, None] == destined[..., None, :]) & earlier
    return destined, jnp.sum(same.astype(jnp.int32), axis=-1)


def shards(wavefunction, left_env, right_env, block_left, block_right, channel_class, hop_target):
    block_count = wavefunction.shape[0]
    hop_count = hop_target.shape[1]
    owners = lax.axis_size("lsec") * lax.axis_size("rsec")
    item_count = block_count * hop_count
    capacity = 2 * ((item_count + owners - 1) // owners)
    slot_count = owners * capacity
    me = lax.axis_index("lsec") * lax.axis_size("rsec") + lax.axis_index("rsec")
    device = jnp.stack([lax.axis_index(axis) for axis in ("mpo", "lsec", "rsec")]).astype(jnp.int32)
    targets = hop_target.reshape(owners, item_count)
    own_targets = lax.dynamic_index_in_dim(targets, me, 0, False)
    own, early_slots, *parts = products(
        (device, block_left, block_right, channel_class, own_targets),
        owners,
        capacity,
        wavefunction,
        left_env,
        right_env,
        hop_count + 1,
    )

    destined, slot = item_places(own_targets, block_count)
    position = destined * capacity + slot
    held = position[:, None] == jnp.arange(slot_count, dtype=jnp.int32)[None, :]
    index = jnp.arange(item_count, dtype=jnp.int32)
    slot_items = jnp.sum(jnp.where(held, index[:, None], 0), axis=0)
    destined_all, slot_all = item_places(targets, block_count)
    mine = (destined_all == me)[:, :, None] & (
        slot_all[:, :, None] == jnp.arange(capacity, dtype=jnp.int32)
    )
    local = targets - (me + 1) * block_count
    places = jnp.sum(jnp.where(mine, local[:, :, None], 0), axis=1).reshape(slot_count)
    places = places + block_count

    beside = [(i, i ^ 1) for i in range(4)]
    mirror = [(i, 3 - i) for i in range(4)]
    across = [(i, (i + 2) % 4) for i in range(4)]

    def second(keep, got):
        return (keep[1].astype(F32) + got[1].astype(F32)).astype(BF16)

    early = lax.all_to_all(early_slots, ("lsec", "rsec"), 0, 0, tiled=True)
    got, last = [], []
    for j in range(len(CHUNKS)):
        keep_a, send_a, keep_b, send_b = parts[4 * j : 4 * j + 4]
        got.append((lax.ppermute(send_a, "mpo", beside), lax.ppermute(send_b, "mpo", mirror)))
    for j in range(len(CHUNKS)):
        keep_a, _, keep_b, _ = parts[4 * j : 4 * j + 4]
        got_a, got_b = got[j]
        if j > 0:
            got_a, got_b, *last[j - 1] = lax.optimization_barrier((got_a, got_b, *last[j - 1]))
        then_a, then_b = lax.optimization_barrier((second(keep_a, got_a), second(keep_b, got_b)))
        last.append([lax.ppermute(then_a, "mpo", mirror), lax.ppermute(then_b, "mpo", beside)])

    def send(j, last_a, last_b):
        keep_a, _, keep_b, _ = parts[4 * j : 4 * j + 4]
        group = (keep_a, got[j][0], last_a, keep_b, got[j][1], last_b)
        return fill_slots(slot_items, group, j + 1 == len(CHUNKS))

    last_a, last_b, early, then_a, then_b = lax.optimization_barrier(
        (*last[0], early, then_a, then_b)
    )
    slots = send(0, last_a, last_b)
    early, slots = lax.optimization_barrier((early, slots))
    received = lax.all_to_all(slots, ("lsec", "rsec"), 0, 0, tiled=True)
    out_mine, *out_others = merge_early(device, places, early, own)
    others = [
        lax.ppermute(part, "mpo", pairs)
        for part, pairs in zip(out_others, (beside, mirror, across))
    ]
    slots = send(1, *last[1])
    received_last = lax.all_to_all(slots, ("lsec", "rsec"), 0, 0, tiled=True)
    base = first_sum(places, received, out_mine, others, EARLY_ROWS)
    return last_sum(places, received_last, base, EARLY_ROWS + CHUNKS[0])


def solution(mesh):
    in_specs = (
        P(("lsec", "rsec"), None, None),
        P("mpo", "lsec", None, None),
        P("mpo", "rsec", None, None),
        P(("lsec", "rsec")),
        P(("lsec", "rsec")),
        P(),
        P(),
    )
    out_specs = P(("lsec", "rsec"), "mpo", None)
    return jax.shard_map(shards, mesh=mesh, in_specs=in_specs, out_specs=out_specs, check_vma=False)
```

time: 213 us -> 156 us (0.73)
  local copies, waits for them, and re-layouts: 43.4 us -> 5.48 us
  starting transfers between devices: 48.9 us -> 37.7 us
  other arithmetic: 12.7 us -> 4.84 us
  Pallas kernels: 41.3 us -> 46.9 us
  waiting for transfers between devices: 64.9 us -> 60.1 us
    all_to_all x4 -> x1, starting transfers between devices: 34.2 us -> 7.78 us  [shards(): received = lax.all_to_all(slots, ('lsec', 'rsec'), 0, 0, tiled=True)]
    all_to_all x0 -> x2, starting transfers between devices: none -> 18.4 us  [the longest x1 10.6 us: shards(): early = lax.all_to_all(early_slots, ('lsec', 'rsec'), 0, 0, tiled=True)]
    ppermute x16 -> x11, waiting for transfers between devices: 61.8 us -> 44.8 us  [the longest x2 25.2 us: shards(): lax.ppermute(then_a, 'mpo', mirror)]
    unnamed x53 -> x23, local copies, waits for them, and re-layouts: 20.6 us -> 4.55 us
    all_to_all x0 -> x2, waiting for transfers between devices: none -> 15.2 us  [the longest x1 13.6 us: shards(): received_last = lax.all_to_all(slots, ('lsec', 'rsec'), 0, 0, tiled=True)]
    pallas_call x8 -> x0, local copies, waits for them, and re-layouts: 12.2 us -> none  [products(): pl.pallas_call(functools.partial(products_kernel, chunks), out_shape=out_...]
    ppermute x8 -> x0, local copies, waits for them, and re-layouts: 9.61 us -> none  [the longest x4 4.8 us: shards(): got_a = lax.ppermute(send_a, 'mpo', beside)]
    convert_element_type x9 -> x3, other arithmetic: 10.4 us -> 1.77 us  [second(): return (keep[1].astype(F32) + got[1].astype(F32)).astype(BF16)]
  transfers between devices with their start and end apart: 20 -> 14, of which waited for: 8 -> 8; matrix products, arithmetic and copies ran while one was open for 16% -> 3% of each run, Pallas kernels for 7% -> 12%
where the time goes in v3:
time: 156 us; the launch traced here: 155 us
  waiting for transfers between devices  60.1 us (39%)
  Pallas kernels  46.9 us (30%)
  starting transfers between devices  37.7 us (24%)
  local copies, waits for them, and re-layouts  5.48 us (4%)
  other arithmetic  4.84 us (3%)
    ppermute x2, waiting for transfers between devices, shards(): lax.ppermute(then_a, 'mpo', mirror)  25.2 us
    pallas_call x1, Pallas kernels, products(): pl.pallas_call(functools.partial(products_kernel, capacity), out_shape=ou...  24.1 us
    all_to_all x1, waiting for transfers between devices, shards(): received_last = lax.all_to_all(slots, ('lsec', 'rsec'), 0, 0, tiled=True)  13.6 us
    all_to_all x1, starting transfers between devices, shards(): early = lax.all_to_all(early_slots, ('lsec', 'rsec'), 0, 0, tiled=True)  10.6 us
    ppermute x3, waiting for transfers between devices, shards(): lax.ppermute(part, 'mpo', pairs)  8.97 us
    ppermute x2, waiting for transfers between devices, shards(): lax.ppermute(send_a, 'mpo', beside)  8.59 us
    pallas_call x2, Pallas kernels, fill_slots(): pl.pallas_call(slots_kernel, out_shape=pltpu.HBM((slot_count, rows, 2 * L...  8.53 us
    all_to_all x1, starting transfers between devices, shards(): received = lax.all_to_all(slots, ('lsec', 'rsec'), 0, 0, tiled=True)  7.78 us
  transfers between devices with their start and end apart: 14, of which 8 were waited for; matrix products, arithmetic and copies ran while one was open for 3% of the time, Pallas kernels for 12%

profile of v3, /device:TPU:1, one launch (start us, length us, event | category | flops | bytes accessed | tf_op | source)
XLA Modules:
  0.0 155.2 jit_solution(9255801089244635881)
XLA Ops:
  0.0 0.8 copy.10
  2.2 24.1 %products.1 = (bf16[4,16,64,256]{3,2,1,0:T(8,128)(2,1)}, bf16[128,64,256]{2,1,0:T(8,128)(2,1)}, bf16[2,64,16,128]{3,2,1,0:T(8,128)(2,1)}, bf16[2,64,16,128]{3,2,...) custom-call(s32[3]{0:T(128)} %pad_add_fusion.device, ...), custom_call_target="tpu_custom_call" | custom-call | flops 10737418240 | bytes 23068672 | tf_op jit(solution)/shard_map/products/pallas_call | solution.py:171
  26.3 10.6 %all-to-all-start.1 = ((bf16[128,64,256]{2,1,0:T(8,128)(2,1)}), bf16[128,64,256]{2,1,0:T(8,128)(2,1)}, u32[]{:S(2)}, u32[]{:S(2)}) async-start(bf16[128,64,256]{2,1,0:T(8,128)(2,1)} %get-tuple-element.48), calls=%async_computation.1 | async-start | bytes 8388608 | tf_op jit(solution)/shard_map/all_to_all | solution.py:397
  36.9 1.3 collective-permute-start.2
  38.2 1.8 %collective-permute-start.3 = (bf16[2,64,16,128]{3,2,1,0:T(8,128)(2,1)}, bf16[2,64,16,128]{3,2,1,0:T(8,128)(2,1)S(1)}, u32[]{:S(2)}, u32[]{:S(2)}) collective-permute-start(bf16[2,64,16,128]{3,2,1,0:T(8,128)(2,1)} %get-tuple-element.38), channel_id=1, source_target_pairs={{0,3},{1,2},{2,1},{3,0},{4,7},{5,6},{6,5},{7,4},{8,11},{9,10},{10,... | collective-permute-start | bytes 1572872 | tf_op jit(solution)/shard_map/ppermute | solution.py:401
  40.4 0.6 collective-permute-start.1
  41.0 0.9 convert_reduce_fusion
  41.9 8.6 %collective-permute-done.2.got_a = bf16[2,64,16,128]{3,2,1,0:T(8,128)(2,1)S(1)} collective-permute-done((bf16[2,64,16,128]{3,2,1,0:T(8,128)(2,1)}, bf16[2,64,16,128]{3,2,1,0:T(8,128)(2,1)S(1)}, u32[]{:S(2)}, u32[]{:S(2)}) %collective-permute-start.2) | collective-permute-done | bytes 524320 | tf_op jit(solution)/shard_map/ppermute | solution.py:401
  50.6 2.0 %collective-permute-done.3.got_b = bf16[2,64,16,128]{3,2,1,0:T(8,128)(2,1)S(1)} collective-permute-done((bf16[2,64,16,128]{3,2,1,0:T(8,128)(2,1)}, bf16[2,64,16,128]{3,2,1,0:T(8,128)(2,1)S(1)}, u32[]{:S(2)}, u32[]{:S(2)}) %collective-permute-start.3) | collective-permute-done | bytes 524320 | tf_op jit(solution)/shard_map/ppermute | solution.py:401
  52.7 1.9 %collective-permute-start.4 = (bf16[64,16,128]{2,1,0:T(8,128)(2,1)S(1)}, bf16[64,16,128]{2,1,0:T(8,128)(2,1)S(1)}, u32[]{:S(2)}, u32[]{:S(2)}) collective-permute-start(bf16[64,16,128]{2,1,0:T(8,128)(2,1)S(1)} %fusion.2), channel_id=1, source_target_pairs={{0,3},{1,2},{2,1},{3,0},{4,7},{5,6},{6,5},{7,4},{8,11},{9,10},{10,... | collective-permute-start | bytes 786440 | tf_op jit(solution)/shard_map/ppermute | solution.py:408
  54.9 0.7 add.66.places
  55.6 25.2 %collective-permute-done.4.last_a = bf16[64,16,128]{2,1,0:T(8,128)(2,1)S(1)} collective-permute-done((bf16[64,16,128]{2,1,0:T(8,128)(2,1)S(1)}, bf16[64,16,128]{2,1,0:T(8,128)(2,1)S(1)}, u32[]{:S(2)}, u32[]{:S(2)}) %collective-permute-start.4) | collective-permute-done | bytes 262176 | tf_op jit(solution)/shard_map/ppermute | solution.py:408
  80.8 0.7 copy-done.7
  81.5 1.6 %fusion = (bf16[64,32,128]{2,1,0:T(8,128)(2,1)S(1)}, bf16[64,32,128]{2,1,0:T(8,128)(2,1)S(1)}) fusion(bf16[2,64,32,128]{3,2,1,0:T(8,128)(2,1)} %collective-permute-done.got_a, bf16[2,64,32,128]{3,2,1,0:T(8,128)(2,1)S(1)} %copy-done.6, bf16[2,64,32,128]{3,2,1,0:T(8,128)(2,1)} %collective-permute-done.1.got_b, bf16[2,64,32,128]{3,2,1,0:T(8,128)(2,1)} %get-tuple-element.42.keep_b), kind=kLoop, calls=%fused_computation.3 | loop fusion | flops 2097152 | bytes 3145728 | tf_op jit(solution)/shard_map/convert_element_type | solution.py:395
  83.2 1.9 %collective-permute-start.6 = (bf16[64,32,128]{2,1,0:T(8,128)(2,1)S(1)}, bf16[64,32,128]{2,1,0:T(8,128)(2,1)S(1)}, u32[]{:S(2)}, u32[]{:S(2)}) collective-permute-start(bf16[64,32,128]{2,1,0:T(8,128)(2,1)S(1)} %get-tuple-element.44), channel_id=1, source_target_pairs={{0,3},{1,2},{2,1},{3,0},{4,7},{5,6},{6,5},{7,4},{8,11},{9,10},{10,... | collective-permute-start | bytes 1572872 | tf_op jit(solution)/shard_map/ppermute | solution.py:408
  85.9 1.6 %all-to-all-done.1.received = bf16[128,64,256]{2,1,0:T(8,128)(2,1)} async-done(((bf16[128,64,256]{2,1,0:T(8,128)(2,1)}), bf16[128,64,256]{2,1,0:T(8,128)(2,1)}, u32[]{:S(2)}, u32[]{:S(2)}) %all-to-all-start.1) | async-done | bytes 4194336 | tf_op jit(solution)/shard_map/all_to_all | solution.py:397
  87.5 3.6 %fill_slots.3 = bf16[128,16,256]{2,1,0:T(8,128)(2,1)} custom-call(s32[128]{0:T(128)} %select_reduce_fusion.1.items, bf16[2,64,16,128]{3,2,1,0:T(8,128)(2,1)} %get-tuple-element.35.keep_a, bf16[2,64,16,128]{3,2,1,0:T(8,128)(2,1)} %copy-done.3, bf16[64,16,128]{2,1,0:T(8,128)(2,1)} %copy-done.7, bf16[2,64,16,128]{3,2,1,0:T(8,128)(2,1)} %get-tuple-element.37.keep_b, ...), custom_call_target="tpu_custom_call" | custom-call | flops 1 | bytes 1 | tf_op jit(solution)/shard_map/fill_slots/pallas_call | solution.py:228
  91.1 7.8 %all-to-all-start.2 = ((bf16[128,16,256]{2,1,0:T(8,128)(2,1)}), bf16[128,16,256]{2,1,0:T(8,128)(2,1)S(1)}, u32[]{:S(2)}, u32[]{:S(2)}) async-start(bf16[128,16,256]{2,1,0:T(8,128)(2,1)} %fill_slots.3), calls=%async_computation.2 | async-start | bytes 2097152 | tf_op jit(solution)/shard_map/all_to_all | solution.py:420
  98.9 6.0 %merge_early.1 = (bf16[16,64,256]{2,1,0:T(8,128)(2,1)}, bf16[16,64,256]{2,1,0:T(8,128)(2,1)}, bf16[16,64,256]{2,1,0:T(8,128)(2,1)}, bf16[16,64,256]{2,1,0:T(8,128)(2,1)}) custom-call(s32[3]{0:T(128)} %pad_add_fusion.device, s32[128]{0:T(128)} %add.66.places, bf16[128,64,256]{2,1,0:T(8,128)(2,1)} %all-to-all-done.1.received, ...), custom_call_target="tpu_custom_call" | custom-call | flops 1 | bytes 1 | tf_op jit(solution)/shard_map/merge_early/pallas_call | solution.py:262
  104.9 1.2 collective-permute-start.8
  106.2 1.8 %collective-permute-start.9 = (bf16[16,64,256]{2,1,0:T(8,128)(2,1)}, bf16[16,64,256]{2,1,0:T(8,128)(2,1)}, u32[]{:S(2)}, u32[]{:S(2)}) collective-permute-start(bf16[16,64,256]{2,1,0:T(8,128)(2,1)} %get-tuple-element.57), channel_id=1, source_target_pairs={{0,3},{1,2},{2,1},{3,0},{4,7},{5,6},{6,5},{7,4},{8,11},{9,10},{10,... | collective-permute-start | bytes 1572872 | tf_op jit(solution)/shard_map/ppermute | solution.py:423
  108.0 0.6 collective-permute-start.10
  108.6 0.8 copy-done.9
  109.4 0.8 copy-done.10
  110.2 4.9 %fill_slots.2 = bf16[128,32,256]{2,1,0:T(8,128)(2,1)} custom-call(s32[128]{0:T(128)} %select_reduce_fusion.1.items, bf16[2,64,32,128]{3,2,1,0:T(8,128)(2,1)} %get-tuple-element.32.keep_a, bf16[2,64,32,128]{3,2,1,0:T(8,128)(2,1)} %collective-permute-done.got_a, bf16[64,32,128]{2,1,0:T(8,128)(2,1)} %copy-done.9, ...), custom_call_target="tpu_custom_call" | custom-call | flops 60000002048 | bytes 1 | tf_op jit(solution)/shard_map/fill_slots/pallas_call | solution.py:228
  115.2 7.8 %all-to-all-start = ((bf16[128,32,256]{2,1,0:T(8,128)(2,1)}), bf16[128,32,256]{2,1,0:T(8,128)(2,1)S(1)}, u32[]{:S(2)}, u32[]{:S(2)}) async-start(bf16[128,32,256]{2,1,0:T(8,128)(2,1)} %fill_slots.2), calls=%async_computation | async-start | bytes 4194304 | tf_op jit(solution)/shard_map/all_to_all | solution.py:427
  123.0 7.1 %collective-permute-done.9.rest_2_ = bf16[16,64,256]{2,1,0:T(8,128)(2,1)} collective-permute-done((bf16[16,64,256]{2,1,0:T(8,128)(2,1)}, bf16[16,64,256]{2,1,0:T(8,128)(2,1)}, u32[]{:S(2)}, u32[]{:S(2)}) %collective-permute-start.9) | collective-permute-done | bytes 524320 | tf_op jit(solution)/shard_map/ppermute | solution.py:423
  130.1 1.9 %collective-permute-done.10.rest_3_ = bf16[16,64,256]{2,1,0:T(8,128)(2,1)} collective-permute-done((bf16[16,64,256]{2,1,0:T(8,128)(2,1)}, bf16[16,64,256]{2,1,0:T(8,128)(2,1)}, u32[]{:S(2)}, u32[]{:S(2)}) %collective-permute-start.10) | collective-permute-done | bytes 524320 | tf_op jit(solution)/shard_map/ppermute | solution.py:423
  132.0 4.4 %first_sum.1.so_far = f32[16,64,256]{2,1,0:T(8,128)} custom-call(s32[128]{0:T(128)} %add.66.places, bf16[128,16,256]{2,1,0:T(8,128)(2,1)} %copy-done.5, bf16[16,64,256]{2,1,0:T(8,128)(2,1)} %get-tuple-element.55.rest_0_, bf16[16,64,256]{2,1,0:T(8,128)(2,1)} %collective-permute-done.8.rest_1_, bf16[16,64,256]{2,1,0:T(8,128)(2,1)} %collective-permute-done.9.rest_2_, ...), custom_call_target="tpu_custom_call" | custom-call | flops 60000002048 | bytes 1 | tf_op jit(solution)/shard_map/first_sum/pallas_call | solution.py:305
  136.4 13.6 %all-to-all-done.received = bf16[128,32,256]{2,1,0:T(8,128)(2,1)S(1)} async-done(((bf16[128,32,256]{2,1,0:T(8,128)(2,1)}), bf16[128,32,256]{2,1,0:T(8,128)(2,1)S(1)}, u32[]{:S(2)}, u32[]{:S(2)}) %all-to-all-start) | async-done | bytes 2097184 | tf_op jit(solution)/shard_map/all_to_all | solution.py:427
  150.0 1.3 copy-done
  151.3 3.9 %last_sum.1 = f32[16,64,256]{2,1,0:T(8,128)} custom-call(s32[128]{0:T(128)} %add.66.places, bf16[128,32,256]{2,1,0:T(8,128)(2,1)} %copy-done, f32[16,64,256]{2,1,0:T(8,128)} %first_sum.1.so_far), custom_call_target="tpu_custom_call", output_to_operand_aliasing={{}: (2, {})} | custom-call | flops 1 | bytes 1 | tf_op jit(solution)/shard_map/last_sum/pallas_call | solution.py:331
  (43 shorter events, 3.1 us)
Async XLA Ops:
  26.3 24.3 %copy-start.1 = (bf16[2,64,16,128]{3,2,1,0:T(8,128)(2,1)S(1)}, bf16[2,64,16,128]{3,2,1,0:T(8,128)(2,1)}, u32[]{:S(2)}) copy-start(bf16[2,64,16,128]{3,2,1,0:T(8,128)(2,1)} %get-tuple-element.35.keep_a) | copy-start | bytes 1572868
  26.3 26.4 %copy-start.2 = (bf16[2,64,16,128]{3,2,1,0:T(8,128)(2,1)S(1)}, bf16[2,64,16,128]{3,2,1,0:T(8,128)(2,1)}, u32[]{:S(2)}) copy-start(bf16[2,64,16,128]{3,2,1,0:T(8,128)(2,1)} %get-tuple-element.37.keep_b) | copy-start | bytes 1572868
  26.3 55.3 %copy-start.6 = (bf16[2,64,32,128]{3,2,1,0:T(8,128)(2,1)S(1)}, bf16[2,64,32,128]{3,2,1,0:T(8,128)(2,1)}, u32[]{:S(2)}) copy-start(bf16[2,64,32,128]{3,2,1,0:T(8,128)(2,1)} %get-tuple-element.32.keep_a) | copy-start | bytes 3145732
  26.3 61.2 %all-to-all-start.1 = ((bf16[128,64,256]{2,1,0:T(8,128)(2,1)}), bf16[128,64,256]{2,1,0:T(8,128)(2,1)}, u32[]{:S(2)}, u32[]{:S(2)}) async-start(bf16[128,64,256]{2,1,0:T(8,128)(2,1)} %get-tuple-element.48), calls=%async_computation.1 | async-start | bytes 8388608 | tf_op jit(solution)/shard_map/all_to_all | solution.py:397
  36.9 13.6 %collective-permute-start.2 = (bf16[2,64,16,128]{3,2,1,0:T(8,128)(2,1)}, bf16[2,64,16,128]{3,2,1,0:T(8,128)(2,1)S(1)}, u32[]{:S(2)}, u32[]{:S(2)}) collective-permute-start(bf16[2,64,16,128]{3,2,1,0:T(8,128)(2,1)} %get-tuple-element.36), channel_id=1, source_target_pairs={{0,1},{1,0},{2,3},{3,2},{4,5},{5,4},{6,7},{7,6},{8,9},{9,8},{10,11... | collective-permute-start | bytes 1572872 | tf_op jit(solution)/shard_map/ppermute | solution.py:401
  38.2 14.4 %collective-permute-start.3 = (bf16[2,64,16,128]{3,2,1,0:T(8,128)(2,1)}, bf16[2,64,16,128]{3,2,1,0:T(8,128)(2,1)S(1)}, u32[]{:S(2)}, u32[]{:S(2)}) collective-permute-start(bf16[2,64,16,128]{3,2,1,0:T(8,128)(2,1)} %get-tuple-element.38), channel_id=1, source_target_pairs={{0,3},{1,2},{2,1},{3,0},{4,7},{5,6},{6,5},{7,4},{8,11},{9,10},{10,... | collective-permute-start | bytes 1572872 | tf_op jit(solution)/shard_map/ppermute | solution.py:401
  40.1 40.7 %collective-permute-start = (bf16[2,64,32,128]{3,2,1,0:T(8,128)(2,1)}, bf16[2,64,32,128]{3,2,1,0:T(8,128)(2,1)}, u32[]{:S(2)}, u32[]{:S(2)}) collective-permute-start(bf16[2,64,32,128]{3,2,1,0:T(8,128)(2,1)} %get-tuple-element.33), channel_id=1, source_target_pairs={{0,1},{1,0},{2,3},{3,2},{4,5},{5,4},{6,7},{7,6},{8,9},{9,8},{10,11... | collective-permute-start | bytes 3145736 | tf_op jit(solution)/shard_map/ppermute | solution.py:401
  40.4 40.4 %collective-permute-start.1 = (bf16[2,64,32,128]{3,2,1,0:T(8,128)(2,1)}, bf16[2,64,32,128]{3,2,1,0:T(8,128)(2,1)}, u32[]{:S(2)}, u32[]{:S(2)}) collective-permute-start(bf16[2,64,32,128]{3,2,1,0:T(8,128)(2,1)} %get-tuple-element.34), channel_id=1, source_target_pairs={{0,3},{1,2},{2,1},{3,0},{4,7},{5,6},{6,5},{7,4},{8,11},{9,10},{10,... | collective-permute-start | bytes 3145736 | tf_op jit(solution)/shard_map/ppermute | solution.py:401
  50.5 36.9 %copy-start.3 = (bf16[2,64,16,128]{3,2,1,0:T(8,128)(2,1)}, bf16[2,64,16,128]{3,2,1,0:T(8,128)(2,1)S(1)}, u32[]{:S(2)}) copy-start(bf16[2,64,16,128]{3,2,1,0:T(8,128)(2,1)S(1)} %collective-permute-done.2.got_a) | copy-start | bytes 1572868
  52.7 34.8 %copy-start.4 = (bf16[2,64,16,128]{3,2,1,0:T(8,128)(2,1)}, bf16[2,64,16,128]{3,2,1,0:T(8,128)(2,1)S(1)}, u32[]{:S(2)}) copy-start(bf16[2,64,16,128]{3,2,1,0:T(8,128)(2,1)S(1)} %collective-permute-done.3.got_b) | copy-start | bytes 1572868
  52.7 28.0 %collective-permute-start.4 = (bf16[64,16,128]{2,1,0:T(8,128)(2,1)S(1)}, bf16[64,16,128]{2,1,0:T(8,128)(2,1)S(1)}, u32[]{:S(2)}, u32[]{:S(2)}) collective-permute-start(bf16[64,16,128]{2,1,0:T(8,128)(2,1)S(1)} %fusion.2), channel_id=1, source_target_pairs={{0,3},{1,2},{2,1},{3,0},{4,7},{5,6},{6,5},{7,4},{8,11},{9,10},{10,... | collective-permute-start | bytes 786440 | tf_op jit(solution)/shard_map/ppermute | solution.py:408
  54.6 26.1 %collective-permute-start.5 = (bf16[64,16,128]{2,1,0:T(8,128)(2,1)S(1)}, bf16[64,16,128]{2,1,0:T(8,128)(2,1)S(1)}, u32[]{:S(2)}, u32[]{:S(2)}) collective-permute-start(bf16[64,16,128]{2,1,0:T(8,128)(2,1)S(1)} %fusion.3), channel_id=1, source_target_pairs={{0,1},{1,0},{2,3},{3,2},{4,5},{5,4},{6,7},{7,6},{8,9},{9,8},{10,11... | collective-permute-start | bytes 786440 | tf_op jit(solution)/shard_map/ppermute | solution.py:408
  80.7 0.7 copy-start.7
  80.7 0.8 copy-start.8
  83.2 25.4 %collective-permute-start.6 = (bf16[64,32,128]{2,1,0:T(8,128)(2,1)S(1)}, bf16[64,32,128]{2,1,0:T(8,128)(2,1)S(1)}, u32[]{:S(2)}, u32[]{:S(2)}) collective-permute-start(bf16[64,32,128]{2,1,0:T(8,128)(2,1)S(1)} %get-tuple-element.44), channel_id=1, source_target_pairs={{0,3},{1,2},{2,1},{3,0},{4,7},{5,6},{6,5},{7,4},{8,11},{9,10},{10,... | collective-permute-start | bytes 1572872 | tf_op jit(solution)/shard_map/ppermute | solution.py:408
  85.1 23.5 %collective-permute-start.7 = (bf16[64,32,128]{2,1,0:T(8,128)(2,1)S(1)}, bf16[64,32,128]{2,1,0:T(8,128)(2,1)S(1)}, u32[]{:S(2)}, u32[]{:S(2)}) collective-permute-start(bf16[64,32,128]{2,1,0:T(8,128)(2,1)S(1)} %get-tuple-element.45), channel_id=1, source_target_pairs={{0,1},{1,0},{2,3},{3,2},{4,5},{5,4},{6,7},{7,6},{8,9},{9,8},{10,11... | collective-permute-start | bytes 1572872 | tf_op jit(solution)/shard_map/ppermute | solution.py:408
  91.1 24.1 %all-to-all-start.2 = ((bf16[128,16,256]{2,1,0:T(8,128)(2,1)}), bf16[128,16,256]{2,1,0:T(8,128)(2,1)S(1)}, u32[]{:S(2)}, u32[]{:S(2)}) async-start(bf16[128,16,256]{2,1,0:T(8,128)(2,1)} %fill_slots.3), calls=%async_computation.2 | async-start | bytes 2097152 | tf_op jit(solution)/shard_map/all_to_all | solution.py:420
  104.9 18.1 %collective-permute-start.8 = (bf16[16,64,256]{2,1,0:T(8,128)(2,1)}, bf16[16,64,256]{2,1,0:T(8,128)(2,1)}, u32[]{:S(2)}, u32[]{:S(2)}) collective-permute-start(bf16[16,64,256]{2,1,0:T(8,128)(2,1)} %get-tuple-element.56), channel_id=1, source_target_pairs={{0,1},{1,0},{2,3},{3,2},{4,5},{5,4},{6,7},{7,6},{8,9},{9,8},{10,11... | collective-permute-start | bytes 1572872 | tf_op jit(solution)/shard_map/ppermute | solution.py:423
  106.2 24.0 %collective-permute-start.9 = (bf16[16,64,256]{2,1,0:T(8,128)(2,1)}, bf16[16,64,256]{2,1,0:T(8,128)(2,1)}, u32[]{:S(2)}, u32[]{:S(2)}) collective-permute-start(bf16[16,64,256]{2,1,0:T(8,128)(2,1)} %get-tuple-element.57), channel_id=1, source_target_pairs={{0,3},{1,2},{2,1},{3,0},{4,7},{5,6},{6,5},{7,4},{8,11},{9,10},{10,... | collective-permute-start | bytes 1572872 | tf_op jit(solution)/shard_map/ppermute | solution.py:423
  108.0 24.0 %collective-permute-start.10 = (bf16[16,64,256]{2,1,0:T(8,128)(2,1)}, bf16[16,64,256]{2,1,0:T(8,128)(2,1)}, u32[]{:S(2)}, u32[]{:S(2)}) collective-permute-start(bf16[16,64,256]{2,1,0:T(8,128)(2,1)} %get-tuple-element.58), channel_id=1, source_target_pairs={{0,2},{1,3},{2,0},{3,1},{4,6},{5,7},{6,4},{7,5},{8,10},{9,11},{10,... | collective-permute-start | bytes 1572872 | tf_op jit(solution)/shard_map/ppermute | solution.py:423
  108.6 0.8 copy-start.9
  109.4 0.8 copy-start.10
  115.2 16.8 %copy-start.5 = (bf16[128,16,256]{2,1,0:T(8,128)(2,1)}, bf16[128,16,256]{2,1,0:T(8,128)(2,1)S(1)}, u32[]{:S(2)}) copy-start(bf16[128,16,256]{2,1,0:T(8,128)(2,1)S(1)} %all-to-all-done.2.received) | copy-start | bytes 3145732
  115.2 34.7 %all-to-all-start = ((bf16[128,32,256]{2,1,0:T(8,128)(2,1)}), bf16[128,32,256]{2,1,0:T(8,128)(2,1)S(1)}, u32[]{:S(2)}, u32[]{:S(2)}) async-start(bf16[128,32,256]{2,1,0:T(8,128)(2,1)} %fill_slots.2), calls=%async_computation | async-start | bytes 4194304 | tf_op jit(solution)/shard_map/all_to_all | solution.py:427
  150.0 1.3 copy-start

commit v4 on v3

v4 whole, which is shorter than its diff:
```python
import functools

import jax
import jax.numpy as jnp
from jax import lax
from jax.experimental import pallas as pl
from jax.experimental.pallas import tpu as pltpu
from jax.sharding import PartitionSpec as P

LANES = 128
EARLY_ROWS = 16
CHUNKS = (16, 32)
SIDES = 2
HEAD = 3
AHEAD = 2
BF16 = jnp.bfloat16
F32 = jnp.float32


SMALL_VMEM = 20 * 2**20
IN_VMEM = pl.BlockSpec(memory_space=pltpu.VMEM)


def small_cost():
    return pl.CostEstimate(flops=1, bytes_accessed=1, transcendentals=0)


def large_cost():
    return pl.CostEstimate(flops=6 * 10**10, bytes_accessed=1, transcendentals=0)


def whole(shape):
    return pl.BlockSpec(shape, lambda i, *_: (0,) * len(shape))


def relative_quarters(x):
    return x, x ^ 1, 3 - x, (3 - x) ^ 1


def products_kernel(
    capacity, device, block_left, block_right, channel_class, own_targets, psi_hbm, left_hbm,
    right_hbm, own, slots_hbm, *rest
):
    chunk_outs = rest[: 4 * len(CHUNKS)]
    (
        psi_ref, left_ref, right_ref, half_ref, acc_ref, stage_ref, seen_ref, first_ref, empty_ref,
        slot_ref, psi_sems, left_sems, right_sems, slot_sems,
    ) = rest[4 * len(CHUNKS) :]
    channels, left_count, _, _ = left_ref.shape
    right_count = right_ref.shape[1]
    classes = acc_ref.shape[1]
    hops = classes - 1
    quarter = acc_ref.shape[2] // 4
    head = SIDES * HEAD
    step = pl.program_id(0)
    steps = pl.num_programs(0)
    blocks = SIDES * steps
    x = device[0]

    def psi_copy(part):
        at = pl.ds(0, head) if part == 0 else pl.ds(head, psi_ref.shape[0] - head)
        return pltpu.make_async_copy(psi_hbm.at[at], psi_ref.at[at], psi_sems.at[part])

    def left_copy(w):
        return pltpu.make_async_copy(left_hbm.at[w], left_ref.at[w], left_sems.at[w])

    def right_copy(w):
        return pltpu.make_async_copy(right_hbm.at[w], right_ref.at[w], right_sems.at[w])

    def slot_copy(turn, side, h):
        flip = lax.rem(turn, 2)
        k = SIDES * turn + side
        return pltpu.make_async_copy(
            stage_ref.at[flip, side, h],
            slots_hbm.at[slot_ref[k * hops + h]],
            slot_sems.at[flip, side, h],
        )

    def each_slot(turn, act):
        for side in range(SIDES):
            for h in range(hops):
                act(slot_copy(turn, side, h))

    def sectors(k):
        return (
            block_left[k] - device[1] * left_count,
            block_right[k] - device[2] * right_count,
        )

    def first_product(w, k, left_id, place):
        half_ref[place] = jnp.dot(
            left_ref[w, left_id], psi_ref[k], preferred_element_type=F32
        ).astype(BF16)

    def second_product(w, right_id, place, at):
        full = jnp.dot(half_ref[place], right_ref[w, right_id], preferred_element_type=F32)
        member = channel_class[x * channels + w]
        before = acc_ref[at, member]
        acc_ref[at, member] = jnp.where(first_ref[w] != 0, 0.0, before) + full

    def emit_parts():
        flip = lax.rem(step, 2)
        here, beside, mirror, across = relative_quarters(x)
        orders = ((here, mirror, beside, across), (here, beside, mirror, across))

        def early_part(side, at, h):
            for q in range(4):
                rows = slice(q * EARLY_ROWS, (q + 1) * EARLY_ROWS)
                first = q * quarter
                stage_ref[flip, side, h, rows] = acc_ref[
                    at, h + 1, first : first + EARLY_ROWS
                ].astype(BF16)

        def own_part(side, at, place, q):
            row = pl.multiple_of(q * quarter, quarter)
            own[place, side] = acc_ref[at, 0, pl.ds(row, quarter)].astype(BF16)

        def chunk_part(side, at, h, j, start, rows, s):
            keep, send = chunk_outs[4 * j + 2 * s : 4 * j + 2 * s + 2]
            for place, q in enumerate(orders[s]):
                target = keep if place < 2 else send
                row = pl.multiple_of(q * quarter + start, 16)
                target[place % 2, side * hops + h] = acc_ref[
                    at, h + 1, pl.ds(row, rows), s * LANES : (s + 1) * LANES
                ].astype(BF16)

        work = []
        for side in range(SIDES):
            at = SIDES * lax.rem(step, HEAD) + side
            for h in range(hops):
                work.append(functools.partial(early_part, side, at, h))
            for place, q in enumerate((here, beside, mirror, across)):
                work.append(functools.partial(own_part, side, at, place, q))
            start = EARLY_ROWS
            for j, rows in enumerate(CHUNKS):
                for s in range(2):
                    for h in range(hops):
                        work.append(
                            functools.partial(chunk_part, side, at, h, j, start, rows, s)
                        )
                start += rows
        return work

    @pl.when(step == 0)
    def _():
        psi_copy(0).start()
        for w in range(AHEAD):
            left_copy(w).start()
            right_copy(w).start()
        for i in range(seen_ref.shape[0]):
            seen_ref[i] = 0

        def place(i, _):
            owner = lax.div(own_targets[i], blocks)
            earlier = seen_ref[owner]
            slot_ref[i] = owner * capacity + earlier
            seen_ref[owner] = earlier + 1
            return 0

        lax.fori_loop(0, slot_ref.shape[0], place, 0)
        for c in range(classes):
            empty_ref[c] = 1
        for w in range(channels):
            member = channel_class[x * channels + w]
            first_ref[w] = empty_ref[member]
            empty_ref[member] = 0
        for c in range(classes):

            @pl.when(empty_ref[c] != 0)
            def _():
                for at in range(head):
                    acc_ref[at, c] = jnp.zeros(acc_ref.shape[2:], F32)

        psi_copy(0).wait()

        def channel(w, _):
            left_copy(w).wait()
            right_copy(w).wait()

            @pl.when(w + AHEAD < channels)
            def _():
                left_copy(w + AHEAD).start()
                right_copy(w + AHEAD).start()

            @pl.when(w + AHEAD == channels)
            def _():
                psi_copy(1).start()

            ids = [sectors(k) for k in range(head)]
            for k in range(head):
                first_product(w, k, ids[k][0], k)
            for k in range(head):
                second_product(w, ids[k][1], k, k)
            return 0

        lax.fori_loop(0, channels, channel, 0)
        for part in emit_parts():
            part()

    @pl.when(step == 1)
    def _():
        psi_copy(1).wait()

    @pl.when(step >= 2)
    def _():
        each_slot(step - 2, lambda copy: copy.wait())

    @pl.when((step > 0) & (step <= steps - HEAD))
    def _():
        work = emit_parts()
        turns = SIDES * channels
        pair = step + HEAD - 1
        for side in range(SIDES):
            k = SIDES * pair + side
            left_id, right_id = sectors(k)
            at = SIDES * lax.rem(pair, HEAD) + side
            for w in range(channels):
                first_product(w, k, left_id, side * channels + w)
            for w in range(channels):
                second_product(w, right_id, side * channels + w, at)
                turn = side * channels + w
                for part in work[turn * len(work) // turns : (turn + 1) * len(work) // turns]:
                    part()

    @pl.when(step > steps - HEAD)
    def _():
        for part in emit_parts():
            part()

    each_slot(step, lambda copy: copy.start())

    @pl.when(step == steps - 1)
    def _():
        each_slot(step - 1, lambda copy: copy.wait())
        each_slot(step, lambda copy: copy.wait())


def products(tables, owners, capacity, psi, left_env, right_env, classes):
    blocks, block, _ = psi.shape
    channels = left_env.shape[0]
    quarter = block // 4
    early = 4 * EARLY_ROWS
    hops = classes - 1
    head = SIDES * HEAD
    out_shape = [
        pltpu.HBM((4, blocks, quarter, block), BF16),
        pltpu.HBM((owners * capacity, early, block), BF16),
    ]
    out_specs = [
        pl.BlockSpec((4, SIDES, quarter, block), lambda k, *_: (0, k, 0, 0)),
        pl.BlockSpec(memory_space=pltpu.HBM),
    ]
    for rows in CHUNKS:
        out_shape += [pltpu.HBM((2, blocks * hops, rows, LANES), BF16)] * 4
        block_shape = (2, SIDES * hops, rows, LANES)
        out_specs += [pl.BlockSpec(block_shape, lambda k, *_: (0, k, 0, 0))] * 4
    return pl.pallas_call(
        functools.partial(products_kernel, capacity),
        out_shape=out_shape,
        grid_spec=pltpu.PrefetchScalarGridSpec(
            num_scalar_prefetch=len(tables),
            grid=(blocks // SIDES,),
            in_specs=[pl.BlockSpec(memory_space=pltpu.HBM)] * 3,
            out_specs=out_specs,
            scratch_shapes=[
                pltpu.VMEM(psi.shape, BF16),
                pltpu.VMEM(left_env.shape, BF16),
                pltpu.VMEM(right_env.shape, BF16),
                pltpu.VMEM((max(head, SIDES * channels), block, block), BF16),
                pltpu.VMEM((head, classes, block, block), F32),
                pltpu.VMEM((2, SIDES, hops, early, block), BF16),
                pltpu.SMEM((owners,), jnp.int32),
                pltpu.SMEM((channels,), jnp.int32),
                pltpu.SMEM((classes,), jnp.int32),
                pltpu.SMEM((blocks * hops,), jnp.int32),
                pltpu.SemaphoreType.DMA((2,)),
                pltpu.SemaphoreType.DMA((channels,)),
                pltpu.SemaphoreType.DMA((channels,)),
                pltpu.SemaphoreType.DMA((2, SIDES, hops)),
            ],
        ),
        compiler_params=pltpu.CompilerParams(vmem_limit_bytes=60 * 2**20),
        cost_estimate=pl.CostEstimate(
            flops=4 * channels * blocks * block**3,
            bytes_accessed=2 * (left_env.size + right_env.size + psi.size * (1 + classes)),
            transcendentals=0,
        ),
        name="products",
    )(*tables, psi, left_env, right_env)


def slots_kernel(positions, keep_a, got_a, last_a, keep_b, got_b, last_b, slots, stage, sems):
    def total(keep, got, last, i):
        value = keep[0, i].astype(F32) + got[0, i].astype(F32) + last[i].astype(F32)
        return value.astype(BF16)

    def copy(i):
        return pltpu.make_async_copy(stage.at[i], slots.at[positions[i]], sems.at[i])

    def fill(i, _):
        stage[i, :, :LANES] = total(keep_a, got_a, last_a, i)
        stage[i, :, LANES:] = total(keep_b, got_b, last_b, i)
        copy(i).start()
        return 0

    def finish(i, _):
        copy(i).wait()
        return 0

    lax.fori_loop(0, stage.shape[0], fill, 0, unroll=4)
    lax.fori_loop(0, stage.shape[0], finish, 0, unroll=4)


def fill_slots(positions, slot_count, parts, final):
    _, count, rows, _ = parts[0].shape
    return pl.pallas_call(
        slots_kernel,
        out_shape=pltpu.HBM((slot_count, rows, 2 * LANES), BF16),
        grid_spec=pltpu.PrefetchScalarGridSpec(
            num_scalar_prefetch=1,
            grid=(1,),
            in_specs=[IN_VMEM] * 6,
            out_specs=pl.BlockSpec(memory_space=pltpu.HBM),
            scratch_shapes=[
                pltpu.VMEM((count, rows, 2 * LANES), BF16),
                pltpu.SemaphoreType.DMA((count,)),
            ],
        ),
        compiler_params=pltpu.CompilerParams(vmem_limit_bytes=SMALL_VMEM),
        cost_estimate=large_cost() if final else small_cost(),
        name="fill_slots",
    )(positions, *parts)


def merge_kernel(device, places, received, own, *rest):
    *outs, acc = rest
    _, blocks, quarter, _ = own.shape
    at = [pl.multiple_of(q * EARLY_ROWS, EARLY_ROWS) for q in relative_quarters(device[0])]
    for p in range(4):
        acc[:blocks, pl.ds(at[p], EARLY_ROWS)] = own[p, :, :EARLY_ROWS].astype(F32)

    def add(p, _):
        acc[places[p]] += received[p].astype(F32)
        return 0

    lax.fori_loop(0, received.shape[0], add, 0, unroll=4)
    for p in range(4):
        outs[p][:, :EARLY_ROWS] = acc[:blocks, pl.ds(at[p], EARLY_ROWS)].astype(BF16)
        outs[p][:, EARLY_ROWS:] = own[p, :, EARLY_ROWS:]


def merge_early(device, places, received, own):
    _, blocks, quarter, width = own.shape
    return pl.pallas_call(
        merge_kernel,
        out_shape=[pltpu.HBM((blocks, quarter, width), BF16)] * 4,
        grid_spec=pltpu.PrefetchScalarGridSpec(
            num_scalar_prefetch=2,
            grid=(1,),
            in_specs=[IN_VMEM, IN_VMEM],
            out_specs=[whole((blocks, quarter, width))] * 4,
            scratch_shapes=[pltpu.VMEM((blocks + 1, 4 * EARLY_ROWS, width), F32)],
        ),
        compiler_params=pltpu.CompilerParams(vmem_limit_bytes=SMALL_VMEM),
        cost_estimate=small_cost(),
        name="merge_early",
    )(device, places, received, own)


def add_slots(acc, places, received):
    def add(p, _):
        acc[places[p]] += received[p].astype(F32)
        return 0

    lax.fori_loop(0, received.shape[0], add, 0, unroll=4)


def first_sum(places, received, mine, others, start):
    blocks, quarter, width = mine.shape
    rows = received.shape[1]

    def kernel(places, received, *rest):
        *parts, result, acc = rest

        def total(at):
            value = parts[0][:, at].astype(F32)
            for part in parts[1:]:
                value = value + part[:, at].astype(F32)
            return value

        acc[:blocks] = total(slice(start, start + rows))
        add_slots(acc, places, received)
        result[:, :start] = total(slice(0, start))
        result[:, start : start + rows] = acc[:blocks]
        result[:, start + rows :] = total(slice(start + rows, quarter))

    return pl.pallas_call(
        kernel,
        out_shape=pltpu.HBM(mine.shape, F32),
        grid_spec=pltpu.PrefetchScalarGridSpec(
            num_scalar_prefetch=1,
            grid=(1,),
            in_specs=[IN_VMEM] * (2 + len(others)),
            out_specs=whole(mine.shape),
            scratch_shapes=[pltpu.VMEM((blocks + 1, rows, width), F32)],
        ),
        compiler_params=pltpu.CompilerParams(vmem_limit_bytes=SMALL_VMEM),
        cost_estimate=large_cost(),
        name="first_sum",
    )(places, received, mine, *others)


def last_sum(places, received, so_far, start):
    blocks, _, width = so_far.shape
    rows = received.shape[1]
    part = pl.BlockSpec((blocks, rows, width), lambda i, *_: (0, start // rows, 0))

    def kernel(places, received, so_far, result, acc):
        acc[:blocks] = so_far[...]
        add_slots(acc, places, received)
        result[...] = acc[:blocks]

    return pl.pallas_call(
        kernel,
        out_shape=pltpu.HBM(so_far.shape, F32),
        grid_spec=pltpu.PrefetchScalarGridSpec(
            num_scalar_prefetch=1,
            grid=(1,),
            in_specs=[IN_VMEM, part],
            out_specs=part,
            scratch_shapes=[pltpu.VMEM((blocks + 1, rows, width), F32)],
        ),
        input_output_aliases={2: 0},
        compiler_params=pltpu.CompilerParams(vmem_limit_bytes=SMALL_VMEM),
        cost_estimate=small_cost(),
        name="last_sum",
    )(places, received, so_far)


def item_places(targets, block_count):
    destined = targets // block_count
    count = targets.shape[-1]
    earlier = jnp.arange(count)[:, None] > jnp.arange(count)[None, :]
    same = (destined[..., :, None] == destined[..., None, :]) & earlier
    return destined, jnp.sum(same.astype(jnp.int32), axis=-1)


def shards(wavefunction, left_env, right_env, block_left, block_right, channel_class, hop_target):
    block_count = wavefunction.shape[0]
    hop_count = hop_target.shape[1]
    owners = lax.axis_size("lsec") * lax.axis_size("rsec")
    item_count = block_count * hop_count
    capacity = 2 * ((item_count + owners - 1) // owners)
    slot_count = owners * capacity
    me = lax.axis_index("lsec") * lax.axis_size("rsec") + lax.axis_index("rsec")
    device = jnp.stack([lax.axis_index(axis) for axis in ("mpo", "lsec", "rsec")]).astype(jnp.int32)
    targets = hop_target.reshape(owners, item_count)
    own_targets = lax.dynamic_index_in_dim(targets, me, 0, False)
    own, early_slots, *parts = products(
        (device, block_left, block_right, channel_class, own_targets),
        owners,
        capacity,
        wavefunction,
        left_env,
        right_env,
        hop_count + 1,
    )

    destined, slot = item_places(own_targets, block_count)
    position = destined * capacity + slot
    destined_all, slot_all = item_places(targets, block_count)
    mine = (destined_all == me)[:, :, None] & (
        slot_all[:, :, None] == jnp.arange(capacity, dtype=jnp.int32)
    )
    local = targets - (me + 1) * block_count
    places = jnp.sum(jnp.where(mine, local[:, :, None], 0), axis=1).reshape(slot_count)
    places = places + block_count

    beside = [(i, i ^ 1) for i in range(4)]
    mirror = [(i, 3 - i) for i in range(4)]
    across = [(i, (i + 2) % 4) for i in range(4)]

    def second(keep, got):
        return (keep[1].astype(F32) + got[1].astype(F32)).astype(BF16)

    early = lax.all_to_all(early_slots, ("lsec", "rsec"), 0, 0, tiled=True)
    got, last = [], []
    for j in range(len(CHUNKS)):
        keep_a, send_a, keep_b, send_b = parts[4 * j : 4 * j + 4]
        got.append((lax.ppermute(send_a, "mpo", beside), lax.ppermute(send_b, "mpo", mirror)))
    for j in range(len(CHUNKS)):
        keep_a, _, keep_b, _ = parts[4 * j : 4 * j + 4]
        got_a, got_b = got[j]
        if j > 0:
            got_a, got_b, *last[j - 1] = lax.optimization_barrier((got_a, got_b, *last[j - 1]))
        then_a, then_b = lax.optimization_barrier((second(keep_a, got_a), second(keep_b, got_b)))
        last.append([lax.ppermute(then_a, "mpo", mirror), lax.ppermute(then_b, "mpo", beside)])

    def send(j, last_a, last_b):
        keep_a, _, keep_b, _ = parts[4 * j : 4 * j + 4]
        group = (keep_a, got[j][0], last_a, keep_b, got[j][1], last_b)
        return fill_slots(position, slot_count, group, j + 1 == len(CHUNKS))

    last_a, last_b, then_a, then_b = lax.optimization_barrier((*last[0], then_a, then_b))
    slots = send(0, last_a, last_b)
    early, slots = lax.optimization_barrier((early, slots))
    received = lax.all_to_all(slots, ("lsec", "rsec"), 0, 0, tiled=True)
    out_mine, *out_others = merge_early(device, places, early, own)
    slots = send(1, *last[1])
    out_others, slots = lax.optimization_barrier((out_others, slots))
    others = [
        lax.ppermute(part, "mpo", pairs)
        for part, pairs in zip(out_others, (beside, mirror, across))
    ]
    received_last = lax.all_to_all(slots, ("lsec", "rsec"), 0, 0, tiled=True)
    base = first_sum(places, received, out_mine, others, EARLY_ROWS)
    return last_sum(places, received_last, base, EARLY_ROWS + CHUNKS[0])


def solution(mesh):
    in_specs = (
        P(("lsec", "rsec"), None, None),
        P("mpo", "lsec", None, None),
        P("mpo", "rsec", None, None),
        P(("lsec", "rsec")),
        P(("lsec", "rsec")),
        P(),
        P(),
    )
    out_specs = P(("lsec", "rsec"), "mpo", None)
    return jax.shard_map(shards, mesh=mesh, in_specs=in_specs, out_specs=out_specs, check_vma=False)
```

time: 156 us -> 150 us (0.962)
  Pallas kernels: 46.9 us -> 40.3 us
    all_to_all x1, waiting for transfers between devices: 13.6 us -> 8.54 us  [shards(): received_last = lax.all_to_all(slots, ('lsec', 'rsec'), 0, 0, tiled=True)]
    ppermute x3, waiting for transfers between devices: 8.97 us -> 13.6 us  [shards(): lax.ppermute(part, 'mpo', pairs)]
    pallas_call x2, Pallas kernels: 8.53 us -> 6.1 us  [fill_slots(): pl.pallas_call(slots_kernel, out_shape=pltpu.HBM((slot_count, rows, 2 * L...]
    pallas_call x1, Pallas kernels: 24.1 us -> 22 us  [products(): pl.pallas_call(functools.partial(products_kernel, capacity), out_shape=ou...]
    all_to_all x1, waiting for transfers between devices: 0.16 us -> 1.98 us  [shards(): received = lax.all_to_all(slots, ('lsec', 'rsec'), 0, 0, tiled=True)]
    all_to_all x1, waiting for transfers between devices: 1.6 us -> 0.01 us  [shards(): early = lax.all_to_all(early_slots, ('lsec', 'rsec'), 0, 0, tiled=True)]
    unnamed x23 -> x21, local copies, waits for them, and re-layouts: 4.55 us -> 4.92 us
  transfers between devices with their start and end apart: 14 -> 14, of which waited for: 8 -> 6; matrix products, arithmetic and copies ran while one was open for 3% -> 3% of each run, Pallas kernels for 12% -> 10%
where the time goes in v4:
time: 150 us; the launch traced here: 149 us
  waiting for transfers between devices  60.7 us (40%)
  Pallas kernels  40.3 us (27%)
  starting transfers between devices  37.6 us (25%)
  other arithmetic  5.28 us (4%)
  local copies, waits for them, and re-layouts  5.26 us (4%)
    ppermute x2, waiting for transfers between devices, shards(): lax.ppermute(then_a, 'mpo', mirror)  25 us
    pallas_call x1, Pallas kernels, products(): pl.pallas_call(functools.partial(products_kernel, capacity), out_shape=ou...  22 us
    ppermute x3, waiting for transfers between devices, shards(): lax.ppermute(part, 'mpo', pairs)  13.6 us
    all_to_all x1, starting transfers between devices, shards(): early = lax.all_to_all(early_slots, ('lsec', 'rsec'), 0, 0, tiled=True)  9.81 us
    ppermute x2, waiting for transfers between devices, shards(): lax.ppermute(send_a, 'mpo', beside)  9.53 us
    all_to_all x1, starting transfers between devices, shards(): received = lax.all_to_all(slots, ('lsec', 'rsec'), 0, 0, tiled=True)  8.67 us
    all_to_all x1, waiting for transfers between devices, shards(): received_last = lax.all_to_all(slots, ('lsec', 'rsec'), 0, 0, tiled=True)  8.54 us
    all_to_all x1, starting transfers between devices, shards(): received_last = lax.all_to_all(slots, ('lsec', 'rsec'), 0, 0, tiled=True)  7.87 us
  transfers between devices with their start and end apart: 14, of which 6 were waited for; matrix products, arithmetic and copies ran while one was open for 3% of the time, Pallas kernels for 10%

profile of v4, /device:TPU:1, one launch (start us, length us, event | category | flops | bytes accessed | tf_op | source)
XLA Modules:
  0.0 149.4 jit_solution(17857629984840266610)
XLA Ops:
  0.0 0.8 copy.10
  1.0 0.6 and_select_fusion.1
  1.6 0.7 pad_add_fusion.device
  2.2 22.0 %products.1 = (bf16[4,16,64,256]{3,2,1,0:T(8,128)(2,1)}, bf16[128,64,256]{2,1,0:T(8,128)(2,1)}, bf16[2,64,16,128]{3,2,1,0:T(8,128)(2,1)}, bf16[2,64,16,128]{3,2,...) custom-call(s32[3]{0:T(128)} %pad_add_fusion.device, ...), custom_call_target="tpu_custom_call" | custom-call | flops 10737418240 | bytes 23068672 | tf_op jit(solution)/shard_map/products/pallas_call | solution.py:257
  24.2 9.8 %all-to-all-start = ((bf16[128,64,256]{2,1,0:T(8,128)(2,1)}), bf16[128,64,256]{2,1,0:T(8,128)(2,1)}, u32[]{:S(2)}, u32[]{:S(2)}) async-start(bf16[128,64,256]{2,1,0:T(8,128)(2,1)} %get-tuple-element.35), calls=%async_computation | async-start | bytes 8388608 | tf_op jit(solution)/shard_map/all_to_all | solution.py:486
  34.1 1.3 collective-permute-start
  35.4 1.8 %collective-permute-start.3 = (bf16[2,64,16,128]{3,2,1,0:T(8,128)(2,1)}, bf16[2,64,16,128]{3,2,1,0:T(8,128)(2,1)S(1)}, u32[]{:S(2)}, u32[]{:S(2)}) collective-permute-start(bf16[2,64,16,128]{3,2,1,0:T(8,128)(2,1)} %get-tuple-element.41), channel_id=1, source_target_pairs={{0,3},{1,2},{2,1},{3,0},{4,7},{5,6},{6,5},{7,4},{8,11},{9,10},{10,... | collective-permute-start | bytes 1572872 | tf_op jit(solution)/shard_map/ppermute | solution.py:490
  37.5 0.6 collective-permute-start.2
  38.1 9.5 %collective-permute-done.got_a = bf16[2,64,16,128]{3,2,1,0:T(8,128)(2,1)S(1)} collective-permute-done((bf16[2,64,16,128]{3,2,1,0:T(8,128)(2,1)}, bf16[2,64,16,128]{3,2,1,0:T(8,128)(2,1)S(1)}, u32[]{:S(2)}, u32[]{:S(2)}) %collective-permute-start) | collective-permute-done | bytes 524320 | tf_op jit(solution)/shard_map/ppermute | solution.py:490
  47.7 2.0 %collective-permute-done.3.got_b = bf16[2,64,16,128]{3,2,1,0:T(8,128)(2,1)S(1)} collective-permute-done((bf16[2,64,16,128]{3,2,1,0:T(8,128)(2,1)}, bf16[2,64,16,128]{3,2,1,0:T(8,128)(2,1)S(1)}, u32[]{:S(2)}, u32[]{:S(2)}) %collective-permute-start.3) | collective-permute-done | bytes 524320 | tf_op jit(solution)/shard_map/ppermute | solution.py:490
  49.8 1.9 %collective-permute-start.4 = (bf16[64,16,128]{2,1,0:T(8,128)(2,1)S(1)}, bf16[64,16,128]{2,1,0:T(8,128)(2,1)S(1)}, u32[]{:S(2)}, u32[]{:S(2)}) collective-permute-start(bf16[64,16,128]{2,1,0:T(8,128)(2,1)S(1)} %fusion.2), channel_id=1, source_target_pairs={{0,3},{1,2},{2,1},{3,0},{4,7},{5,6},{6,5},{7,4},{8,11},{9,10},{10,... | collective-permute-start | bytes 786440 | tf_op jit(solution)/shard_map/ppermute | solution.py:497
  51.7 0.9 convert_reduce_fusion
  52.8 25.0 %collective-permute-done.4.last_a = bf16[64,16,128]{2,1,0:T(8,128)(2,1)S(1)} collective-permute-done((bf16[64,16,128]{2,1,0:T(8,128)(2,1)S(1)}, bf16[64,16,128]{2,1,0:T(8,128)(2,1)S(1)}, u32[]{:S(2)}, u32[]{:S(2)}) %collective-permute-start.4) | collective-permute-done | bytes 262176 | tf_op jit(solution)/shard_map/ppermute | solution.py:497
  77.9 0.7 copy-done.6
  78.6 2.6 %fusion = (bf16[64,32,128]{2,1,0:T(8,128)(2,1)}, bf16[64,32,128]{2,1,0:T(8,128)(2,1)}) fusion(bf16[2,64,32,128]{3,2,1,0:T(8,128)(2,1)} %collective-permute-done.1.got_a, bf16[2,64,32,128]{3,2,1,0:T(8,128)(2,1)S(1)} %copy-done.3, bf16[2,64,32,128]{3,2,1,0:T(8,128)(2,1)} %collective-permute-done.2.got_b, bf16[2,64,32,128]{3,2,1,0:T(8,128)(2,1)} %get-tuple-element.48.keep_b), kind=kLoop, calls=%fused_computation.3 | loop fusion | flops 2097152 | bytes 3145728 | tf_op jit(solution)/shard_map/convert_element_type | solution.py:484
  81.2 1.8 %collective-permute-start.6 = (bf16[64,32,128]{2,1,0:T(8,128)(2,1)}, bf16[64,32,128]{2,1,0:T(8,128)(2,1)}, u32[]{:S(2)}, u32[]{:S(2)}) collective-permute-start(bf16[64,32,128]{2,1,0:T(8,128)(2,1)} %get-tuple-element.50), channel_id=1, source_target_pairs={{0,3},{1,2},{2,1},{3,0},{4,7},{5,6},{6,5},{7,4},{8,11},{9,10},{10,... | collective-permute-start | bytes 1572872 | tf_op jit(solution)/shard_map/ppermute | solution.py:497
  83.4 0.9 copy-done.7
  84.4 2.0 %fill_slots.2 = bf16[128,16,256]{2,1,0:T(8,128)(2,1)} custom-call(s32[64]{0:T(128)S(1)} %multiply_add_fusion.positions, bf16[2,64,16,128]{3,2,1,0:T(8,128)(2,1)S(1)} %copy-done.1, bf16[2,64,16,128]{3,2,1,0:T(8,128)(2,1)S(1)} %collective-permute-done.got_a, bf16[64,16,128]{2,1,0:T(8,128)(2,1)S(1)} %collective-permute-done.4.last_a, ...), custom_call_target="tpu_custom_call" | custom-call | flops 1 | bytes 1 | tf_op jit(solution)/shard_map/fill_slots/pallas_call | solution.py:316
  86.4 8.7 %all-to-all-start.2 = ((bf16[128,16,256]{2,1,0:T(8,128)(2,1)}), bf16[128,16,256]{2,1,0:T(8,128)(2,1)S(1)}, u32[]{:S(2)}, u32[]{:S(2)}) async-start(bf16[128,16,256]{2,1,0:T(8,128)(2,1)} %fill_slots.2), calls=%async_computation.2 | async-start | bytes 2097152 | tf_op jit(solution)/shard_map/all_to_all | solution.py:507
  95.1 1.4 copy-done.4
  96.5 4.1 %fill_slots.3 = bf16[128,32,256]{2,1,0:T(8,128)(2,1)} custom-call(s32[64]{0:T(128)S(1)} %multiply_add_fusion.positions, bf16[2,64,32,128]{3,2,1,0:T(8,128)(2,1)S(1)} %copy-done.4, bf16[2,64,32,128]{3,2,1,0:T(8,128)(2,1)} %collective-permute-done.1.got_a, bf16[64,32,128]{2,1,0:T(8,128)(2,1)} %collective-permute-done.6.last_a, ...), custom_call_target="tpu_custom_call" | custom-call | flops 60000002048 | bytes 1 | tf_op jit(solution)/shard_map/fill_slots/pallas_call | solution.py:316
  100.6 5.3 %merge_early.1 = (bf16[16,64,256]{2,1,0:T(8,128)(2,1)}, bf16[16,64,256]{2,1,0:T(8,128)(2,1)}, bf16[16,64,256]{2,1,0:T(8,128)(2,1)}, bf16[16,64,256]{2,1,0:T(8,128)(2,1)}) custom-call(s32[3]{0:T(128)S(1)} %copy-done.8, s32[128]{0:T(128)S(1)} %add.59.places, bf16[128,64,256]{2,1,0:T(8,128)(2,1)} %all-to-all-done.received, bf16[4,16,64,256]{3,2,1,0:T(8,128)(2,1)S(1)} %copy-done), custom_call_target="tpu_custom_call" | custom-call | flops 1 | bytes 1 | tf_op jit(solution)/shard_map/merge_early/pallas_call | solution.py:354
  105.9 1.7 %collective-permute-start.8 = (bf16[16,64,256]{2,1,0:T(8,128)(2,1)}, bf16[16,64,256]{2,1,0:T(8,128)(2,1)}, u32[]{:S(2)}, u32[]{:S(2)}) collective-permute-start(bf16[16,64,256]{2,1,0:T(8,128)(2,1)} %get-tuple-element.62), channel_id=1, source_target_pairs={{0,1},{1,0},{2,3},{3,2},{4,5},{5,4},{6,7},{7,6},{8,9},{9,8},{10,11... | collective-permute-start | bytes 1572872 | tf_op jit(solution)/shard_map/ppermute | solution.py:512
  107.6 0.9 collective-permute-start.9
  108.5 0.9 collective-permute-start.10
  109.4 2.0 %all-to-all-done.2.received = bf16[128,16,256]{2,1,0:T(8,128)(2,1)S(1)} async-done(((bf16[128,16,256]{2,1,0:T(8,128)(2,1)}), bf16[128,16,256]{2,1,0:T(8,128)(2,1)S(1)}, u32[]{:S(2)}, u32[]{:S(2)}) %all-to-all-start.2) | async-done | bytes 1048608 | tf_op jit(solution)/shard_map/all_to_all | solution.py:507
  111.4 7.9 %all-to-all-start.1 = ((bf16[128,32,256]{2,1,0:T(8,128)(2,1)}), bf16[128,32,256]{2,1,0:T(8,128)(2,1)S(1)}, u32[]{:S(2)}, u32[]{:S(2)}) async-start(bf16[128,32,256]{2,1,0:T(8,128)(2,1)} %fill_slots.3), calls=%async_computation.1 | async-start | bytes 4194304 | tf_op jit(solution)/shard_map/all_to_all | solution.py:515
  119.3 13.6 %collective-permute-done.9.rest_2_ = bf16[16,64,256]{2,1,0:T(8,128)(2,1)} collective-permute-done((bf16[16,64,256]{2,1,0:T(8,128)(2,1)}, bf16[16,64,256]{2,1,0:T(8,128)(2,1)}, u32[]{:S(2)}, u32[]{:S(2)}) %collective-permute-start.9) | collective-permute-done | bytes 524320 | tf_op jit(solution)/shard_map/ppermute | solution.py:512
  132.9 1.0 copy-done.9
  133.9 3.8 %first_sum.1.so_far = f32[16,64,256]{2,1,0:T(8,128)} custom-call(s32[128]{0:T(128)S(1)} %add.59.places, bf16[128,16,256]{2,1,0:T(8,128)(2,1)S(1)} %all-to-all-done.2.received, bf16[16,64,256]{2,1,0:T(8,128)(2,1)S(1)} %copy-done.9, bf16[16,64,256]{2,1,0:T(8,128)(2,1)} %collective-permute-done.8.rest_1_, bf16[16,64,256]{2,1,0:T(8,128)(2,1)} %collective-permute-done.9.rest_2_, ...), custom_call_target="tpu_custom_call" | custom-call | flops 60000002048 | bytes 1 | tf_op jit(solution)/shard_map/first_sum/pallas_call | solution.py:397
  137.7 8.5 %all-to-all-done.1.received = bf16[128,32,256]{2,1,0:T(8,128)(2,1)S(1)} async-done(((bf16[128,32,256]{2,1,0:T(8,128)(2,1)}), bf16[128,32,256]{2,1,0:T(8,128)(2,1)S(1)}, u32[]{:S(2)}, u32[]{:S(2)}) %all-to-all-start.1) | async-done | bytes 2097184 | tf_op jit(solution)/shard_map/all_to_all | solution.py:515
  146.2 3.2 %last_sum.1 = f32[16,64,256]{2,1,0:T(8,128)} custom-call(s32[128]{0:T(128)S(1)} %add.59.places, bf16[128,32,256]{2,1,0:T(8,128)(2,1)S(1)} %all-to-all-done.1.received, f32[16,64,256]{2,1,0:T(8,128)} %first_sum.1.so_far), custom_call_target="tpu_custom_call", output_to_operand_aliasing={{}: (2, {})} | custom-call | flops 1 | bytes 1 | tf_op jit(solution)/shard_map/last_sum/pallas_call | solution.py:423
  (40 shorter events, 1.3 us)
Async XLA Ops:
  24.2 23.5 %copy-start.1 = (bf16[2,64,16,128]{3,2,1,0:T(8,128)(2,1)S(1)}, bf16[2,64,16,128]{3,2,1,0:T(8,128)(2,1)}, u32[]{:S(2)}) copy-start(bf16[2,64,16,128]{3,2,1,0:T(8,128)(2,1)} %get-tuple-element.36.keep_a) | copy-start | bytes 1572868
  24.2 25.6 %copy-start.2 = (bf16[2,64,16,128]{3,2,1,0:T(8,128)(2,1)S(1)}, bf16[2,64,16,128]{3,2,1,0:T(8,128)(2,1)}, u32[]{:S(2)}) copy-start(bf16[2,64,16,128]{3,2,1,0:T(8,128)(2,1)} %get-tuple-element.40.keep_b) | copy-start | bytes 1572868
  24.2 54.4 %copy-start.3 = (bf16[2,64,32,128]{3,2,1,0:T(8,128)(2,1)S(1)}, bf16[2,64,32,128]{3,2,1,0:T(8,128)(2,1)}, u32[]{:S(2)}) copy-start(bf16[2,64,32,128]{3,2,1,0:T(8,128)(2,1)} %get-tuple-element.46.keep_a) | copy-start | bytes 3145732
  24.2 62.2 %all-to-all-start = ((bf16[128,64,256]{2,1,0:T(8,128)(2,1)}), bf16[128,64,256]{2,1,0:T(8,128)(2,1)}, u32[]{:S(2)}, u32[]{:S(2)}) async-start(bf16[128,64,256]{2,1,0:T(8,128)(2,1)} %get-tuple-element.35), calls=%async_computation | async-start | bytes 8388608 | tf_op jit(solution)/shard_map/all_to_all | solution.py:486
  34.1 13.6 %collective-permute-start = (bf16[2,64,16,128]{3,2,1,0:T(8,128)(2,1)}, bf16[2,64,16,128]{3,2,1,0:T(8,128)(2,1)S(1)}, u32[]{:S(2)}, u32[]{:S(2)}) collective-permute-start(bf16[2,64,16,128]{3,2,1,0:T(8,128)(2,1)} %get-tuple-element.37), channel_id=1, source_target_pairs={{0,1},{1,0},{2,3},{3,2},{4,5},{5,4},{6,7},{7,6},{8,9},{9,8},{10,11... | collective-permute-start | bytes 1572872 | tf_op jit(solution)/shard_map/ppermute | solution.py:490
  35.4 14.4 %collective-permute-start.3 = (bf16[2,64,16,128]{3,2,1,0:T(8,128)(2,1)}, bf16[2,64,16,128]{3,2,1,0:T(8,128)(2,1)S(1)}, u32[]{:S(2)}, u32[]{:S(2)}) collective-permute-start(bf16[2,64,16,128]{3,2,1,0:T(8,128)(2,1)} %get-tuple-element.41), channel_id=1, source_target_pairs={{0,3},{1,2},{2,1},{3,0},{4,7},{5,6},{6,5},{7,4},{8,11},{9,10},{10,... | collective-permute-start | bytes 1572872 | tf_op jit(solution)/shard_map/ppermute | solution.py:490
  37.2 41.4 %collective-permute-start.1 = (bf16[2,64,32,128]{3,2,1,0:T(8,128)(2,1)}, bf16[2,64,32,128]{3,2,1,0:T(8,128)(2,1)}, u32[]{:S(2)}, u32[]{:S(2)}) collective-permute-start(bf16[2,64,32,128]{3,2,1,0:T(8,128)(2,1)} %get-tuple-element.38), channel_id=1, source_target_pairs={{0,1},{1,0},{2,3},{3,2},{4,5},{5,4},{6,7},{7,6},{8,9},{9,8},{10,11... | collective-permute-start | bytes 3145736 | tf_op jit(solution)/shard_map/ppermute | solution.py:490
  37.5 41.1 %collective-permute-start.2 = (bf16[2,64,32,128]{3,2,1,0:T(8,128)(2,1)}, bf16[2,64,32,128]{3,2,1,0:T(8,128)(2,1)}, u32[]{:S(2)}, u32[]{:S(2)}) collective-permute-start(bf16[2,64,32,128]{3,2,1,0:T(8,128)(2,1)} %get-tuple-element.39), channel_id=1, source_target_pairs={{0,3},{1,2},{2,1},{3,0},{4,7},{5,6},{6,5},{7,4},{8,11},{9,10},{10,... | collective-permute-start | bytes 3145736 | tf_op jit(solution)/shard_map/ppermute | solution.py:490
  49.8 28.0 %collective-permute-start.4 = (bf16[64,16,128]{2,1,0:T(8,128)(2,1)S(1)}, bf16[64,16,128]{2,1,0:T(8,128)(2,1)S(1)}, u32[]{:S(2)}, u32[]{:S(2)}) collective-permute-start(bf16[64,16,128]{2,1,0:T(8,128)(2,1)S(1)} %fusion.2), channel_id=1, source_target_pairs={{0,3},{1,2},{2,1},{3,0},{4,7},{5,6},{6,5},{7,4},{8,11},{9,10},{10,... | collective-permute-start | bytes 786440 | tf_op jit(solution)/shard_map/ppermute | solution.py:497
  51.7 26.1 %collective-permute-start.5 = (bf16[64,16,128]{2,1,0:T(8,128)(2,1)S(1)}, bf16[64,16,128]{2,1,0:T(8,128)(2,1)S(1)}, u32[]{:S(2)}, u32[]{:S(2)}) collective-permute-start(bf16[64,16,128]{2,1,0:T(8,128)(2,1)S(1)} %fusion.3), channel_id=1, source_target_pairs={{0,1},{1,0},{2,3},{3,2},{4,5},{5,4},{6,7},{7,6},{8,9},{9,8},{10,11... | collective-permute-start | bytes 786440 | tf_op jit(solution)/shard_map/ppermute | solution.py:497
  77.9 0.7 copy-start.6
  81.2 13.9 %copy-start.5 = (bf16[2,64,32,128]{3,2,1,0:T(8,128)(2,1)S(1)}, bf16[2,64,32,128]{3,2,1,0:T(8,128)(2,1)}, u32[]{:S(2)}) copy-start(bf16[2,64,32,128]{3,2,1,0:T(8,128)(2,1)} %get-tuple-element.48.keep_b) | copy-start | bytes 3145732
  81.2 13.9 %collective-permute-start.6 = (bf16[64,32,128]{2,1,0:T(8,128)(2,1)}, bf16[64,32,128]{2,1,0:T(8,128)(2,1)}, u32[]{:S(2)}, u32[]{:S(2)}) collective-permute-start(bf16[64,32,128]{2,1,0:T(8,128)(2,1)} %get-tuple-element.50), channel_id=1, source_target_pairs={{0,3},{1,2},{2,1},{3,0},{4,7},{5,6},{6,5},{7,4},{8,11},{9,10},{10,... | collective-permute-start | bytes 1572872 | tf_op jit(solution)/shard_map/ppermute | solution.py:497
  83.0 12.1 %collective-permute-start.7 = (bf16[64,32,128]{2,1,0:T(8,128)(2,1)}, bf16[64,32,128]{2,1,0:T(8,128)(2,1)}, u32[]{:S(2)}, u32[]{:S(2)}) collective-permute-start(bf16[64,32,128]{2,1,0:T(8,128)(2,1)} %get-tuple-element.51), channel_id=1, source_target_pairs={{0,1},{1,0},{2,3},{3,2},{4,5},{5,4},{6,7},{7,6},{8,9},{9,8},{10,11... | collective-permute-start | bytes 1572872 | tf_op jit(solution)/shard_map/ppermute | solution.py:497
  83.4 1.0 copy-start.7
  86.4 14.2 %copy-start.8 = (s32[3]{0:T(128)S(1)}, s32[3]{0:T(128)}, u32[]{:S(2)}) copy-start(s32[3]{0:T(128)} %pad_add_fusion.device) | copy-start | bytes 40
  86.4 25.0 %all-to-all-start.2 = ((bf16[128,16,256]{2,1,0:T(8,128)(2,1)}), bf16[128,16,256]{2,1,0:T(8,128)(2,1)S(1)}, u32[]{:S(2)}, u32[]{:S(2)}) async-start(bf16[128,16,256]{2,1,0:T(8,128)(2,1)} %fill_slots.2), calls=%async_computation.2 | async-start | bytes 2097152 | tf_op jit(solution)/shard_map/all_to_all | solution.py:507
  95.1 5.5 %copy-start = (bf16[4,16,64,256]{3,2,1,0:T(8,128)(2,1)S(1)}, bf16[4,16,64,256]{3,2,1,0:T(8,128)(2,1)}, u32[]{:S(2)}) copy-start(bf16[4,16,64,256]{3,2,1,0:T(8,128)(2,1)} %get-tuple-element.55.own) | copy-start | bytes 6291460
  95.1 1.4 copy-start.4
  105.9 13.4 %collective-permute-start.8 = (bf16[16,64,256]{2,1,0:T(8,128)(2,1)}, bf16[16,64,256]{2,1,0:T(8,128)(2,1)}, u32[]{:S(2)}, u32[]{:S(2)}) collective-permute-start(bf16[16,64,256]{2,1,0:T(8,128)(2,1)} %get-tuple-element.62), channel_id=1, source_target_pairs={{0,1},{1,0},{2,3},{3,2},{4,5},{5,4},{6,7},{7,6},{8,9},{9,8},{10,11... | collective-permute-start | bytes 1572872 | tf_op jit(solution)/shard_map/ppermute | solution.py:512
  107.6 25.2 %collective-permute-start.9 = (bf16[16,64,256]{2,1,0:T(8,128)(2,1)}, bf16[16,64,256]{2,1,0:T(8,128)(2,1)}, u32[]{:S(2)}, u32[]{:S(2)}) collective-permute-start(bf16[16,64,256]{2,1,0:T(8,128)(2,1)} %get-tuple-element.63), channel_id=1, source_target_pairs={{0,3},{1,2},{2,1},{3,0},{4,7},{5,6},{6,5},{7,4},{8,11},{9,10},{10,... | collective-permute-start | bytes 1572872 | tf_op jit(solution)/shard_map/ppermute | solution.py:512
  108.5 24.4 %collective-permute-start.10 = (bf16[16,64,256]{2,1,0:T(8,128)(2,1)}, bf16[16,64,256]{2,1,0:T(8,128)(2,1)}, u32[]{:S(2)}, u32[]{:S(2)}) collective-permute-start(bf16[16,64,256]{2,1,0:T(8,128)(2,1)} %get-tuple-element.64), channel_id=1, source_target_pairs={{0,2},{1,3},{2,0},{3,1},{4,6},{5,7},{6,4},{7,5},{8,10},{9,11},{10,... | collective-permute-start | bytes 1572872 | tf_op jit(solution)/shard_map/ppermute | solution.py:512
  111.4 34.8 %all-to-all-start.1 = ((bf16[128,32,256]{2,1,0:T(8,128)(2,1)}), bf16[128,32,256]{2,1,0:T(8,128)(2,1)S(1)}, u32[]{:S(2)}, u32[]{:S(2)}) async-start(bf16[128,32,256]{2,1,0:T(8,128)(2,1)} %fill_slots.3), calls=%async_computation.1 | async-start | bytes 4194304 | tf_op jit(solution)/shard_map/all_to_all | solution.py:515
  132.9 1.0 copy-start.9

commit v5 on v4

--- a/solution.py
+++ b/solution.py
@@ -9,7 +9,8 @@
 
 LANES = 128
 EARLY_ROWS = 16
-CHUNKS = (16, 32)
+CHUNKS = (48,)
+FILL_FLOPS = 3 * 10**10
 SIDES = 2
 HEAD = 3
 AHEAD = 2
@@ -21,12 +22,8 @@
 IN_VMEM = pl.BlockSpec(memory_space=pltpu.VMEM)
 
 
-def small_cost():
-    return pl.CostEstimate(flops=1, bytes_accessed=1, transcendentals=0)
-
-
-def large_cost():
-    return pl.CostEstimate(flops=6 * 10**10, bytes_accessed=1, transcendentals=0)
+def cost(flops=1):
+    return pl.CostEstimate(flops=flops, bytes_accessed=1, transcendentals=0)
 
 
 def whole(shape):
@@ -39,13 +36,14 @@
 
 def products_kernel(
     capacity, device, block_left, block_right, channel_class, own_targets, psi_hbm, left_hbm,
-    right_hbm, own, slots_hbm, *rest
+    right_hbm, own_early, slots_hbm, *rest
 ):
-    chunk_outs = rest[: 4 * len(CHUNKS)]
+    own_late = rest[:4]
+    chunk_outs = rest[4 : 4 + 4 * len(CHUNKS)]
     (
         psi_ref, left_ref, right_ref, half_ref, acc_ref, stage_ref, seen_ref, first_ref, empty_ref,
         slot_ref, psi_sems, left_sems, right_sems, slot_sems,
-    ) = rest[4 * len(CHUNKS) :]
+    ) = rest[4 + 4 * len(CHUNKS) :]
     channels, left_count, _, _ = left_ref.shape
     right_count = right_ref.shape[1]
     classes = acc_ref.shape[1]
@@ -113,7 +111,9 @@
 
         def own_part(side, at, place, q):
             row = pl.multiple_of(q * quarter, quarter)
-            own[place, side] = acc_ref[at, 0, pl.ds(row, quarter)].astype(BF16)
+            own_early[place, side] = acc_ref[at, 0, pl.ds(row, EARLY_ROWS)].astype(BF16)
+            row = pl.multiple_of(row + EARLY_ROWS, EARLY_ROWS)
+            own_late[place][side] = acc_ref[at, 0, pl.ds(row, quarter - EARLY_ROWS)].astype(BF16)
 
         def chunk_part(side, at, h, j, start, rows, s):
             keep, send = chunk_outs[4 * j + 2 * s : 4 * j + 2 * s + 2]
@@ -243,13 +243,13 @@
     hops = classes - 1
     head = SIDES * HEAD
     out_shape = [
-        pltpu.HBM((4, blocks, quarter, block), BF16),
+        pltpu.HBM((4, blocks, EARLY_ROWS, block), BF16),
         pltpu.HBM((owners * capacity, early, block), BF16),
-    ]
+    ] + [pltpu.HBM((blocks, quarter - EARLY_ROWS, block), BF16)] * 4
     out_specs = [
-        pl.BlockSpec((4, SIDES, quarter, block), lambda k, *_: (0, k, 0, 0)),
+        pl.BlockSpec((4, SIDES, EARLY_ROWS, block), lambda k, *_: (0, k, 0, 0)),
         pl.BlockSpec(memory_space=pltpu.HBM),
-    ]
+    ] + [pl.BlockSpec((SIDES, quarter - EARLY_ROWS, block), lambda k, *_: (k, 0, 0))] * 4
     for rows in CHUNKS:
         out_shape += [pltpu.HBM((2, blocks * hops, rows, LANES), BF16)] * 4
         block_shape = (2, SIDES * hops, rows, LANES)
@@ -311,15 +311,16 @@
     lax.fori_loop(0, stage.shape[0], finish, 0, unroll=4)
 
 
-def fill_slots(positions, slot_count, parts, final):
+def fill_slots(positions, slot_count, parts):
     _, count, rows, _ = parts[0].shape
+    pair = whole((1, count, rows, LANES))
     return pl.pallas_call(
         slots_kernel,
         out_shape=pltpu.HBM((slot_count, rows, 2 * LANES), BF16),
         grid_spec=pltpu.PrefetchScalarGridSpec(
             num_scalar_prefetch=1,
             grid=(1,),
-            in_specs=[IN_VMEM] * 6,
+            in_specs=[pair, IN_VMEM, IN_VMEM, pair, IN_VMEM, IN_VMEM],
             out_specs=pl.BlockSpec(memory_space=pltpu.HBM),
             scratch_shapes=[
                 pltpu.VMEM((count, rows, 2 * LANES), BF16),
@@ -327,42 +328,37 @@
             ],
         ),
         compiler_params=pltpu.CompilerParams(vmem_limit_bytes=SMALL_VMEM),
-        cost_estimate=large_cost() if final else small_cost(),
+        cost_estimate=cost(FILL_FLOPS),
         name="fill_slots",
     )(positions, *parts)
 
 
 def merge_kernel(device, places, received, own, *rest):
     *outs, acc = rest
-    _, blocks, quarter, _ = own.shape
+    blocks = own.shape[1]
     at = [pl.multiple_of(q * EARLY_ROWS, EARLY_ROWS) for q in relative_quarters(device[0])]
     for p in range(4):
-        acc[:blocks, pl.ds(at[p], EARLY_ROWS)] = own[p, :, :EARLY_ROWS].astype(F32)
-
-    def add(p, _):
-        acc[places[p]] += received[p].astype(F32)
-        return 0
-
-    lax.fori_loop(0, received.shape[0], add, 0, unroll=4)
+        acc[:blocks, pl.ds(at[p], EARLY_ROWS)] = own[p].astype(F32)
+    add_slots(acc, places, received)
     for p in range(4):
-        outs[p][:, :EARLY_ROWS] = acc[:blocks, pl.ds(at[p], EARLY_ROWS)].astype(BF16)
-        outs[p][:, EARLY_ROWS:] = own[p, :, EARLY_ROWS:]
+        outs[p][...] = acc[:blocks, pl.ds(at[p], EARLY_ROWS)].astype(BF16)
 
 
 def merge_early(device, places, received, own):
-    _, blocks, quarter, width = own.shape
+    _, blocks, rows, width = own.shape
+    shape = (blocks, rows, width)
     return pl.pallas_call(
         merge_kernel,
-        out_shape=[pltpu.HBM((blocks, quarter, width), BF16)] * 4,
+        out_shape=[pltpu.HBM(shape, BF16)] * 4,
         grid_spec=pltpu.PrefetchScalarGridSpec(
             num_scalar_prefetch=2,
             grid=(1,),
-            in_specs=[IN_VMEM, IN_VMEM],
-            out_specs=[whole((blocks, quarter, width))] * 4,
-            scratch_shapes=[pltpu.VMEM((blocks + 1, 4 * EARLY_ROWS, width), F32)],
+            in_specs=[IN_VMEM, whole(own.shape)],
+            out_specs=[whole(shape)] * 4,
+            scratch_shapes=[pltpu.VMEM((blocks + 1, 4 * rows, width), F32)],
         ),
         compiler_params=pltpu.CompilerParams(vmem_limit_bytes=SMALL_VMEM),
-        cost_estimate=small_cost(),
+        cost_estimate=cost(),
         name="merge_early",
     )(device, places, received, own)
 
@@ -375,49 +371,48 @@
     lax.fori_loop(0, received.shape[0], add, 0, unroll=4)
 
 
-def first_sum(places, received, mine, others, start):
-    blocks, quarter, width = mine.shape
-    rows = received.shape[1]
-
-    def kernel(places, received, *rest):
-        *parts, result, acc = rest
-
-        def total(at):
-            value = parts[0][:, at].astype(F32)
-            for part in parts[1:]:
-                value = value + part[:, at].astype(F32)
-            return value
-
-        acc[:blocks] = total(slice(start, start + rows))
-        add_slots(acc, places, received)
-        result[:, :start] = total(slice(0, start))
-        result[:, start : start + rows] = acc[:blocks]
-        result[:, start + rows :] = total(slice(start + rows, quarter))
+def first_sum(early, late):
+    blocks, early_rows, width = early[0].shape
+    late_rows = late[0].shape[1]
+    shape = (blocks, early_rows + late_rows, width)
+
+    def total(parts):
+        value = parts[0][...].astype(F32)
+        for part in parts[1:]:
+            value = value + part[...].astype(F32)
+        return value
+
+    def kernel(*refs):
+        *parts, result = refs
+        result[:, :early_rows] = total(parts[:4])
+        result[:, early_rows:] = total(parts[4:])
 
     return pl.pallas_call(
         kernel,
-        out_shape=pltpu.HBM(mine.shape, F32),
-        grid_spec=pltpu.PrefetchScalarGridSpec(
-            num_scalar_prefetch=1,
-            grid=(1,),
-            in_specs=[IN_VMEM] * (2 + len(others)),
-            out_specs=whole(mine.shape),
-            scratch_shapes=[pltpu.VMEM((blocks + 1, rows, width), F32)],
-        ),
+        out_shape=pltpu.HBM(shape, F32),
+        grid=(1,),
+        in_specs=[IN_VMEM] * 8,
+        out_specs=whole(shape),
         compiler_params=pltpu.CompilerParams(vmem_limit_bytes=SMALL_VMEM),
-        cost_estimate=large_cost(),
+        cost_estimate=cost(),
         name="first_sum",
-    )(places, received, mine, *others)
-
-
-def last_sum(places, received, so_far, start):
+    )(*early, *late)
+
+
+def last_sum(places, received, so_far):
     blocks, _, width = so_far.shape
-    rows = received.shape[1]
-    part = pl.BlockSpec((blocks, rows, width), lambda i, *_: (0, start // rows, 0))
+    rows = EARLY_ROWS
+    part = pl.BlockSpec((blocks, rows, width), lambda i, *_: (0, i + 1, 0))
 
     def kernel(places, received, so_far, result, acc):
+        at = pl.multiple_of(pl.program_id(0) * rows, rows)
         acc[:blocks] = so_far[...]
-        add_slots(acc, places, received)
+
+        def add(p, _):
+            acc[places[p]] += received[p, pl.ds(at, rows)].astype(F32)
+            return 0
+
+        lax.fori_loop(0, received.shape[0], add, 0, unroll=8)
         result[...] = acc[:blocks]
 
     return pl.pallas_call(
@@ -425,14 +420,14 @@
         out_shape=pltpu.HBM(so_far.shape, F32),
         grid_spec=pltpu.PrefetchScalarGridSpec(
             num_scalar_prefetch=1,
-            grid=(1,),
+            grid=(received.shape[1] // rows,),
             in_specs=[IN_VMEM, part],
             out_specs=part,
             scratch_shapes=[pltpu.VMEM((blocks + 1, rows, width), F32)],
         ),
         input_output_aliases={2: 0},
         compiler_params=pltpu.CompilerParams(vmem_limit_bytes=SMALL_VMEM),
-        cost_estimate=small_cost(),
+        cost_estimate=cost(),
         name="last_sum",
     )(places, received, so_far)
 
@@ -456,7 +451,7 @@
     device = jnp.stack([lax.axis_index(axis) for axis in ("mpo", "lsec", "rsec")]).astype(jnp.int32)
     targets = hop_target.reshape(owners, item_count)
     own_targets = lax.dynamic_index_in_dim(targets, me, 0, False)
-    own, early_slots, *parts = products(
+    own_early, early_slots, *parts = products(
         (device, block_left, block_right, channel_class, own_targets),
         owners,
         capacity,
@@ -466,6 +461,7 @@
         hop_count + 1,
     )
 
+    own_late, parts = parts[:4], parts[4:]
     destined, slot = item_places(own_targets, block_count)
     position = destined * capacity + slot
     destined_all, slot_all = item_places(targets, block_count)
@@ -484,37 +480,25 @@
         return (keep[1].astype(F32) + got[1].astype(F32)).astype(BF16)
 
     early = lax.all_to_all(early_slots, ("lsec", "rsec"), 0, 0, tiled=True)
-    got, last = [], []
-    for j in range(len(CHUNKS)):
-        keep_a, send_a, keep_b, send_b = parts[4 * j : 4 * j + 4]
-        got.append((lax.ppermute(send_a, "mpo", beside), lax.ppermute(send_b, "mpo", mirror)))
-    for j in range(len(CHUNKS)):
-        keep_a, _, keep_b, _ = parts[4 * j : 4 * j + 4]
-        got_a, got_b = got[j]
-        if j > 0:
-            got_a, got_b, *last[j - 1] = lax.optimization_barrier((got_a, got_b, *last[j - 1]))
-        then_a, then_b = lax.optimization_barrier((second(keep_a, got_a), second(keep_b, got_b)))
-        last.append([lax.ppermute(then_a, "mpo", mirror), lax.ppermute(then_b, "mpo", beside)])
-
-    def send(j, last_a, last_b):
-        keep_a, _, keep_b, _ = parts[4 * j : 4 * j + 4]
-        group = (keep_a, got[j][0], last_a, keep_b, got[j][1], last_b)
-        return fill_slots(position, slot_count, group, j + 1 == len(CHUNKS))
-
-    last_a, last_b, then_a, then_b = lax.optimization_barrier((*last[0], then_a, then_b))
-    slots = send(0, last_a, last_b)
-    early, slots = lax.optimization_barrier((early, slots))
+    keep_a, send_a, keep_b, send_b = parts
+    got_a = lax.ppermute(send_a, "mpo", beside)
+    got_b = lax.ppermute(send_b, "mpo", mirror)
+    last_a = lax.ppermute(second(keep_a, got_a), "mpo", mirror)
+    last_b = lax.ppermute(second(keep_b, got_b), "mpo", beside)
+    slots = fill_slots(position, slot_count, (keep_a, got_a, last_a, keep_b, got_b, last_b))
     received = lax.all_to_all(slots, ("lsec", "rsec"), 0, 0, tiled=True)
-    out_mine, *out_others = merge_early(device, places, early, own)
-    slots = send(1, *last[1])
-    out_others, slots = lax.optimization_barrier((out_others, slots))
-    others = [
-        lax.ppermute(part, "mpo", pairs)
-        for part, pairs in zip(out_others, (beside, mirror, across))
-    ]
-    received_last = lax.all_to_all(slots, ("lsec", "rsec"), 0, 0, tiled=True)
-    base = first_sum(places, received, out_mine, others, EARLY_ROWS)
-    return last_sum(places, received_last, base, EARLY_ROWS + CHUNKS[0])
+    early, slots, *own_late = lax.optimization_barrier((early, slots, *own_late))
+
+    def over_groups(parts):
+        mine, *theirs = parts
+        return [mine] + [
+            lax.ppermute(part, "mpo", pairs)
+            for part, pairs in zip(theirs, (beside, mirror, across))
+        ]
+
+    late = over_groups(own_late)
+    early = over_groups(merge_early(device, places, early, own_early))
+    return last_sum(places, received, first_sum(early, late))
 
 
 def solution(mesh):

time: 150 us -> 141 us (0.940)
  starting transfers between devices: 37.6 us -> 30.6 us
  Pallas kernels: 40.3 us -> 37.1 us
  waiting for transfers between devices: 60.7 us -> 63.4 us
    all_to_all x1 -> x0, waiting for transfers between devices: 8.54 us -> none  [shards(): received_last = lax.all_to_all(slots, ('lsec', 'rsec'), 0, 0, tiled=True)]
    all_to_all x1 -> x0, starting transfers between devices: 7.87 us -> none  [shards(): received_last = lax.all_to_all(slots, ('lsec', 'rsec'), 0, 0, tiled=True)]
    ppermute x11 -> x10, waiting for transfers between devices: 50.2 us -> 55 us  [the longest x1 22.6 us: shards(): got_a = lax.ppermute(send_a, 'mpo', beside)]
    all_to_all x1, waiting for transfers between devices: 1.98 us -> 6.35 us  [shards(): received = lax.all_to_all(slots, ('lsec', 'rsec'), 0, 0, tiled=True)]
    pallas_call x2 -> x1, Pallas kernels: 6.1 us -> 3.83 us  [fill_slots(): pl.pallas_call(slots_kernel, out_shape=pltpu.HBM((slot_count, rows, 2 * L...]
    unnamed x21 -> x13, local copies, waits for them, and re-layouts: 4.92 us -> 2.79 us
    pallas_call x2, Pallas kernels: 9.05 us -> 6.97 us  [the longest x1 4.64 us: merge_early(): pl.pallas_call(merge_kernel, out_shape=[pltpu.HBM(shape, BF16)] * 4, grid...]
    all_to_all x1, waiting for transfers between devices: 0.01 us -> 2.03 us  [shards(): early = lax.all_to_all(early_slots, ('lsec', 'rsec'), 0, 0, tiled=True)]
  transfers between devices with their start and end apart: 14 -> 12, of which waited for: 6 -> 8; matrix products, arithmetic and copies ran while one was open for 3% -> 3% of each run, Pallas kernels for 10% -> 8%
where the time goes in v5:
time: 141 us; the launch traced here: 140 us
  waiting for transfers between devices  63.4 us (45%)
  Pallas kernels  37.1 us (26%)
  starting transfers between devices  30.6 us (22%)
  local copies, waits for them, and re-layouts  4.44 us (3%)
  other arithmetic  4.05 us (3%)
    ppermute x1, waiting for transfers between devices, shards(): got_a = lax.ppermute(send_a, 'mpo', beside)  22.6 us
    pallas_call x1, Pallas kernels, products(): pl.pallas_call(functools.partial(products_kernel, capacity), out_shape=ou...  21.8 us
    ppermute x6, waiting for transfers between devices, over_groups(): lax.ppermute(part, 'mpo', pairs)  15.3 us
    ppermute x1, waiting for transfers between devices, shards(): last_a = lax.ppermute(second(keep_a, got_a), 'mpo', mirror)  14.7 us
    all_to_all x1, starting transfers between devices, shards(): early = lax.all_to_all(early_slots, ('lsec', 'rsec'), 0, 0, tiled=True)  9.53 us
    all_to_all x1, starting transfers between devices, shards(): received = lax.all_to_all(slots, ('lsec', 'rsec'), 0, 0, tiled=True)  8.61 us
    all_to_all x1, waiting for transfers between devices, shards(): received = lax.all_to_all(slots, ('lsec', 'rsec'), 0, 0, tiled=True)  6.35 us
    ppermute x6, starting transfers between devices, over_groups(): lax.ppermute(part, 'mpo', pairs)  5.4 us
  transfers between devices with their start and end apart: 12, of which 8 were waited for; matrix products, arithmetic and copies ran while one was open for 3% of the time, Pallas kernels for 8%

profile of v5, /device:TPU:1, one launch (start us, length us, event | category | flops | bytes accessed | tf_op | source)
XLA Modules:
  0.0 139.8 jit_solution(16663443520568363103)
XLA Ops:
  0.0 0.8 copy.10
  1.0 0.6 and_select_fusion.1
  1.6 0.6 pad_add_fusion.device
  2.2 21.8 %products.1 = (bf16[4,16,16,256]{3,2,1,0:T(8,128)(2,1)}, bf16[128,64,256]{2,1,0:T(8,128)(2,1)}, bf16[16,48,256]{2,1,0:T(8,128)(2,1)}, bf16[16,48,256]{2,1,0:T(8,...) custom-call(s32[3]{0:T(128)} %pad_add_fusion.device, ...), custom_call_target="tpu_custom_call" | custom-call | flops 10737418240 | bytes 23068672 | tf_op jit(solution)/shard_map/products/pallas_call | solution.py:257
  24.0 2.1 %collective-permute-start = (bf16[2,64,48,128]{3,2,1,0:T(8,128)(2,1)}, bf16[2,64,48,128]{3,2,1,0:T(8,128)(2,1)S(1)}, u32[]{:S(2)}, u32[]{:S(2)}) collective-permute-start(bf16[2,64,48,128]{3,2,1,0:T(8,128)(2,1)} %get-tuple-element.25), channel_id=1, source_target_pairs={{0,1},{1,0},{2,3},{3,2},{4,5},{5,4},{6,7},{7,6},{8,9},{9,8},{10,11... | collective-permute-start | bytes 4718600 | tf_op jit(solution)/shard_map/ppermute | solution.py:484
  26.1 1.8 %collective-permute-start.2 = (bf16[2,64,48,128]{3,2,1,0:T(8,128)(2,1)}, bf16[2,64,48,128]{3,2,1,0:T(8,128)(2,1)}, u32[]{:S(2)}, u32[]{:S(2)}) collective-permute-start(bf16[2,64,48,128]{3,2,1,0:T(8,128)(2,1)} %get-tuple-element.27), channel_id=1, source_target_pairs={{0,3},{1,2},{2,1},{3,0},{4,7},{5,6},{6,5},{7,4},{8,11},{9,10},{10,... | collective-permute-start | bytes 4718600 | tf_op jit(solution)/shard_map/ppermute | solution.py:485
  27.9 9.5 %all-to-all-start.1 = ((bf16[128,64,256]{2,1,0:T(8,128)(2,1)}), bf16[128,64,256]{2,1,0:T(8,128)(2,1)}, u32[]{:S(2)}, u32[]{:S(2)}) async-start(bf16[128,64,256]{2,1,0:T(8,128)(2,1)} %get-tuple-element.28), calls=%async_computation.1 | async-start | bytes 8388608 | tf_op jit(solution)/shard_map/all_to_all | solution.py:482
  37.5 22.6 %collective-permute-done.got_a = bf16[2,64,48,128]{3,2,1,0:T(8,128)(2,1)S(1)} collective-permute-done((bf16[2,64,48,128]{3,2,1,0:T(8,128)(2,1)}, bf16[2,64,48,128]{3,2,1,0:T(8,128)(2,1)S(1)}, u32[]{:S(2)}, u32[]{:S(2)}) %collective-permute-start) | collective-permute-done | bytes 1572896 | tf_op jit(solution)/shard_map/ppermute | solution.py:484
  60.0 0.2 fusion
  60.2 3.0 %collective-permute-start.1 = (bf16[64,48,128]{2,1,0:T(8,128)(2,1)S(1)}, bf16[64,48,128]{2,1,0:T(8,128)(2,1)S(1)}, u32[]{:S(2)}, u32[]{:S(2)}) collective-permute-start(bf16[64,48,128]{2,1,0:T(8,128)(2,1)S(1)} %fusion), channel_id=1, source_target_pairs={{0,3},{1,2},{2,1},{3,0},{4,7},{5,6},{6,5},{7,4},{8,11},{9,10},{10,... | collective-permute-start | bytes 2359304 | tf_op jit(solution)/shard_map/ppermute | solution.py:486
  63.3 1.3 fusion.1
  64.9 14.7 %collective-permute-done.1.last_a = bf16[64,48,128]{2,1,0:T(8,128)(2,1)S(1)} collective-permute-done((bf16[64,48,128]{2,1,0:T(8,128)(2,1)S(1)}, bf16[64,48,128]{2,1,0:T(8,128)(2,1)S(1)}, u32[]{:S(2)}, u32[]{:S(2)}) %collective-permute-start.1) | collective-permute-done | bytes 786464 | tf_op jit(solution)/shard_map/ppermute | solution.py:486
  79.6 2.5 %collective-permute-done.3.last_b = bf16[64,48,128]{2,1,0:T(8,128)(2,1)S(1)} collective-permute-done((bf16[64,48,128]{2,1,0:T(8,128)(2,1)S(1)}, bf16[64,48,128]{2,1,0:T(8,128)(2,1)S(1)}, u32[]{:S(2)}, u32[]{:S(2)}) %collective-permute-start.3) | collective-permute-done | bytes 786464 | tf_op jit(solution)/shard_map/ppermute | solution.py:487
  82.1 3.8 %fill_slots.1 = bf16[128,48,256]{2,1,0:T(8,128)(2,1)} custom-call(s32[64]{0:T(128)S(1)} %multiply_add_fusion.positions, bf16[2,64,48,128]{3,2,1,0:T(8,128)(2,1)S(1)} %copy-done.2, bf16[2,64,48,128]{3,2,1,0:T(8,128)(2,1)S(1)} %collective-permute-done.got_a, bf16[64,48,128]{2,1,0:T(8,128)(2,1)S(1)} %collective-permute-done.1.last_a, ...), custom_call_target="tpu_custom_call" | custom-call | flops 30000001024 | bytes 1 | tf_op jit(solution)/shard_map/fill_slots/pallas_call | solution.py:317
  86.0 2.0 %all-to-all-done.1.received = bf16[128,64,256]{2,1,0:T(8,128)(2,1)} async-done(((bf16[128,64,256]{2,1,0:T(8,128)(2,1)}), bf16[128,64,256]{2,1,0:T(8,128)(2,1)}, u32[]{:S(2)}, u32[]{:S(2)}) %all-to-all-start.1) | async-done | bytes 4194336 | tf_op jit(solution)/shard_map/all_to_all | solution.py:482
  88.0 8.6 %all-to-all-start = ((bf16[128,48,256]{2,1,0:T(8,128)(2,1)}), bf16[128,48,256]{2,1,0:T(8,128)(2,1)S(1)}, u32[]{:S(2)}, u32[]{:S(2)}) async-start(bf16[128,48,256]{2,1,0:T(8,128)(2,1)} %fill_slots.1), calls=%async_computation | async-start | bytes 6291456 | tf_op jit(solution)/shard_map/all_to_all | solution.py:489
  96.7 0.9 convert_reduce_fusion
  97.8 1.2 collective-permute-start.8
  99.0 2.0 %collective-permute-start.9 = (bf16[16,48,256]{2,1,0:T(8,128)(2,1)}, bf16[16,48,256]{2,1,0:T(8,128)(2,1)}, u32[]{:S(2)}, u32[]{:S(2)}) collective-permute-start(bf16[16,48,256]{2,1,0:T(8,128)(2,1)} %get-tuple-element.42), channel_id=1, source_target_pairs={{0,2},{1,3},{2,0},{3,1},{4,6},{5,7},{6,4},{7,5},{8,10},{9,11},{10,... | collective-permute-start | bytes 1179656 | tf_op jit(solution)/shard_map/ppermute | solution.py:495
  101.1 0.7 copy.11
  101.8 0.8 add.51.places
  102.6 1.0 copy-done
  103.6 4.6 %merge_early.1 = (bf16[16,16,256]{2,1,0:T(8,128)(2,1)}, bf16[16,16,256]{2,1,0:T(8,128)(2,1)}, bf16[16,16,256]{2,1,0:T(8,128)(2,1)}, bf16[16,16,256]{2,1,0:T(8,128)(2,1)}) custom-call(s32[3]{0:T(128)S(1)} %copy-done.5, s32[128]{0:T(128)S(1)} %add.51.places, bf16[128,64,256]{2,1,0:T(8,128)(2,1)} %all-to-all-done.1.received, bf16[4,16,16,256]{3,2,1,0:T(8,128)(2,1)S(1)} %copy-done), custom_call_target="tpu_custom_call" | custom-call | flops 1 | bytes 1 | tf_op jit(solution)/shard_map/merge_early/pallas_call | solution.py:350
  108.4 1.1 collective-permute-start.5
  109.5 10.3 %collective-permute-done.4.refs_1_ = bf16[16,16,256]{2,1,0:T(8,128)(2,1)S(1)} collective-permute-done((bf16[16,16,256]{2,1,0:T(8,128)(2,1)}, bf16[16,16,256]{2,1,0:T(8,128)(2,1)S(1)}, u32[]{:S(2)}, u32[]{:S(2)}) %collective-permute-start.4) | collective-permute-done | bytes 131104 | tf_op jit(solution)/shard_map/ppermute | solution.py:495
  119.8 0.9 collective-permute-start.6
  120.6 0.8 collective-permute-done.5.refs_2_
  121.4 4.2 %collective-permute-done.6.refs_3_ = bf16[16,16,256]{2,1,0:T(8,128)(2,1)S(1)} collective-permute-done((bf16[16,16,256]{2,1,0:T(8,128)(2,1)}, bf16[16,16,256]{2,1,0:T(8,128)(2,1)S(1)}, u32[]{:S(2)}, u32[]{:S(2)}) %collective-permute-start.6) | collective-permute-done | bytes 131104 | tf_op jit(solution)/shard_map/ppermute | solution.py:495
  125.7 0.9 copy-done.4
  126.6 2.3 %first_sum.1.so_far = f32[16,64,256]{2,1,0:T(8,128)} custom-call(bf16[16,16,256]{2,1,0:T(8,128)(2,1)S(1)} %copy-done.4, bf16[16,16,256]{2,1,0:T(8,128)(2,1)S(1)} %collective-permute-done.4.refs_1_, bf16[16,16,256]{2,1,0:T(8,128)(2,1)S(1)} %collective-permute-done.5.refs_2_, bf16[16,16,256]{2,1,0:T(8,128)(2,1)S(1)} %collective-permute-done.6.refs_3_, ...), custom_call_target="tpu_custom_call" | custom-call | flops 1 | bytes 1 | tf_op jit(solution)/shard_map/first_sum/pallas_call | solution.py:390
  128.9 6.4 %all-to-all-done.received = bf16[128,48,256]{2,1,0:T(8,128)(2,1)S(1)} async-done(((bf16[128,48,256]{2,1,0:T(8,128)(2,1)}), bf16[128,48,256]{2,1,0:T(8,128)(2,1)S(1)}, u32[]{:S(2)}, u32[]{:S(2)}) %all-to-all-start) | async-done | bytes 3145760 | tf_op jit(solution)/shard_map/all_to_all | solution.py:489
  135.2 4.5 %last_sum.1 = f32[16,64,256]{2,1,0:T(8,128)} custom-call(s32[128]{0:T(128)S(1)} %add.51.places, bf16[128,48,256]{2,1,0:T(8,128)(2,1)S(1)} %all-to-all-done.received, f32[16,64,256]{2,1,0:T(8,128)} %first_sum.1.so_far), custom_call_target="tpu_custom_call", output_to_operand_aliasing={{}: (2, {})} | custom-call | flops 1 | bytes 1 | tf_op jit(solution)/shard_map/last_sum/pallas_call | solution.py:418
  (26 shorter events, 0.8 us)
Async XLA Ops:
  24.0 36.1 %collective-permute-start = (bf16[2,64,48,128]{3,2,1,0:T(8,128)(2,1)}, bf16[2,64,48,128]{3,2,1,0:T(8,128)(2,1)S(1)}, u32[]{:S(2)}, u32[]{:S(2)}) collective-permute-start(bf16[2,64,48,128]{3,2,1,0:T(8,128)(2,1)} %get-tuple-element.25), channel_id=1, source_target_pairs={{0,1},{1,0},{2,3},{3,2},{4,5},{5,4},{6,7},{7,6},{8,9},{9,8},{10,11... | collective-permute-start | bytes 4718600 | tf_op jit(solution)/shard_map/ppermute | solution.py:484
  26.1 37.2 %collective-permute-start.2 = (bf16[2,64,48,128]{3,2,1,0:T(8,128)(2,1)}, bf16[2,64,48,128]{3,2,1,0:T(8,128)(2,1)}, u32[]{:S(2)}, u32[]{:S(2)}) collective-permute-start(bf16[2,64,48,128]{3,2,1,0:T(8,128)(2,1)} %get-tuple-element.27), channel_id=1, source_target_pairs={{0,3},{1,2},{2,1},{3,0},{4,7},{5,6},{6,5},{7,4},{8,11},{9,10},{10,... | collective-permute-start | bytes 4718600 | tf_op jit(solution)/shard_map/ppermute | solution.py:485
  27.9 32.1 %copy-start.2 = (bf16[2,64,48,128]{3,2,1,0:T(8,128)(2,1)S(1)}, bf16[2,64,48,128]{3,2,1,0:T(8,128)(2,1)}, u32[]{:S(2)}) copy-start(bf16[2,64,48,128]{3,2,1,0:T(8,128)(2,1)} %get-tuple-element.24.keep_a) | copy-start | bytes 4718596
  27.9 60.1 %all-to-all-start.1 = ((bf16[128,64,256]{2,1,0:T(8,128)(2,1)}), bf16[128,64,256]{2,1,0:T(8,128)(2,1)}, u32[]{:S(2)}, u32[]{:S(2)}) async-start(bf16[128,64,256]{2,1,0:T(8,128)(2,1)} %get-tuple-element.28), calls=%async_computation.1 | async-start | bytes 8388608 | tf_op jit(solution)/shard_map/all_to_all | solution.py:482
  37.5 25.8 %copy-start.3 = (bf16[2,64,48,128]{3,2,1,0:T(8,128)(2,1)S(1)}, bf16[2,64,48,128]{3,2,1,0:T(8,128)(2,1)}, u32[]{:S(2)}) copy-start(bf16[2,64,48,128]{3,2,1,0:T(8,128)(2,1)} %get-tuple-element.26.keep_b) | copy-start | bytes 4718596
  60.2 19.3 %collective-permute-start.1 = (bf16[64,48,128]{2,1,0:T(8,128)(2,1)S(1)}, bf16[64,48,128]{2,1,0:T(8,128)(2,1)S(1)}, u32[]{:S(2)}, u32[]{:S(2)}) collective-permute-start(bf16[64,48,128]{2,1,0:T(8,128)(2,1)S(1)} %fusion), channel_id=1, source_target_pairs={{0,3},{1,2},{2,1},{3,0},{4,7},{5,6},{6,5},{7,4},{8,11},{9,10},{10,... | collective-permute-start | bytes 2359304 | tf_op jit(solution)/shard_map/ppermute | solution.py:486
  64.6 17.5 %collective-permute-start.3 = (bf16[64,48,128]{2,1,0:T(8,128)(2,1)S(1)}, bf16[64,48,128]{2,1,0:T(8,128)(2,1)S(1)}, u32[]{:S(2)}, u32[]{:S(2)}) collective-permute-start(bf16[64,48,128]{2,1,0:T(8,128)(2,1)S(1)} %fusion.1), channel_id=1, source_target_pairs={{0,1},{1,0},{2,3},{3,2},{4,5},{5,4},{6,7},{7,6},{8,9},{9,8},{10,11... | collective-permute-start | bytes 2359304 | tf_op jit(solution)/shard_map/ppermute | solution.py:487
  85.9 16.6 %copy-start.5 = (s32[3]{0:T(128)S(1)}, s32[3]{0:T(128)}, u32[]{:S(2)}) copy-start(s32[3]{0:T(128)} %pad_add_fusion.device) | copy-start | bytes 40
  88.0 47.2 %all-to-all-start = ((bf16[128,48,256]{2,1,0:T(8,128)(2,1)}), bf16[128,48,256]{2,1,0:T(8,128)(2,1)S(1)}, u32[]{:S(2)}, u32[]{:S(2)}) async-start(bf16[128,48,256]{2,1,0:T(8,128)(2,1)} %fill_slots.1), calls=%async_computation | async-start | bytes 6291456 | tf_op jit(solution)/shard_map/all_to_all | solution.py:489
  97.7 27.9 %collective-permute-start.7 = (bf16[16,48,256]{2,1,0:T(8,128)(2,1)}, bf16[16,48,256]{2,1,0:T(8,128)(2,1)S(1)}, u32[]{:S(2)}, u32[]{:S(2)}) collective-permute-start(bf16[16,48,256]{2,1,0:T(8,128)(2,1)} %get-tuple-element.40), channel_id=1, source_target_pairs={{0,1},{1,0},{2,3},{3,2},{4,5},{5,4},{6,7},{7,6},{8,9},{9,8},{10,11... | collective-permute-start | bytes 1179656 | tf_op jit(solution)/shard_map/ppermute | solution.py:495
  97.8 27.8 %collective-permute-start.8 = (bf16[16,48,256]{2,1,0:T(8,128)(2,1)}, bf16[16,48,256]{2,1,0:T(8,128)(2,1)}, u32[]{:S(2)}, u32[]{:S(2)}) collective-permute-start(bf16[16,48,256]{2,1,0:T(8,128)(2,1)} %get-tuple-element.41), channel_id=1, source_target_pairs={{0,3},{1,2},{2,1},{3,0},{4,7},{5,6},{6,5},{7,4},{8,11},{9,10},{10,... | collective-permute-start | bytes 1179656 | tf_op jit(solution)/shard_map/ppermute | solution.py:495
  99.0 26.6 %collective-permute-start.9 = (bf16[16,48,256]{2,1,0:T(8,128)(2,1)}, bf16[16,48,256]{2,1,0:T(8,128)(2,1)}, u32[]{:S(2)}, u32[]{:S(2)}) collective-permute-start(bf16[16,48,256]{2,1,0:T(8,128)(2,1)} %get-tuple-element.42), channel_id=1, source_target_pairs={{0,2},{1,3},{2,0},{3,1},{4,6},{5,7},{6,4},{7,5},{8,10},{9,11},{10,... | collective-permute-start | bytes 1179656 | tf_op jit(solution)/shard_map/ppermute | solution.py:495
  102.6 1.0 copy-start
  103.6 22.0 %copy-start.1 = (bf16[16,48,256]{2,1,0:T(8,128)(2,1)S(1)}, bf16[16,48,256]{2,1,0:T(8,128)(2,1)}, u32[]{:S(2)}) copy-start(bf16[16,48,256]{2,1,0:T(8,128)(2,1)} %get-tuple-element.39.refs_4_) | copy-start | bytes 1179652
  108.3 11.5 %collective-permute-start.4 = (bf16[16,16,256]{2,1,0:T(8,128)(2,1)}, bf16[16,16,256]{2,1,0:T(8,128)(2,1)S(1)}, u32[]{:S(2)}, u32[]{:S(2)}) collective-permute-start(bf16[16,16,256]{2,1,0:T(8,128)(2,1)} %get-tuple-element.36), channel_id=1, source_target_pairs={{0,1},{1,0},{2,3},{3,2},{4,5},{5,4},{6,7},{7,6},{8,9},{9,8},{10,11... | collective-permute-start | bytes 393224 | tf_op jit(solution)/shard_map/ppermute | solution.py:495
  108.4 13.0 %collective-permute-start.5 = (bf16[16,16,256]{2,1,0:T(8,128)(2,1)}, bf16[16,16,256]{2,1,0:T(8,128)(2,1)S(1)}, u32[]{:S(2)}, u32[]{:S(2)}) collective-permute-start(bf16[16,16,256]{2,1,0:T(8,128)(2,1)} %get-tuple-element.37), channel_id=1, source_target_pairs={{0,3},{1,2},{2,1},{3,0},{4,7},{5,6},{6,5},{7,4},{8,11},{9,10},{10,... | collective-permute-start | bytes 393224 | tf_op jit(solution)/shard_map/ppermute | solution.py:495
  119.8 5.8 %collective-permute-start.6 = (bf16[16,16,256]{2,1,0:T(8,128)(2,1)}, bf16[16,16,256]{2,1,0:T(8,128)(2,1)S(1)}, u32[]{:S(2)}, u32[]{:S(2)}) collective-permute-start(bf16[16,16,256]{2,1,0:T(8,128)(2,1)} %get-tuple-element.38), channel_id=1, source_target_pairs={{0,2},{1,3},{2,0},{3,1},{4,6},{5,7},{6,4},{7,5},{8,10},{9,11},{10,... | collective-permute-start | bytes 393224 | tf_op jit(solution)/shard_map/ppermute | solution.py:495
  125.6 0.9 copy-start.4

commit v6 on v5

--- a/solution.py
+++ b/solution.py
@@ -10,7 +10,7 @@
 LANES = 128
 EARLY_ROWS = 16
 CHUNKS = (48,)
-FILL_FLOPS = 3 * 10**10
+FILL_FLOPS = 30000000000
 SIDES = 2
 HEAD = 3
 AHEAD = 2
@@ -401,29 +401,42 @@
 
 def last_sum(places, received, so_far):
     blocks, _, width = so_far.shape
-    rows = EARLY_ROWS
-    part = pl.BlockSpec((blocks, rows, width), lambda i, *_: (0, i + 1, 0))
-
-    def kernel(places, received, so_far, result, acc):
-        at = pl.multiple_of(pl.program_id(0) * rows, rows)
-        acc[:blocks] = so_far[...]
-
-        def add(p, _):
-            acc[places[p]] += received[p, pl.ds(at, rows)].astype(F32)
+    rows = received.shape[1]
+
+    def kernel(places, received, so_far, result, base, acc_a, acc_b, sems):
+        later = pl.ds(EARLY_ROWS, rows)
+        fetch = pltpu.make_async_copy(so_far.at[:, later], base, sems.at[0])
+        fetch.start()
+        acc_a[...] = jnp.zeros_like(acc_a)
+        acc_b[...] = jnp.zeros_like(acc_b)
+
+        def add(turn, _):
+            for i, acc in enumerate((acc_a, acc_b)):
+                p = turn * 2 + i
+                acc[places[p]] += received[p].astype(F32)
             return 0
 
-        lax.fori_loop(0, received.shape[0], add, 0, unroll=8)
-        result[...] = acc[:blocks]
+        lax.fori_loop(0, received.shape[0] // 2, add, 0, unroll=2)
+        fetch.wait()
+        base[...] += acc_a[:blocks] + acc_b[:blocks]
+        store = pltpu.make_async_copy(base, result.at[:, later], sems.at[1])
+        store.start()
+        store.wait()
 
     return pl.pallas_call(
         kernel,
         out_shape=pltpu.HBM(so_far.shape, F32),
         grid_spec=pltpu.PrefetchScalarGridSpec(
             num_scalar_prefetch=1,
-            grid=(received.shape[1] // rows,),
-            in_specs=[IN_VMEM, part],
-            out_specs=part,
-            scratch_shapes=[pltpu.VMEM((blocks + 1, rows, width), F32)],
+            grid=(1,),
+            in_specs=[IN_VMEM, pl.BlockSpec(memory_space=pltpu.HBM)],
+            out_specs=pl.BlockSpec(memory_space=pltpu.HBM),
+            scratch_shapes=[
+                pltpu.VMEM((blocks, rows, width), F32),
+                pltpu.VMEM((blocks + 1, rows, width), F32),
+                pltpu.VMEM((blocks + 1, rows, width), F32),
+                pltpu.SemaphoreType.DMA((2,)),
+            ],
         ),
         input_output_aliases={2: 0},
         compiler_params=pltpu.CompilerParams(vmem_limit_bytes=SMALL_VMEM),

time: 141 us -> 139 us (0.986)
  Pallas kernels: 37.1 us -> 35.3 us
    pallas_call x1, Pallas kernels: 4.54 us -> 2.68 us  [last_sum(): pl.pallas_call(kernel, out_shape=pltpu.HBM(so_far.shape, F32), grid_spec=...]
where the time goes in v6:
time: 139 us; the launch traced here: 138 us
  waiting for transfers between devices  63.4 us (46%)
  Pallas kernels  35.3 us (25%)
  starting transfers between devices  30.6 us (22%)
  local copies, waits for them, and re-layouts  4.44 us (3%)
  other arithmetic  4.05 us (3%)
    ppermute x1, waiting for transfers between devices, shards(): got_a = lax.ppermute(send_a, 'mpo', beside)  22.6 us
    pallas_call x1, Pallas kernels, products(): pl.pallas_call(functools.partial(products_kernel, capacity), out_shape=ou...  21.8 us
    ppermute x6, waiting for transfers between devices, over_groups(): lax.ppermute(part, 'mpo', pairs)  15.3 us
    ppermute x1, waiting for transfers between devices, shards(): last_a = lax.ppermute(second(keep_a, got_a), 'mpo', mirror)  14.6 us
    all_to_all x1, starting transfers between devices, shards(): early = lax.all_to_all(early_slots, ('lsec', 'rsec'), 0, 0, tiled=True)  9.53 us
    all_to_all x1, starting transfers between devices, shards(): received = lax.all_to_all(slots, ('lsec', 'rsec'), 0, 0, tiled=True)  8.67 us
    all_to_all x1, waiting for transfers between devices, shards(): received = lax.all_to_all(slots, ('lsec', 'rsec'), 0, 0, tiled=True)  6.35 us
    ppermute x6, starting transfers between devices, over_groups(): lax.ppermute(part, 'mpo', pairs)  5.4 us
  transfers between devices with their start and end apart: 12, of which 8 were waited for; matrix products, arithmetic and copies ran while one was open for 3% of the time, Pallas kernels for 8%

profile of v6, /device:TPU:1, one launch (start us, length us, event | category | flops | bytes accessed | tf_op | source)
XLA Modules:
  0.0 138.0 jit_solution(16344140116140896917)
XLA Ops:
  0.0 0.8 copy.10
  1.0 0.6 and_select_fusion.1
  1.6 0.6 pad_add_fusion.device
  2.2 21.8 %products.1 = (bf16[4,16,16,256]{3,2,1,0:T(8,128)(2,1)}, bf16[128,64,256]{2,1,0:T(8,128)(2,1)}, bf16[16,48,256]{2,1,0:T(8,128)(2,1)}, bf16[16,48,256]{2,1,0:T(8,...) custom-call(s32[3]{0:T(128)} %pad_add_fusion.device, ...), custom_call_target="tpu_custom_call" | custom-call | flops 10737418240 | bytes 23068672 | tf_op jit(solution)/shard_map/products/pallas_call | solution.py:257
  24.0 2.1 %collective-permute-start = (bf16[2,64,48,128]{3,2,1,0:T(8,128)(2,1)}, bf16[2,64,48,128]{3,2,1,0:T(8,128)(2,1)S(1)}, u32[]{:S(2)}, u32[]{:S(2)}) collective-permute-start(bf16[2,64,48,128]{3,2,1,0:T(8,128)(2,1)} %get-tuple-element.25), channel_id=1, source_target_pairs={{0,1},{1,0},{2,3},{3,2},{4,5},{5,4},{6,7},{7,6},{8,9},{9,8},{10,11... | collective-permute-start | bytes 4718600 | tf_op jit(solution)/shard_map/ppermute | solution.py:497
  26.1 1.8 %collective-permute-start.2 = (bf16[2,64,48,128]{3,2,1,0:T(8,128)(2,1)}, bf16[2,64,48,128]{3,2,1,0:T(8,128)(2,1)}, u32[]{:S(2)}, u32[]{:S(2)}) collective-permute-start(bf16[2,64,48,128]{3,2,1,0:T(8,128)(2,1)} %get-tuple-element.27), channel_id=1, source_target_pairs={{0,3},{1,2},{2,1},{3,0},{4,7},{5,6},{6,5},{7,4},{8,11},{9,10},{10,... | collective-permute-start | bytes 4718600 | tf_op jit(solution)/shard_map/ppermute | solution.py:498
  27.9 9.5 %all-to-all-start.1 = ((bf16[128,64,256]{2,1,0:T(8,128)(2,1)}), bf16[128,64,256]{2,1,0:T(8,128)(2,1)}, u32[]{:S(2)}, u32[]{:S(2)}) async-start(bf16[128,64,256]{2,1,0:T(8,128)(2,1)} %get-tuple-element.28), calls=%async_computation.1 | async-start | bytes 8388608 | tf_op jit(solution)/shard_map/all_to_all | solution.py:495
  37.5 22.6 %collective-permute-done.got_a = bf16[2,64,48,128]{3,2,1,0:T(8,128)(2,1)S(1)} collective-permute-done((bf16[2,64,48,128]{3,2,1,0:T(8,128)(2,1)}, bf16[2,64,48,128]{3,2,1,0:T(8,128)(2,1)S(1)}, u32[]{:S(2)}, u32[]{:S(2)}) %collective-permute-start) | collective-permute-done | bytes 1572896 | tf_op jit(solution)/shard_map/ppermute | solution.py:497
  60.0 0.2 fusion
  60.2 3.0 %collective-permute-start.1 = (bf16[64,48,128]{2,1,0:T(8,128)(2,1)S(1)}, bf16[64,48,128]{2,1,0:T(8,128)(2,1)S(1)}, u32[]{:S(2)}, u32[]{:S(2)}) collective-permute-start(bf16[64,48,128]{2,1,0:T(8,128)(2,1)S(1)} %fusion), channel_id=1, source_target_pairs={{0,3},{1,2},{2,1},{3,0},{4,7},{5,6},{6,5},{7,4},{8,11},{9,10},{10,... | collective-permute-start | bytes 2359304 | tf_op jit(solution)/shard_map/ppermute | solution.py:499
  63.2 1.3 fusion.1
  64.9 14.6 %collective-permute-done.1.last_a = bf16[64,48,128]{2,1,0:T(8,128)(2,1)S(1)} collective-permute-done((bf16[64,48,128]{2,1,0:T(8,128)(2,1)S(1)}, bf16[64,48,128]{2,1,0:T(8,128)(2,1)S(1)}, u32[]{:S(2)}, u32[]{:S(2)}) %collective-permute-start.1) | collective-permute-done | bytes 786464 | tf_op jit(solution)/shard_map/ppermute | solution.py:499
  79.5 2.5 %collective-permute-done.3.last_b = bf16[64,48,128]{2,1,0:T(8,128)(2,1)S(1)} collective-permute-done((bf16[64,48,128]{2,1,0:T(8,128)(2,1)S(1)}, bf16[64,48,128]{2,1,0:T(8,128)(2,1)S(1)}, u32[]{:S(2)}, u32[]{:S(2)}) %collective-permute-start.3) | collective-permute-done | bytes 786464 | tf_op jit(solution)/shard_map/ppermute | solution.py:500
  82.1 3.9 %fill_slots.1 = bf16[128,48,256]{2,1,0:T(8,128)(2,1)} custom-call(s32[64]{0:T(128)S(1)} %multiply_add_fusion.positions, bf16[2,64,48,128]{3,2,1,0:T(8,128)(2,1)S(1)} %copy-done.2, bf16[2,64,48,128]{3,2,1,0:T(8,128)(2,1)S(1)} %collective-permute-done.got_a, bf16[64,48,128]{2,1,0:T(8,128)(2,1)S(1)} %collective-permute-done.1.last_a, ...), custom_call_target="tpu_custom_call" | custom-call | flops 30000001024 | bytes 1 | tf_op jit(solution)/shard_map/fill_slots/pallas_call | solution.py:317
  86.0 2.0 %all-to-all-done.1.received = bf16[128,64,256]{2,1,0:T(8,128)(2,1)} async-done(((bf16[128,64,256]{2,1,0:T(8,128)(2,1)}), bf16[128,64,256]{2,1,0:T(8,128)(2,1)}, u32[]{:S(2)}, u32[]{:S(2)}) %all-to-all-start.1) | async-done | bytes 4194336 | tf_op jit(solution)/shard_map/all_to_all | solution.py:495
  88.0 8.7 %all-to-all-start = ((bf16[128,48,256]{2,1,0:T(8,128)(2,1)}), bf16[128,48,256]{2,1,0:T(8,128)(2,1)S(1)}, u32[]{:S(2)}, u32[]{:S(2)}) async-start(bf16[128,48,256]{2,1,0:T(8,128)(2,1)} %fill_slots.1), calls=%async_computation | async-start | bytes 6291456 | tf_op jit(solution)/shard_map/all_to_all | solution.py:502
  96.7 0.9 convert_reduce_fusion
  97.9 1.2 collective-permute-start.8
  99.1 2.0 %collective-permute-start.9 = (bf16[16,48,256]{2,1,0:T(8,128)(2,1)}, bf16[16,48,256]{2,1,0:T(8,128)(2,1)}, u32[]{:S(2)}, u32[]{:S(2)}) collective-permute-start(bf16[16,48,256]{2,1,0:T(8,128)(2,1)} %get-tuple-element.42), channel_id=1, source_target_pairs={{0,2},{1,3},{2,0},{3,1},{4,6},{5,7},{6,4},{7,5},{8,10},{9,11},{10,... | collective-permute-start | bytes 1179656 | tf_op jit(solution)/shard_map/ppermute | solution.py:508
  101.1 0.7 copy.11
  101.8 0.8 add.51.places
  102.7 1.0 copy-done
  103.7 4.6 %merge_early.1 = (bf16[16,16,256]{2,1,0:T(8,128)(2,1)}, bf16[16,16,256]{2,1,0:T(8,128)(2,1)}, bf16[16,16,256]{2,1,0:T(8,128)(2,1)}, bf16[16,16,256]{2,1,0:T(8,128)(2,1)}) custom-call(s32[3]{0:T(128)S(1)} %copy-done.5, s32[128]{0:T(128)S(1)} %add.51.places, bf16[128,64,256]{2,1,0:T(8,128)(2,1)} %all-to-all-done.1.received, bf16[4,16,16,256]{3,2,1,0:T(8,128)(2,1)S(1)} %copy-done), custom_call_target="tpu_custom_call" | custom-call | flops 1 | bytes 1 | tf_op jit(solution)/shard_map/merge_early/pallas_call | solution.py:350
  108.4 1.1 collective-permute-start.5
  109.6 10.3 %collective-permute-done.4.refs_1_ = bf16[16,16,256]{2,1,0:T(8,128)(2,1)S(1)} collective-permute-done((bf16[16,16,256]{2,1,0:T(8,128)(2,1)}, bf16[16,16,256]{2,1,0:T(8,128)(2,1)S(1)}, u32[]{:S(2)}, u32[]{:S(2)}) %collective-permute-start.4) | collective-permute-done | bytes 131104 | tf_op jit(solution)/shard_map/ppermute | solution.py:508
  119.8 0.9 collective-permute-start.6
  120.7 0.8 collective-permute-done.5.refs_2_
  121.5 4.2 %collective-permute-done.6.refs_3_ = bf16[16,16,256]{2,1,0:T(8,128)(2,1)S(1)} collective-permute-done((bf16[16,16,256]{2,1,0:T(8,128)(2,1)}, bf16[16,16,256]{2,1,0:T(8,128)(2,1)S(1)}, u32[]{:S(2)}, u32[]{:S(2)}) %collective-permute-start.6) | collective-permute-done | bytes 131104 | tf_op jit(solution)/shard_map/ppermute | solution.py:508
  125.7 0.9 copy-done.4
  126.6 2.3 %first_sum.1.so_far = f32[16,64,256]{2,1,0:T(8,128)} custom-call(bf16[16,16,256]{2,1,0:T(8,128)(2,1)S(1)} %copy-done.4, bf16[16,16,256]{2,1,0:T(8,128)(2,1)S(1)} %collective-permute-done.4.refs_1_, bf16[16,16,256]{2,1,0:T(8,128)(2,1)S(1)} %collective-permute-done.5.refs_2_, bf16[16,16,256]{2,1,0:T(8,128)(2,1)S(1)} %collective-permute-done.6.refs_3_, ...), custom_call_target="tpu_custom_call" | custom-call | flops 1 | bytes 1 | tf_op jit(solution)/shard_map/first_sum/pallas_call | solution.py:390
  128.9 6.4 %all-to-all-done.received = bf16[128,48,256]{2,1,0:T(8,128)(2,1)S(1)} async-done(((bf16[128,48,256]{2,1,0:T(8,128)(2,1)}), bf16[128,48,256]{2,1,0:T(8,128)(2,1)S(1)}, u32[]{:S(2)}, u32[]{:S(2)}) %all-to-all-start) | async-done | bytes 3145760 | tf_op jit(solution)/shard_map/all_to_all | solution.py:502
  135.3 2.7 %last_sum.1 = f32[16,64,256]{2,1,0:T(8,128)} custom-call(s32[128]{0:T(128)S(1)} %add.51.places, bf16[128,48,256]{2,1,0:T(8,128)(2,1)S(1)} %all-to-all-done.received, f32[16,64,256]{2,1,0:T(8,128)} %first_sum.1.so_far), custom_call_target="tpu_custom_call", output_to_operand_aliasing={{}: (2, {})} | custom-call | flops 1 | bytes 1 | tf_op jit(solution)/shard_map/last_sum/pallas_call | solution.py:426
  (26 shorter events, 0.8 us)
Async XLA Ops:
  24.0 36.0 %collective-permute-start = (bf16[2,64,48,128]{3,2,1,0:T(8,128)(2,1)}, bf16[2,64,48,128]{3,2,1,0:T(8,128)(2,1)S(1)}, u32[]{:S(2)}, u32[]{:S(2)}) collective-permute-start(bf16[2,64,48,128]{3,2,1,0:T(8,128)(2,1)} %get-tuple-element.25), channel_id=1, source_target_pairs={{0,1},{1,0},{2,3},{3,2},{4,5},{5,4},{6,7},{7,6},{8,9},{9,8},{10,11... | collective-permute-start | bytes 4718600 | tf_op jit(solution)/shard_map/ppermute | solution.py:497
  26.1 37.1 %collective-permute-start.2 = (bf16[2,64,48,128]{3,2,1,0:T(8,128)(2,1)}, bf16[2,64,48,128]{3,2,1,0:T(8,128)(2,1)}, u32[]{:S(2)}, u32[]{:S(2)}) collective-permute-start(bf16[2,64,48,128]{3,2,1,0:T(8,128)(2,1)} %get-tuple-element.27), channel_id=1, source_target_pairs={{0,3},{1,2},{2,1},{3,0},{4,7},{5,6},{6,5},{7,4},{8,11},{9,10},{10,... | collective-permute-start | bytes 4718600 | tf_op jit(solution)/shard_map/ppermute | solution.py:498
  27.9 32.1 %copy-start.2 = (bf16[2,64,48,128]{3,2,1,0:T(8,128)(2,1)S(1)}, bf16[2,64,48,128]{3,2,1,0:T(8,128)(2,1)}, u32[]{:S(2)}) copy-start(bf16[2,64,48,128]{3,2,1,0:T(8,128)(2,1)} %get-tuple-element.24.keep_a) | copy-start | bytes 4718596
  27.9 60.1 %all-to-all-start.1 = ((bf16[128,64,256]{2,1,0:T(8,128)(2,1)}), bf16[128,64,256]{2,1,0:T(8,128)(2,1)}, u32[]{:S(2)}, u32[]{:S(2)}) async-start(bf16[128,64,256]{2,1,0:T(8,128)(2,1)} %get-tuple-element.28), calls=%async_computation.1 | async-start | bytes 8388608 | tf_op jit(solution)/shard_map/all_to_all | solution.py:495
  37.4 25.8 %copy-start.3 = (bf16[2,64,48,128]{3,2,1,0:T(8,128)(2,1)S(1)}, bf16[2,64,48,128]{3,2,1,0:T(8,128)(2,1)}, u32[]{:S(2)}) copy-start(bf16[2,64,48,128]{3,2,1,0:T(8,128)(2,1)} %get-tuple-element.26.keep_b) | copy-start | bytes 4718596
  60.2 19.3 %collective-permute-start.1 = (bf16[64,48,128]{2,1,0:T(8,128)(2,1)S(1)}, bf16[64,48,128]{2,1,0:T(8,128)(2,1)S(1)}, u32[]{:S(2)}, u32[]{:S(2)}) collective-permute-start(bf16[64,48,128]{2,1,0:T(8,128)(2,1)S(1)} %fusion), channel_id=1, source_target_pairs={{0,3},{1,2},{2,1},{3,0},{4,7},{5,6},{6,5},{7,4},{8,11},{9,10},{10,... | collective-permute-start | bytes 2359304 | tf_op jit(solution)/shard_map/ppermute | solution.py:499
  64.6 17.5 %collective-permute-start.3 = (bf16[64,48,128]{2,1,0:T(8,128)(2,1)S(1)}, bf16[64,48,128]{2,1,0:T(8,128)(2,1)S(1)}, u32[]{:S(2)}, u32[]{:S(2)}) collective-permute-start(bf16[64,48,128]{2,1,0:T(8,128)(2,1)S(1)} %fusion.1), channel_id=1, source_target_pairs={{0,1},{1,0},{2,3},{3,2},{4,5},{5,4},{6,7},{7,6},{8,9},{9,8},{10,11... | collective-permute-start | bytes 2359304 | tf_op jit(solution)/shard_map/ppermute | solution.py:500
  86.0 16.7 %copy-start.5 = (s32[3]{0:T(128)S(1)}, s32[3]{0:T(128)}, u32[]{:S(2)}) copy-start(s32[3]{0:T(128)} %pad_add_fusion.device) | copy-start | bytes 40
  88.0 47.3 %all-to-all-start = ((bf16[128,48,256]{2,1,0:T(8,128)(2,1)}), bf16[128,48,256]{2,1,0:T(8,128)(2,1)S(1)}, u32[]{:S(2)}, u32[]{:S(2)}) async-start(bf16[128,48,256]{2,1,0:T(8,128)(2,1)} %fill_slots.1), calls=%async_computation | async-start | bytes 6291456 | tf_op jit(solution)/shard_map/all_to_all | solution.py:502
  97.8 27.9 %collective-permute-start.7 = (bf16[16,48,256]{2,1,0:T(8,128)(2,1)}, bf16[16,48,256]{2,1,0:T(8,128)(2,1)S(1)}, u32[]{:S(2)}, u32[]{:S(2)}) collective-permute-start(bf16[16,48,256]{2,1,0:T(8,128)(2,1)} %get-tuple-element.40), channel_id=1, source_target_pairs={{0,1},{1,0},{2,3},{3,2},{4,5},{5,4},{6,7},{7,6},{8,9},{9,8},{10,11... | collective-permute-start | bytes 1179656 | tf_op jit(solution)/shard_map/ppermute | solution.py:508
  97.9 27.8 %collective-permute-start.8 = (bf16[16,48,256]{2,1,0:T(8,128)(2,1)}, bf16[16,48,256]{2,1,0:T(8,128)(2,1)}, u32[]{:S(2)}, u32[]{:S(2)}) collective-permute-start(bf16[16,48,256]{2,1,0:T(8,128)(2,1)} %get-tuple-element.41), channel_id=1, source_target_pairs={{0,3},{1,2},{2,1},{3,0},{4,7},{5,6},{6,5},{7,4},{8,11},{9,10},{10,... | collective-permute-start | bytes 1179656 | tf_op jit(solution)/shard_map/ppermute | solution.py:508
  99.1 26.6 %collective-permute-start.9 = (bf16[16,48,256]{2,1,0:T(8,128)(2,1)}, bf16[16,48,256]{2,1,0:T(8,128)(2,1)}, u32[]{:S(2)}, u32[]{:S(2)}) collective-permute-start(bf16[16,48,256]{2,1,0:T(8,128)(2,1)} %get-tuple-element.42), channel_id=1, source_target_pairs={{0,2},{1,3},{2,0},{3,1},{4,6},{5,7},{6,4},{7,5},{8,10},{9,11},{10,... | collective-permute-start | bytes 1179656 | tf_op jit(solution)/shard_map/ppermute | solution.py:508
  102.6 1.0 copy-start
  103.7 22.0 %copy-start.1 = (bf16[16,48,256]{2,1,0:T(8,128)(2,1)S(1)}, bf16[16,48,256]{2,1,0:T(8,128)(2,1)}, u32[]{:S(2)}) copy-start(bf16[16,48,256]{2,1,0:T(8,128)(2,1)} %get-tuple-element.39.refs_4_) | copy-start | bytes 1179652
  108.3 11.5 %collective-permute-start.4 = (bf16[16,16,256]{2,1,0:T(8,128)(2,1)}, bf16[16,16,256]{2,1,0:T(8,128)(2,1)S(1)}, u32[]{:S(2)}, u32[]{:S(2)}) collective-permute-start(bf16[16,16,256]{2,1,0:T(8,128)(2,1)} %get-tuple-element.36), channel_id=1, source_target_pairs={{0,1},{1,0},{2,3},{3,2},{4,5},{5,4},{6,7},{7,6},{8,9},{9,8},{10,11... | collective-permute-start | bytes 393224 | tf_op jit(solution)/shard_map/ppermute | solution.py:508
  108.4 13.0 %collective-permute-start.5 = (bf16[16,16,256]{2,1,0:T(8,128)(2,1)}, bf16[16,16,256]{2,1,0:T(8,128)(2,1)S(1)}, u32[]{:S(2)}, u32[]{:S(2)}) collective-permute-start(bf16[16,16,256]{2,1,0:T(8,128)(2,1)} %get-tuple-element.37), channel_id=1, source_target_pairs={{0,3},{1,2},{2,1},{3,0},{4,7},{5,6},{6,5},{7,4},{8,11},{9,10},{10,... | collective-permute-start | bytes 393224 | tf_op jit(solution)/shard_map/ppermute | solution.py:508
  119.8 5.8 %collective-permute-start.6 = (bf16[16,16,256]{2,1,0:T(8,128)(2,1)}, bf16[16,16,256]{2,1,0:T(8,128)(2,1)S(1)}, u32[]{:S(2)}, u32[]{:S(2)}) collective-permute-start(bf16[16,16,256]{2,1,0:T(8,128)(2,1)} %get-tuple-element.38), channel_id=1, source_target_pairs={{0,2},{1,3},{2,0},{3,1},{4,6},{5,7},{6,4},{7,5},{8,10},{9,11},{10,... | collective-permute-start | bytes 393224 | tf_op jit(solution)/shard_map/ppermute | solution.py:508
  125.7 0.9 copy-start.4

commit v7 on v6

--- a/solution.py
+++ b/solution.py
@@ -35,8 +35,8 @@
 
 
 def products_kernel(
-    capacity, device, block_left, block_right, channel_class, own_targets, psi_hbm, left_hbm,
-    right_hbm, own_early, slots_hbm, *rest
+    capacity, block_left, block_right, channel_class, own_targets, psi_hbm, left_hbm, right_hbm,
+    own_early, slots_hbm, *rest
 ):
     own_late = rest[:4]
     chunk_outs = rest[4 : 4 + 4 * len(CHUNKS)]
@@ -53,7 +53,9 @@
     step = pl.program_id(0)
     steps = pl.num_programs(0)
     blocks = SIDES * steps
-    x = device[0]
+    x = lax.axis_index("mpo")
+    first_left = lax.axis_index("lsec") * left_count
+    first_right = lax.axis_index("rsec") * right_count
 
     def psi_copy(part):
         at = pl.ds(0, head) if part == 0 else pl.ds(head, psi_ref.shape[0] - head)
@@ -80,10 +82,7 @@
                 act(slot_copy(turn, side, h))
 
     def sectors(k):
-        return (
-            block_left[k] - device[1] * left_count,
-            block_right[k] - device[2] * right_count,
-        )
+        return block_left[k] - first_left, block_right[k] - first_right
 
     def first_product(w, k, left_id, place):
         half_ref[place] = jnp.dot(
@@ -214,9 +213,10 @@
             k = SIDES * pair + side
             left_id, right_id = sectors(k)
             at = SIDES * lax.rem(pair, HEAD) + side
+            first_product(0, k, left_id, side * channels)
             for w in range(channels):
-                first_product(w, k, left_id, side * channels + w)
-            for w in range(channels):
+                if w + 1 < channels:
+                    first_product(w + 1, k, left_id, side * channels + w + 1)
                 second_product(w, right_id, side * channels + w, at)
                 turn = side * channels + w
                 for part in work[turn * len(work) // turns : (turn + 1) * len(work) // turns]:
@@ -465,7 +465,7 @@
     targets = hop_target.reshape(owners, item_count)
     own_targets = lax.dynamic_index_in_dim(targets, me, 0, False)
     own_early, early_slots, *parts = products(
-        (device, block_left, block_right, channel_class, own_targets),
+        (block_left, block_right, channel_class, own_targets),
         owners,
         capacity,
         wavefunction,

time: 139 us -> 137 us (0.986)
    unnamed x13 -> x11, local copies, waits for them, and re-layouts: 2.79 us -> 2.79 us
where the time goes in v7:
time: 137 us
  waiting for transfers between devices  63.3 us (46%)
  Pallas kernels  34.8 us (25%)
  starting transfers between devices  30.6 us (22%)
  local copies, waits for them, and re-layouts  4.44 us (3%)
  other arithmetic  3.53 us (3%)
    ppermute x1, waiting for transfers between devices, shards(): got_a = lax.ppermute(send_a, 'mpo', beside)  22.6 us
    pallas_call x1, Pallas kernels, products(): pl.pallas_call(functools.partial(products_kernel, capacity), out_shape=ou...  21.2 us
    ppermute x6, waiting for transfers between devices, over_groups(): lax.ppermute(part, 'mpo', pairs)  15.1 us
    ppermute x1, waiting for transfers between devices, shards(): last_a = lax.ppermute(second(keep_a, got_a), 'mpo', mirror)  14.6 us
    all_to_all x1, starting transfers between devices, shards(): early = lax.all_to_all(early_slots, ('lsec', 'rsec'), 0, 0, tiled=True)  9.52 us
    all_to_all x1, starting transfers between devices, shards(): received = lax.all_to_all(slots, ('lsec', 'rsec'), 0, 0, tiled=True)  8.67 us
    all_to_all x1, waiting for transfers between devices, shards(): received = lax.all_to_all(slots, ('lsec', 'rsec'), 0, 0, tiled=True)  6.35 us
    ppermute x6, starting transfers between devices, over_groups(): lax.ppermute(part, 'mpo', pairs)  5.44 us
  transfers between devices with their start and end apart: 12, of which 8 were waited for; matrix products, arithmetic and copies ran while one was open for 3% of the time, Pallas kernels for 8%

profile of v7, /device:TPU:1, one launch (start us, length us, event | category | flops | bytes accessed | tf_op | source)
XLA Modules:
  0.0 136.8 jit_solution(1062392184129070246)
XLA Ops:
  0.0 0.8 copy.10
  1.0 0.6 and_select_fusion.1
  1.6 21.2 %products.1 = (bf16[4,16,16,256]{3,2,1,0:T(8,128)(2,1)}, bf16[128,64,256]{2,1,0:T(8,128)(2,1)}, bf16[16,48,256]{2,1,0:T(8,128)(2,1)}, bf16[16,48,256]{2,1,0:T(8,...) custom-call(s32[16]{0:T(128)} %block_left.1, ...), custom_call_target="tpu_custom_call" | custom-call | flops 10737418240 | bytes 23068672 | tf_op jit(solution)/shard_map/products/pallas_call | solution.py:257
  22.8 2.1 %collective-permute-start = (bf16[2,64,48,128]{3,2,1,0:T(8,128)(2,1)}, bf16[2,64,48,128]{3,2,1,0:T(8,128)(2,1)S(1)}, u32[]{:S(2)}, u32[]{:S(2)}) collective-permute-start(bf16[2,64,48,128]{3,2,1,0:T(8,128)(2,1)} %get-tuple-element.25), channel_id=1, source_target_pairs={{0,1},{1,0},{2,3},{3,2},{4,5},{5,4},{6,7},{7,6},{8,9},{9,8},{10,11... | collective-permute-start | bytes 4718600 | tf_op jit(solution)/shard_map/ppermute | solution.py:497
  24.9 1.8 %collective-permute-start.2 = (bf16[2,64,48,128]{3,2,1,0:T(8,128)(2,1)}, bf16[2,64,48,128]{3,2,1,0:T(8,128)(2,1)}, u32[]{:S(2)}, u32[]{:S(2)}) collective-permute-start(bf16[2,64,48,128]{3,2,1,0:T(8,128)(2,1)} %get-tuple-element.27), channel_id=1, source_target_pairs={{0,3},{1,2},{2,1},{3,0},{4,7},{5,6},{6,5},{7,4},{8,11},{9,10},{10,... | collective-permute-start | bytes 4718600 | tf_op jit(solution)/shard_map/ppermute | solution.py:498
  26.8 9.5 %all-to-all-start.1 = ((bf16[128,64,256]{2,1,0:T(8,128)(2,1)}), bf16[128,64,256]{2,1,0:T(8,128)(2,1)}, u32[]{:S(2)}, u32[]{:S(2)}) async-start(bf16[128,64,256]{2,1,0:T(8,128)(2,1)} %get-tuple-element.28), calls=%async_computation.1 | async-start | bytes 8388608 | tf_op jit(solution)/shard_map/all_to_all | solution.py:495
  36.3 22.6 %collective-permute-done.got_a = bf16[2,64,48,128]{3,2,1,0:T(8,128)(2,1)S(1)} collective-permute-done((bf16[2,64,48,128]{3,2,1,0:T(8,128)(2,1)}, bf16[2,64,48,128]{3,2,1,0:T(8,128)(2,1)S(1)}, u32[]{:S(2)}, u32[]{:S(2)}) %collective-permute-start) | collective-permute-done | bytes 1572896 | tf_op jit(solution)/shard_map/ppermute | solution.py:497
  58.9 0.2 fusion
  59.1 3.0 %collective-permute-start.1 = (bf16[64,48,128]{2,1,0:T(8,128)(2,1)S(1)}, bf16[64,48,128]{2,1,0:T(8,128)(2,1)S(1)}, u32[]{:S(2)}, u32[]{:S(2)}) collective-permute-start(bf16[64,48,128]{2,1,0:T(8,128)(2,1)S(1)} %fusion), channel_id=1, source_target_pairs={{0,3},{1,2},{2,1},{3,0},{4,7},{5,6},{6,5},{7,4},{8,11},{9,10},{10,... | collective-permute-start | bytes 2359304 | tf_op jit(solution)/shard_map/ppermute | solution.py:499
  62.1 1.3 fusion.1
  63.5 0.2 convert_reduce_fusion.1
  63.7 14.6 %collective-permute-done.1.last_a = bf16[64,48,128]{2,1,0:T(8,128)(2,1)S(1)} collective-permute-done((bf16[64,48,128]{2,1,0:T(8,128)(2,1)S(1)}, bf16[64,48,128]{2,1,0:T(8,128)(2,1)S(1)}, u32[]{:S(2)}, u32[]{:S(2)}) %collective-permute-start.1) | collective-permute-done | bytes 786464 | tf_op jit(solution)/shard_map/ppermute | solution.py:499
  78.3 2.6 %collective-permute-done.3.last_b = bf16[64,48,128]{2,1,0:T(8,128)(2,1)S(1)} collective-permute-done((bf16[64,48,128]{2,1,0:T(8,128)(2,1)S(1)}, bf16[64,48,128]{2,1,0:T(8,128)(2,1)S(1)}, u32[]{:S(2)}, u32[]{:S(2)}) %collective-permute-start.3) | collective-permute-done | bytes 786464 | tf_op jit(solution)/shard_map/ppermute | solution.py:500
  80.9 3.9 %fill_slots.1 = bf16[128,48,256]{2,1,0:T(8,128)(2,1)} custom-call(s32[64]{0:T(128)S(1)} %multiply_add_fusion.positions, bf16[2,64,48,128]{3,2,1,0:T(8,128)(2,1)S(1)} %copy-done.2, bf16[2,64,48,128]{3,2,1,0:T(8,128)(2,1)S(1)} %collective-permute-done.got_a, bf16[64,48,128]{2,1,0:T(8,128)(2,1)S(1)} %collective-permute-done.1.last_a, ...), custom_call_target="tpu_custom_call" | custom-call | flops 30000001024 | bytes 1 | tf_op jit(solution)/shard_map/fill_slots/pallas_call | solution.py:317
  84.8 2.0 %all-to-all-done.1.received = bf16[128,64,256]{2,1,0:T(8,128)(2,1)} async-done(((bf16[128,64,256]{2,1,0:T(8,128)(2,1)}), bf16[128,64,256]{2,1,0:T(8,128)(2,1)}, u32[]{:S(2)}, u32[]{:S(2)}) %all-to-all-start.1) | async-done | bytes 4194336 | tf_op jit(solution)/shard_map/all_to_all | solution.py:495
  86.8 8.7 %all-to-all-start = ((bf16[128,48,256]{2,1,0:T(8,128)(2,1)}), bf16[128,48,256]{2,1,0:T(8,128)(2,1)S(1)}, u32[]{:S(2)}, u32[]{:S(2)}) async-start(bf16[128,48,256]{2,1,0:T(8,128)(2,1)} %fill_slots.1), calls=%async_computation | async-start | bytes 6291456 | tf_op jit(solution)/shard_map/all_to_all | solution.py:502
  95.5 0.9 convert_reduce_fusion
  96.7 1.2 collective-permute-start.8
  98.0 2.0 %collective-permute-start.9 = (bf16[16,48,256]{2,1,0:T(8,128)(2,1)}, bf16[16,48,256]{2,1,0:T(8,128)(2,1)}, u32[]{:S(2)}, u32[]{:S(2)}) collective-permute-start(bf16[16,48,256]{2,1,0:T(8,128)(2,1)} %get-tuple-element.42), channel_id=1, source_target_pairs={{0,2},{1,3},{2,0},{3,1},{4,6},{5,7},{6,4},{7,5},{8,10},{9,11},{10,... | collective-permute-start | bytes 1179656 | tf_op jit(solution)/shard_map/ppermute | solution.py:508
  100.0 0.7 copy.11
  100.7 0.8 add.51.places
  101.6 1.0 copy-done
  102.6 4.7 %merge_early.1 = (bf16[16,16,256]{2,1,0:T(8,128)(2,1)}, bf16[16,16,256]{2,1,0:T(8,128)(2,1)}, bf16[16,16,256]{2,1,0:T(8,128)(2,1)}, bf16[16,16,256]{2,1,0:T(8,128)(2,1)}) custom-call(s32[3]{0:T(128)S(1)} %pad_add_fusion.device, s32[128]{0:T(128)S(1)} %add.51.places, bf16[128,64,256]{2,1,0:T(8,128)(2,1)} %all-to-all-done.1.received, ...), custom_call_target="tpu_custom_call" | custom-call | flops 1 | bytes 1 | tf_op jit(solution)/shard_map/merge_early/pallas_call | solution.py:350
  107.4 1.1 collective-permute-start.5
  108.5 10.2 %collective-permute-done.4.refs_1_ = bf16[16,16,256]{2,1,0:T(8,128)(2,1)S(1)} collective-permute-done((bf16[16,16,256]{2,1,0:T(8,128)(2,1)}, bf16[16,16,256]{2,1,0:T(8,128)(2,1)S(1)}, u32[]{:S(2)}, u32[]{:S(2)}) %collective-permute-start.4) | collective-permute-done | bytes 131104 | tf_op jit(solution)/shard_map/ppermute | solution.py:508
  118.7 0.9 collective-permute-start.6
  119.6 0.8 collective-permute-done.5.refs_2_
  120.3 4.2 %collective-permute-done.6.refs_3_ = bf16[16,16,256]{2,1,0:T(8,128)(2,1)S(1)} collective-permute-done((bf16[16,16,256]{2,1,0:T(8,128)(2,1)}, bf16[16,16,256]{2,1,0:T(8,128)(2,1)S(1)}, u32[]{:S(2)}, u32[]{:S(2)}) %collective-permute-start.6) | collective-permute-done | bytes 131104 | tf_op jit(solution)/shard_map/ppermute | solution.py:508
  124.6 0.9 copy-done.4
  125.5 2.3 %first_sum.1.so_far = f32[16,64,256]{2,1,0:T(8,128)} custom-call(bf16[16,16,256]{2,1,0:T(8,128)(2,1)S(1)} %copy-done.4, bf16[16,16,256]{2,1,0:T(8,128)(2,1)S(1)} %collective-permute-done.4.refs_1_, bf16[16,16,256]{2,1,0:T(8,128)(2,1)S(1)} %collective-permute-done.5.refs_2_, bf16[16,16,256]{2,1,0:T(8,128)(2,1)S(1)} %collective-permute-done.6.refs_3_, ...), custom_call_target="tpu_custom_call" | custom-call | flops 1 | bytes 1 | tf_op jit(solution)/shard_map/first_sum/pallas_call | solution.py:390
  127.8 6.3 %all-to-all-done.received = bf16[128,48,256]{2,1,0:T(8,128)(2,1)S(1)} async-done(((bf16[128,48,256]{2,1,0:T(8,128)(2,1)}), bf16[128,48,256]{2,1,0:T(8,128)(2,1)S(1)}, u32[]{:S(2)}, u32[]{:S(2)}) %all-to-all-start) | async-done | bytes 3145760 | tf_op jit(solution)/shard_map/all_to_all | solution.py:502
  134.1 2.7 %last_sum.1 = f32[16,64,256]{2,1,0:T(8,128)} custom-call(s32[128]{0:T(128)S(1)} %add.51.places, bf16[128,48,256]{2,1,0:T(8,128)(2,1)S(1)} %all-to-all-done.received, f32[16,64,256]{2,1,0:T(8,128)} %first_sum.1.so_far), custom_call_target="tpu_custom_call", output_to_operand_aliasing={{}: (2, {})} | custom-call | flops 1 | bytes 1 | tf_op jit(solution)/shard_map/last_sum/pallas_call | solution.py:426
  (24 shorter events, 0.7 us)
Async XLA Ops:
  22.8 36.0 %collective-permute-start = (bf16[2,64,48,128]{3,2,1,0:T(8,128)(2,1)}, bf16[2,64,48,128]{3,2,1,0:T(8,128)(2,1)S(1)}, u32[]{:S(2)}, u32[]{:S(2)}) collective-permute-start(bf16[2,64,48,128]{3,2,1,0:T(8,128)(2,1)} %get-tuple-element.25), channel_id=1, source_target_pairs={{0,1},{1,0},{2,3},{3,2},{4,5},{5,4},{6,7},{7,6},{8,9},{9,8},{10,11... | collective-permute-start | bytes 4718600 | tf_op jit(solution)/shard_map/ppermute | solution.py:497
  24.9 37.1 %collective-permute-start.2 = (bf16[2,64,48,128]{3,2,1,0:T(8,128)(2,1)}, bf16[2,64,48,128]{3,2,1,0:T(8,128)(2,1)}, u32[]{:S(2)}, u32[]{:S(2)}) collective-permute-start(bf16[2,64,48,128]{3,2,1,0:T(8,128)(2,1)} %get-tuple-element.27), channel_id=1, source_target_pairs={{0,3},{1,2},{2,1},{3,0},{4,7},{5,6},{6,5},{7,4},{8,11},{9,10},{10,... | collective-permute-start | bytes 4718600 | tf_op jit(solution)/shard_map/ppermute | solution.py:498
  26.8 32.1 %copy-start.2 = (bf16[2,64,48,128]{3,2,1,0:T(8,128)(2,1)S(1)}, bf16[2,64,48,128]{3,2,1,0:T(8,128)(2,1)}, u32[]{:S(2)}) copy-start(bf16[2,64,48,128]{3,2,1,0:T(8,128)(2,1)} %get-tuple-element.24.keep_a) | copy-start | bytes 4718596
  26.8 60.1 %all-to-all-start.1 = ((bf16[128,64,256]{2,1,0:T(8,128)(2,1)}), bf16[128,64,256]{2,1,0:T(8,128)(2,1)}, u32[]{:S(2)}, u32[]{:S(2)}) async-start(bf16[128,64,256]{2,1,0:T(8,128)(2,1)} %get-tuple-element.28), calls=%async_computation.1 | async-start | bytes 8388608 | tf_op jit(solution)/shard_map/all_to_all | solution.py:495
  36.3 25.8 %copy-start.3 = (bf16[2,64,48,128]{3,2,1,0:T(8,128)(2,1)S(1)}, bf16[2,64,48,128]{3,2,1,0:T(8,128)(2,1)}, u32[]{:S(2)}) copy-start(bf16[2,64,48,128]{3,2,1,0:T(8,128)(2,1)} %get-tuple-element.26.keep_b) | copy-start | bytes 4718596
  59.1 19.3 %collective-permute-start.1 = (bf16[64,48,128]{2,1,0:T(8,128)(2,1)S(1)}, bf16[64,48,128]{2,1,0:T(8,128)(2,1)S(1)}, u32[]{:S(2)}, u32[]{:S(2)}) collective-permute-start(bf16[64,48,128]{2,1,0:T(8,128)(2,1)S(1)} %fusion), channel_id=1, source_target_pairs={{0,3},{1,2},{2,1},{3,0},{4,7},{5,6},{6,5},{7,4},{8,11},{9,10},{10,... | collective-permute-start | bytes 2359304 | tf_op jit(solution)/shard_map/ppermute | solution.py:499
  63.4 17.5 %collective-permute-start.3 = (bf16[64,48,128]{2,1,0:T(8,128)(2,1)S(1)}, bf16[64,48,128]{2,1,0:T(8,128)(2,1)S(1)}, u32[]{:S(2)}, u32[]{:S(2)}) collective-permute-start(bf16[64,48,128]{2,1,0:T(8,128)(2,1)S(1)} %fusion.1), channel_id=1, source_target_pairs={{0,1},{1,0},{2,3},{3,2},{4,5},{5,4},{6,7},{7,6},{8,9},{9,8},{10,11... | collective-permute-start | bytes 2359304 | tf_op jit(solution)/shard_map/ppermute | solution.py:500
  86.8 47.3 %all-to-all-start = ((bf16[128,48,256]{2,1,0:T(8,128)(2,1)}), bf16[128,48,256]{2,1,0:T(8,128)(2,1)S(1)}, u32[]{:S(2)}, u32[]{:S(2)}) async-start(bf16[128,48,256]{2,1,0:T(8,128)(2,1)} %fill_slots.1), calls=%async_computation | async-start | bytes 6291456 | tf_op jit(solution)/shard_map/all_to_all | solution.py:502
  96.6 27.9 %collective-permute-start.7 = (bf16[16,48,256]{2,1,0:T(8,128)(2,1)}, bf16[16,48,256]{2,1,0:T(8,128)(2,1)S(1)}, u32[]{:S(2)}, u32[]{:S(2)}) collective-permute-start(bf16[16,48,256]{2,1,0:T(8,128)(2,1)} %get-tuple-element.40), channel_id=1, source_target_pairs={{0,1},{1,0},{2,3},{3,2},{4,5},{5,4},{6,7},{7,6},{8,9},{9,8},{10,11... | collective-permute-start | bytes 1179656 | tf_op jit(solution)/shard_map/ppermute | solution.py:508
  96.7 27.8 %collective-permute-start.8 = (bf16[16,48,256]{2,1,0:T(8,128)(2,1)}, bf16[16,48,256]{2,1,0:T(8,128)(2,1)}, u32[]{:S(2)}, u32[]{:S(2)}) collective-permute-start(bf16[16,48,256]{2,1,0:T(8,128)(2,1)} %get-tuple-element.41), channel_id=1, source_target_pairs={{0,3},{1,2},{2,1},{3,0},{4,7},{5,6},{6,5},{7,4},{8,11},{9,10},{10,... | collective-permute-start | bytes 1179656 | tf_op jit(solution)/shard_map/ppermute | solution.py:508
  98.0 26.6 %collective-permute-start.9 = (bf16[16,48,256]{2,1,0:T(8,128)(2,1)}, bf16[16,48,256]{2,1,0:T(8,128)(2,1)}, u32[]{:S(2)}, u32[]{:S(2)}) collective-permute-start(bf16[16,48,256]{2,1,0:T(8,128)(2,1)} %get-tuple-element.42), channel_id=1, source_target_pairs={{0,2},{1,3},{2,0},{3,1},{4,6},{5,7},{6,4},{7,5},{8,10},{9,11},{10,... | collective-permute-start | bytes 1179656 | tf_op jit(solution)/shard_map/ppermute | solution.py:508
  101.6 1.0 copy-start
  102.6 21.9 %copy-start.1 = (bf16[16,48,256]{2,1,0:T(8,128)(2,1)S(1)}, bf16[16,48,256]{2,1,0:T(8,128)(2,1)}, u32[]{:S(2)}) copy-start(bf16[16,48,256]{2,1,0:T(8,128)(2,1)} %get-tuple-element.39.refs_4_) | copy-start | bytes 1179652
  107.3 11.4 %collective-permute-start.4 = (bf16[16,16,256]{2,1,0:T(8,128)(2,1)}, bf16[16,16,256]{2,1,0:T(8,128)(2,1)S(1)}, u32[]{:S(2)}, u32[]{:S(2)}) collective-permute-start(bf16[16,16,256]{2,1,0:T(8,128)(2,1)} %get-tuple-element.36), channel_id=1, source_target_pairs={{0,1},{1,0},{2,3},{3,2},{4,5},{5,4},{6,7},{7,6},{8,9},{9,8},{10,11... | collective-permute-start | bytes 393224 | tf_op jit(solution)/shard_map/ppermute | solution.py:508
  107.4 13.0 %collective-permute-start.5 = (bf16[16,16,256]{2,1,0:T(8,128)(2,1)}, bf16[16,16,256]{2,1,0:T(8,128)(2,1)S(1)}, u32[]{:S(2)}, u32[]{:S(2)}) collective-permute-start(bf16[16,16,256]{2,1,0:T(8,128)(2,1)} %get-tuple-element.37), channel_id=1, source_target_pairs={{0,3},{1,2},{2,1},{3,0},{4,7},{5,6},{6,5},{7,4},{8,11},{9,10},{10,... | collective-permute-start | bytes 393224 | tf_op jit(solution)/shard_map/ppermute | solution.py:508
  118.7 5.8 %collective-permute-start.6 = (bf16[16,16,256]{2,1,0:T(8,128)(2,1)}, bf16[16,16,256]{2,1,0:T(8,128)(2,1)S(1)}, u32[]{:S(2)}, u32[]{:S(2)}) collective-permute-start(bf16[16,16,256]{2,1,0:T(8,128)(2,1)} %get-tuple-element.38), channel_id=1, source_target_pairs={{0,2},{1,3},{2,0},{3,1},{4,6},{5,7},{6,4},{7,5},{8,10},{9,11},{10,... | collective-permute-start | bytes 393224 | tf_op jit(solution)/shard_map/ppermute | solution.py:508
  124.5 0.9 copy-start.4

commit v8 on v7

--- a/solution.py
+++ b/solution.py
@@ -12,8 +12,8 @@
 CHUNKS = (48,)
 FILL_FLOPS = 30000000000
 SIDES = 2
-HEAD = 3
-AHEAD = 2
+HEAD = 2
+AHEAD = 3
 BF16 = jnp.bfloat16
 F32 = jnp.float32
 

time: 137 us -> 137 us (level)
  no operation moved by 1% of the time
where the time goes in v8:
time: 137 us; the launch traced here: 136 us
  waiting for transfers between devices  63.3 us (46%)
  Pallas kernels  34.4 us (25%)
  starting transfers between devices  30.6 us (22%)
  local copies, waits for them, and re-layouts  4.44 us (3%)
  other arithmetic  3.53 us (3%)
    ppermute x1, waiting for transfers between devices, shards(): got_a = lax.ppermute(send_a, 'mpo', beside)  22.6 us
    pallas_call x1, Pallas kernels, products(): pl.pallas_call(functools.partial(products_kernel, capacity), out_shape=ou...  20.9 us
    ppermute x6, waiting for transfers between devices, over_groups(): lax.ppermute(part, 'mpo', pairs)  15.1 us
    ppermute x1, waiting for transfers between devices, shards(): last_a = lax.ppermute(second(keep_a, got_a), 'mpo', mirror)  14.6 us
    all_to_all x1, starting transfers between devices, shards(): early = lax.all_to_all(early_slots, ('lsec', 'rsec'), 0, 0, tiled=True)  9.53 us
    all_to_all x1, starting transfers between devices, shards(): received = lax.all_to_all(slots, ('lsec', 'rsec'), 0, 0, tiled=True)  8.66 us
    all_to_all x1, waiting for transfers between devices, shards(): received = lax.all_to_all(slots, ('lsec', 'rsec'), 0, 0, tiled=True)  6.35 us
    ppermute x6, starting transfers between devices, over_groups(): lax.ppermute(part, 'mpo', pairs)  5.45 us
  transfers between devices with their start and end apart: 12, of which 8 were waited for; matrix products, arithmetic and copies ran while one was open for 3% of the time, Pallas kernels for 8%

profile of v8, /device:TPU:1, one launch (start us, length us, event | category | flops | bytes accessed | tf_op | source)
XLA Modules:
  0.0 136.5 jit_solution(10980719227248367200)
XLA Ops:
  0.0 0.8 copy.10
  1.0 0.6 and_select_fusion.1
  1.6 20.9 %products.1 = (bf16[4,16,16,256]{3,2,1,0:T(8,128)(2,1)}, bf16[128,64,256]{2,1,0:T(8,128)(2,1)}, bf16[16,48,256]{2,1,0:T(8,128)(2,1)}, bf16[16,48,256]{2,1,0:T(8,...) custom-call(s32[16]{0:T(128)} %block_left.1, ...), custom_call_target="tpu_custom_call" | custom-call | flops 10737418240 | bytes 23068672 | tf_op jit(solution)/shard_map/products/pallas_call | solution.py:257
  22.5 2.1 %collective-permute-start = (bf16[2,64,48,128]{3,2,1,0:T(8,128)(2,1)}, bf16[2,64,48,128]{3,2,1,0:T(8,128)(2,1)S(1)}, u32[]{:S(2)}, u32[]{:S(2)}) collective-permute-start(bf16[2,64,48,128]{3,2,1,0:T(8,128)(2,1)} %get-tuple-element.25), channel_id=1, source_target_pairs={{0,1},{1,0},{2,3},{3,2},{4,5},{5,4},{6,7},{7,6},{8,9},{9,8},{10,11... | collective-permute-start | bytes 4718600 | tf_op jit(solution)/shard_map/ppermute | solution.py:497
  24.6 1.8 %collective-permute-start.2 = (bf16[2,64,48,128]{3,2,1,0:T(8,128)(2,1)}, bf16[2,64,48,128]{3,2,1,0:T(8,128)(2,1)}, u32[]{:S(2)}, u32[]{:S(2)}) collective-permute-start(bf16[2,64,48,128]{3,2,1,0:T(8,128)(2,1)} %get-tuple-element.27), channel_id=1, source_target_pairs={{0,3},{1,2},{2,1},{3,0},{4,7},{5,6},{6,5},{7,4},{8,11},{9,10},{10,... | collective-permute-start | bytes 4718600 | tf_op jit(solution)/shard_map/ppermute | solution.py:498
  26.4 9.5 %all-to-all-start.1 = ((bf16[128,64,256]{2,1,0:T(8,128)(2,1)}), bf16[128,64,256]{2,1,0:T(8,128)(2,1)}, u32[]{:S(2)}, u32[]{:S(2)}) async-start(bf16[128,64,256]{2,1,0:T(8,128)(2,1)} %get-tuple-element.28), calls=%async_computation.1 | async-start | bytes 8388608 | tf_op jit(solution)/shard_map/all_to_all | solution.py:495
  36.0 22.6 %collective-permute-done.got_a = bf16[2,64,48,128]{3,2,1,0:T(8,128)(2,1)S(1)} collective-permute-done((bf16[2,64,48,128]{3,2,1,0:T(8,128)(2,1)}, bf16[2,64,48,128]{3,2,1,0:T(8,128)(2,1)S(1)}, u32[]{:S(2)}, u32[]{:S(2)}) %collective-permute-start) | collective-permute-done | bytes 1572896 | tf_op jit(solution)/shard_map/ppermute | solution.py:497
  58.5 0.2 fusion
  58.7 3.0 %collective-permute-start.1 = (bf16[64,48,128]{2,1,0:T(8,128)(2,1)S(1)}, bf16[64,48,128]{2,1,0:T(8,128)(2,1)S(1)}, u32[]{:S(2)}, u32[]{:S(2)}) collective-permute-start(bf16[64,48,128]{2,1,0:T(8,128)(2,1)S(1)} %fusion), channel_id=1, source_target_pairs={{0,3},{1,2},{2,1},{3,0},{4,7},{5,6},{6,5},{7,4},{8,11},{9,10},{10,... | collective-permute-start | bytes 2359304 | tf_op jit(solution)/shard_map/ppermute | solution.py:499
  61.7 1.3 fusion.1
  63.2 0.2 convert_reduce_fusion.1
  63.4 14.6 %collective-permute-done.1.last_a = bf16[64,48,128]{2,1,0:T(8,128)(2,1)S(1)} collective-permute-done((bf16[64,48,128]{2,1,0:T(8,128)(2,1)S(1)}, bf16[64,48,128]{2,1,0:T(8,128)(2,1)S(1)}, u32[]{:S(2)}, u32[]{:S(2)}) %collective-permute-start.1) | collective-permute-done | bytes 786464 | tf_op jit(solution)/shard_map/ppermute | solution.py:499
  78.0 2.6 %collective-permute-done.3.last_b = bf16[64,48,128]{2,1,0:T(8,128)(2,1)S(1)} collective-permute-done((bf16[64,48,128]{2,1,0:T(8,128)(2,1)S(1)}, bf16[64,48,128]{2,1,0:T(8,128)(2,1)S(1)}, u32[]{:S(2)}, u32[]{:S(2)}) %collective-permute-start.3) | collective-permute-done | bytes 786464 | tf_op jit(solution)/shard_map/ppermute | solution.py:500
  80.6 3.9 %fill_slots.1 = bf16[128,48,256]{2,1,0:T(8,128)(2,1)} custom-call(s32[64]{0:T(128)S(1)} %multiply_add_fusion.positions, bf16[2,64,48,128]{3,2,1,0:T(8,128)(2,1)S(1)} %copy-done.2, bf16[2,64,48,128]{3,2,1,0:T(8,128)(2,1)S(1)} %collective-permute-done.got_a, bf16[64,48,128]{2,1,0:T(8,128)(2,1)S(1)} %collective-permute-done.1.last_a, ...), custom_call_target="tpu_custom_call" | custom-call | flops 30000001024 | bytes 1 | tf_op jit(solution)/shard_map/fill_slots/pallas_call | solution.py:317
  84.4 2.1 %all-to-all-done.1.received = bf16[128,64,256]{2,1,0:T(8,128)(2,1)} async-done(((bf16[128,64,256]{2,1,0:T(8,128)(2,1)}), bf16[128,64,256]{2,1,0:T(8,128)(2,1)}, u32[]{:S(2)}, u32[]{:S(2)}) %all-to-all-start.1) | async-done | bytes 4194336 | tf_op jit(solution)/shard_map/all_to_all | solution.py:495
  86.5 8.7 %all-to-all-start = ((bf16[128,48,256]{2,1,0:T(8,128)(2,1)}), bf16[128,48,256]{2,1,0:T(8,128)(2,1)S(1)}, u32[]{:S(2)}, u32[]{:S(2)}) async-start(bf16[128,48,256]{2,1,0:T(8,128)(2,1)} %fill_slots.1), calls=%async_computation | async-start | bytes 6291456 | tf_op jit(solution)/shard_map/all_to_all | solution.py:502
  95.2 0.9 convert_reduce_fusion
  96.4 1.2 collective-permute-start.8
  97.6 2.0 %collective-permute-start.9 = (bf16[16,48,256]{2,1,0:T(8,128)(2,1)}, bf16[16,48,256]{2,1,0:T(8,128)(2,1)}, u32[]{:S(2)}, u32[]{:S(2)}) collective-permute-start(bf16[16,48,256]{2,1,0:T(8,128)(2,1)} %get-tuple-element.42), channel_id=1, source_target_pairs={{0,2},{1,3},{2,0},{3,1},{4,6},{5,7},{6,4},{7,5},{8,10},{9,11},{10,... | collective-permute-start | bytes 1179656 | tf_op jit(solution)/shard_map/ppermute | solution.py:508
  99.6 0.7 copy.11
  100.3 0.8 add.51.places
  101.2 1.0 copy-done
  102.3 4.7 %merge_early.1 = (bf16[16,16,256]{2,1,0:T(8,128)(2,1)}, bf16[16,16,256]{2,1,0:T(8,128)(2,1)}, bf16[16,16,256]{2,1,0:T(8,128)(2,1)}, bf16[16,16,256]{2,1,0:T(8,128)(2,1)}) custom-call(s32[3]{0:T(128)S(1)} %pad_add_fusion.device, s32[128]{0:T(128)S(1)} %add.51.places, bf16[128,64,256]{2,1,0:T(8,128)(2,1)} %all-to-all-done.1.received, ...), custom_call_target="tpu_custom_call" | custom-call | flops 1 | bytes 1 | tf_op jit(solution)/shard_map/merge_early/pallas_call | solution.py:350
  107.0 1.1 collective-permute-start.5
  108.2 10.2 %collective-permute-done.4.refs_1_ = bf16[16,16,256]{2,1,0:T(8,128)(2,1)S(1)} collective-permute-done((bf16[16,16,256]{2,1,0:T(8,128)(2,1)}, bf16[16,16,256]{2,1,0:T(8,128)(2,1)S(1)}, u32[]{:S(2)}, u32[]{:S(2)}) %collective-permute-start.4) | collective-permute-done | bytes 131104 | tf_op jit(solution)/shard_map/ppermute | solution.py:508
  118.3 0.9 collective-permute-start.6
  119.2 0.7 collective-permute-done.5.refs_2_
  120.0 4.2 %collective-permute-done.6.refs_3_ = bf16[16,16,256]{2,1,0:T(8,128)(2,1)S(1)} collective-permute-done((bf16[16,16,256]{2,1,0:T(8,128)(2,1)}, bf16[16,16,256]{2,1,0:T(8,128)(2,1)S(1)}, u32[]{:S(2)}, u32[]{:S(2)}) %collective-permute-start.6) | collective-permute-done | bytes 131104 | tf_op jit(solution)/shard_map/ppermute | solution.py:508
  124.2 0.9 copy-done.4
  125.1 2.3 %first_sum.1.so_far = f32[16,64,256]{2,1,0:T(8,128)} custom-call(bf16[16,16,256]{2,1,0:T(8,128)(2,1)S(1)} %copy-done.4, bf16[16,16,256]{2,1,0:T(8,128)(2,1)S(1)} %collective-permute-done.4.refs_1_, bf16[16,16,256]{2,1,0:T(8,128)(2,1)S(1)} %collective-permute-done.5.refs_2_, bf16[16,16,256]{2,1,0:T(8,128)(2,1)S(1)} %collective-permute-done.6.refs_3_, ...), custom_call_target="tpu_custom_call" | custom-call | flops 1 | bytes 1 | tf_op jit(solution)/shard_map/first_sum/pallas_call | solution.py:390
  127.4 6.3 %all-to-all-done.received = bf16[128,48,256]{2,1,0:T(8,128)(2,1)S(1)} async-done(((bf16[128,48,256]{2,1,0:T(8,128)(2,1)}), bf16[128,48,256]{2,1,0:T(8,128)(2,1)S(1)}, u32[]{:S(2)}, u32[]{:S(2)}) %all-to-all-start) | async-done | bytes 3145760 | tf_op jit(solution)/shard_map/all_to_all | solution.py:502
  133.8 2.7 %last_sum.1 = f32[16,64,256]{2,1,0:T(8,128)} custom-call(s32[128]{0:T(128)S(1)} %add.51.places, bf16[128,48,256]{2,1,0:T(8,128)(2,1)S(1)} %all-to-all-done.received, f32[16,64,256]{2,1,0:T(8,128)} %first_sum.1.so_far), custom_call_target="tpu_custom_call", output_to_operand_aliasing={{}: (2, {})} | custom-call | flops 1 | bytes 1 | tf_op jit(solution)/shard_map/last_sum/pallas_call | solution.py:426
  (24 shorter events, 0.7 us)
Async XLA Ops:
  22.5 36.0 %collective-permute-start = (bf16[2,64,48,128]{3,2,1,0:T(8,128)(2,1)}, bf16[2,64,48,128]{3,2,1,0:T(8,128)(2,1)S(1)}, u32[]{:S(2)}, u32[]{:S(2)}) collective-permute-start(bf16[2,64,48,128]{3,2,1,0:T(8,128)(2,1)} %get-tuple-element.25), channel_id=1, source_target_pairs={{0,1},{1,0},{2,3},{3,2},{4,5},{5,4},{6,7},{7,6},{8,9},{9,8},{10,11... | collective-permute-start | bytes 4718600 | tf_op jit(solution)/shard_map/ppermute | solution.py:497
  24.6 37.1 %collective-permute-start.2 = (bf16[2,64,48,128]{3,2,1,0:T(8,128)(2,1)}, bf16[2,64,48,128]{3,2,1,0:T(8,128)(2,1)}, u32[]{:S(2)}, u32[]{:S(2)}) collective-permute-start(bf16[2,64,48,128]{3,2,1,0:T(8,128)(2,1)} %get-tuple-element.27), channel_id=1, source_target_pairs={{0,3},{1,2},{2,1},{3,0},{4,7},{5,6},{6,5},{7,4},{8,11},{9,10},{10,... | collective-permute-start | bytes 4718600 | tf_op jit(solution)/shard_map/ppermute | solution.py:498
  26.4 32.1 %copy-start.2 = (bf16[2,64,48,128]{3,2,1,0:T(8,128)(2,1)S(1)}, bf16[2,64,48,128]{3,2,1,0:T(8,128)(2,1)}, u32[]{:S(2)}) copy-start(bf16[2,64,48,128]{3,2,1,0:T(8,128)(2,1)} %get-tuple-element.24.keep_a) | copy-start | bytes 4718596
  26.4 60.1 %all-to-all-start.1 = ((bf16[128,64,256]{2,1,0:T(8,128)(2,1)}), bf16[128,64,256]{2,1,0:T(8,128)(2,1)}, u32[]{:S(2)}, u32[]{:S(2)}) async-start(bf16[128,64,256]{2,1,0:T(8,128)(2,1)} %get-tuple-element.28), calls=%async_computation.1 | async-start | bytes 8388608 | tf_op jit(solution)/shard_map/all_to_all | solution.py:495
  36.0 25.8 %copy-start.3 = (bf16[2,64,48,128]{3,2,1,0:T(8,128)(2,1)S(1)}, bf16[2,64,48,128]{3,2,1,0:T(8,128)(2,1)}, u32[]{:S(2)}) copy-start(bf16[2,64,48,128]{3,2,1,0:T(8,128)(2,1)} %get-tuple-element.26.keep_b) | copy-start | bytes 4718596
  58.7 19.3 %collective-permute-start.1 = (bf16[64,48,128]{2,1,0:T(8,128)(2,1)S(1)}, bf16[64,48,128]{2,1,0:T(8,128)(2,1)S(1)}, u32[]{:S(2)}, u32[]{:S(2)}) collective-permute-start(bf16[64,48,128]{2,1,0:T(8,128)(2,1)S(1)} %fusion), channel_id=1, source_target_pairs={{0,3},{1,2},{2,1},{3,0},{4,7},{5,6},{6,5},{7,4},{8,11},{9,10},{10,... | collective-permute-start | bytes 2359304 | tf_op jit(solution)/shard_map/ppermute | solution.py:499
  63.1 17.5 %collective-permute-start.3 = (bf16[64,48,128]{2,1,0:T(8,128)(2,1)S(1)}, bf16[64,48,128]{2,1,0:T(8,128)(2,1)S(1)}, u32[]{:S(2)}, u32[]{:S(2)}) collective-permute-start(bf16[64,48,128]{2,1,0:T(8,128)(2,1)S(1)} %fusion.1), channel_id=1, source_target_pairs={{0,1},{1,0},{2,3},{3,2},{4,5},{5,4},{6,7},{7,6},{8,9},{9,8},{10,11... | collective-permute-start | bytes 2359304 | tf_op jit(solution)/shard_map/ppermute | solution.py:500
  86.5 47.3 %all-to-all-start = ((bf16[128,48,256]{2,1,0:T(8,128)(2,1)}), bf16[128,48,256]{2,1,0:T(8,128)(2,1)S(1)}, u32[]{:S(2)}, u32[]{:S(2)}) async-start(bf16[128,48,256]{2,1,0:T(8,128)(2,1)} %fill_slots.1), calls=%async_computation | async-start | bytes 6291456 | tf_op jit(solution)/shard_map/all_to_all | solution.py:502
  96.3 27.9 %collective-permute-start.7 = (bf16[16,48,256]{2,1,0:T(8,128)(2,1)}, bf16[16,48,256]{2,1,0:T(8,128)(2,1)S(1)}, u32[]{:S(2)}, u32[]{:S(2)}) collective-permute-start(bf16[16,48,256]{2,1,0:T(8,128)(2,1)} %get-tuple-element.40), channel_id=1, source_target_pairs={{0,1},{1,0},{2,3},{3,2},{4,5},{5,4},{6,7},{7,6},{8,9},{9,8},{10,11... | collective-permute-start | bytes 1179656 | tf_op jit(solution)/shard_map/ppermute | solution.py:508
  96.4 27.8 %collective-permute-start.8 = (bf16[16,48,256]{2,1,0:T(8,128)(2,1)}, bf16[16,48,256]{2,1,0:T(8,128)(2,1)}, u32[]{:S(2)}, u32[]{:S(2)}) collective-permute-start(bf16[16,48,256]{2,1,0:T(8,128)(2,1)} %get-tuple-element.41), channel_id=1, source_target_pairs={{0,3},{1,2},{2,1},{3,0},{4,7},{5,6},{6,5},{7,4},{8,11},{9,10},{10,... | collective-permute-start | bytes 1179656 | tf_op jit(solution)/shard_map/ppermute | solution.py:508
  97.6 26.6 %collective-permute-start.9 = (bf16[16,48,256]{2,1,0:T(8,128)(2,1)}, bf16[16,48,256]{2,1,0:T(8,128)(2,1)}, u32[]{:S(2)}, u32[]{:S(2)}) collective-permute-start(bf16[16,48,256]{2,1,0:T(8,128)(2,1)} %get-tuple-element.42), channel_id=1, source_target_pairs={{0,2},{1,3},{2,0},{3,1},{4,6},{5,7},{6,4},{7,5},{8,10},{9,11},{10,... | collective-permute-start | bytes 1179656 | tf_op jit(solution)/shard_map/ppermute | solution.py:508
  101.2 1.0 copy-start
  102.3 21.9 %copy-start.1 = (bf16[16,48,256]{2,1,0:T(8,128)(2,1)S(1)}, bf16[16,48,256]{2,1,0:T(8,128)(2,1)}, u32[]{:S(2)}) copy-start(bf16[16,48,256]{2,1,0:T(8,128)(2,1)} %get-tuple-element.39.refs_4_) | copy-start | bytes 1179652
  106.9 11.4 %collective-permute-start.4 = (bf16[16,16,256]{2,1,0:T(8,128)(2,1)}, bf16[16,16,256]{2,1,0:T(8,128)(2,1)S(1)}, u32[]{:S(2)}, u32[]{:S(2)}) collective-permute-start(bf16[16,16,256]{2,1,0:T(8,128)(2,1)} %get-tuple-element.36), channel_id=1, source_target_pairs={{0,1},{1,0},{2,3},{3,2},{4,5},{5,4},{6,7},{7,6},{8,9},{9,8},{10,11... | collective-permute-start | bytes 393224 | tf_op jit(solution)/shard_map/ppermute | solution.py:508
  107.0 13.0 %collective-permute-start.5 = (bf16[16,16,256]{2,1,0:T(8,128)(2,1)}, bf16[16,16,256]{2,1,0:T(8,128)(2,1)S(1)}, u32[]{:S(2)}, u32[]{:S(2)}) collective-permute-start(bf16[16,16,256]{2,1,0:T(8,128)(2,1)} %get-tuple-element.37), channel_id=1, source_target_pairs={{0,3},{1,2},{2,1},{3,0},{4,7},{5,6},{6,5},{7,4},{8,11},{9,10},{10,... | collective-permute-start | bytes 393224 | tf_op jit(solution)/shard_map/ppermute | solution.py:508
  118.3 5.8 %collective-permute-start.6 = (bf16[16,16,256]{2,1,0:T(8,128)(2,1)}, bf16[16,16,256]{2,1,0:T(8,128)(2,1)S(1)}, u32[]{:S(2)}, u32[]{:S(2)}) collective-permute-start(bf16[16,16,256]{2,1,0:T(8,128)(2,1)} %get-tuple-element.38), channel_id=1, source_target_pairs={{0,2},{1,3},{2,0},{3,1},{4,6},{5,7},{6,4},{7,5},{8,10},{9,11},{10,... | collective-permute-start | bytes 393224 | tf_op jit(solution)/shard_map/ppermute | solution.py:508
  124.2 0.9 copy-start.4
